TPU v7x, 32 devices: a whole 2x2x4 slice. The times are simulated.
32 devices in a mesh: clips: 2 (over x), seq: 8 (over z, y), head: 2 (over core).
Axes of the slice: x: 2, y: 2, z: 4, core: 2. Of those that a mesh axis runs over, the one named last changes fastest.
Arguments:
- video_q: bfloat16 [2048, 2048], P(('clips', 'seq'), 'head'), parts along dimension 0, may hold values from -105 to 105
- video_k: bfloat16 [2048, 2048], P(('clips', 'seq'), 'head'), parts along dimension 0, may hold values from -5 to 5
- video_v: bfloat16 [2048, 2048], P(('clips', 'seq'), 'head'), parts along dimension 0, may hold values from -6 to 6
- audio_q: bfloat16 [512, 2048], P(('clips', 'seq'), 'head'), parts along dimension 0, may hold values from -105 to 105
- audio_k: bfloat16 [512, 2048], P(('clips', 'seq'), 'head'), parts along dimension 0, may hold values from -5 to 5
- audio_v: bfloat16 [512, 2048], P(('clips', 'seq'), 'head'), parts along dimension 0, may hold values from -6 to 6
- video_query_gain: float32 [2048], P('head'), may hold values from 1 to 2
- video_key_gain: float32 [2048], P('head'), may hold values from 1 to 2
- audio_query_gain: float32 [2048], P('head'), may hold values from 1 to 2
- audio_key_gain: float32 [2048], P('head'), may hold values from 1 to 2
Outputs:
- video_mixed: bfloat16 [2048, 2048], P(('clips', 'seq'), 'head'), parts along dimension 0
- audio_mixed: bfloat16 [512, 2048], P(('clips', 'seq'), 'head'), parts along dimension 0
There are 2 independent parts, one for each index of `clips`. A program takes and returns all parts, laid end to end along the dimension named above; an argument that names none is the same for every part. Nothing has to cross between parts.
All inputs are finite; a program needn't handle non-finite values.
Results may differ from a plain program's by a relative error of at most 0.02.
Values may be sent and summed in bfloat16 or wider, within the bound.
No kernel may reach another device: no remote copies, remote signals or barrier semaphores. Data moves between devices by JAX's collectives and lax.ppermute only.
A program may use at most 128 MiB of HBM per device.

v0:
```python
import jax
import jax.numpy as jnp
from jax import lax
from jax.sharding import PartitionSpec as P

HEAD_DIM = 128


def normed(tokens, gain_row):
    count = tokens.shape[0]
    head_count = tokens.shape[1] // HEAD_DIM
    entries = tokens.astype(jnp.float32).reshape(count, head_count, HEAD_DIM)
    scaled = entries * lax.rsqrt(jnp.mean(entries * entries, axis=2, keepdims=True) + 1e-06)
    return (scaled.reshape(count, head_count * HEAD_DIM) * gain_row).astype(jnp.bfloat16)


def start_state(row_count, head_count):
    return (
        jnp.full((head_count, row_count), -1e30, jnp.float32),
        jnp.zeros((head_count, row_count), jnp.float32),
        jnp.zeros((row_count, head_count, HEAD_DIM), jnp.float32),
    )


def folding(queries, prepare):
    head_count = queries.shape[1]

    def fold_step(state_now, pieces, offset):
        key_rows, values = prepare(pieces)
        key_rows = key_rows.reshape(key_rows.shape[0], head_count, HEAD_DIM)
        values = values.reshape(values.shape[0], head_count, HEAD_DIM)
        scores = jnp.einsum(
            "qhd,khd->hqk", queries, key_rows, preferred_element_type=jnp.float32
        ) * HEAD_DIM ** (-0.5)
        running_max, row_total, accumulated = state_now
        new_max = jnp.maximum(running_max, jnp.max(scores, axis=2))
        rescale = jnp.exp(running_max - new_max)
        weights = jnp.exp(scores - new_max[:, :, None])
        row_total = jnp.sum(weights, axis=2)
        update = jnp.einsum(
            "hqk,khd->qhd", weights.astype(jnp.bfloat16), values, preferred_element_type=jnp.float32
        )
        accumulated = accumulated * rescale.T[:, :, None] + update
        return (new_max, row_total, accumulated)

    return fold_step


def finish(state_now):
    running_max, row_total, accumulated = state_now
    result = accumulated / row_total.T[:, :, None]
    return result.reshape(result.shape[0], result.shape[1] * HEAD_DIM)


def as_heads(tokens):
    return tokens.reshape(tokens.shape[0], tokens.shape[1] // HEAD_DIM, HEAD_DIM)


def keep_pair(pieces):
    return pieces


def per_device(
    video_q,
    video_k,
    video_v,
    audio_q,
    audio_k,
    audio_v,
    video_query_gain,
    video_key_gain,
    audio_query_gain,
    audio_key_gain,
):
    head_count = video_q.shape[1] // HEAD_DIM
    video_rows = video_q.shape[0]
    audio_rows = audio_q.shape[0]
    video_state = folding(as_heads(video_q), keep_pair)(
        start_state(video_rows, head_count),
        (
            lax.all_gather(video_k, "seq", axis=0, tiled=True),
            lax.all_gather(video_v, "seq", axis=0, tiled=True),
        ),
        jnp.int32(0),
    )
    video_self = finish(video_state).astype(jnp.bfloat16)
    audio_state = folding(as_heads(audio_q), keep_pair)(
        start_state(audio_rows, head_count),
        (
            lax.all_gather(audio_k, "seq", axis=0, tiled=True),
            lax.all_gather(audio_v, "seq", axis=0, tiled=True),
        ),
        jnp.int32(0),
    )
    audio_self = finish(audio_state).astype(jnp.bfloat16)
    audio_whole = lax.all_gather(audio_self, "seq", axis=0, tiled=True)
    video_queries = as_heads(normed(video_self, video_query_gain))
    cross_step = folding(video_queries, keep_pair)
    video_cross = finish(
        cross_step(
            start_state(video_rows, head_count),
            (normed(audio_whole, audio_key_gain), audio_whole),
            0,
        )
    )
    audio_queries = normed(audio_self, audio_query_gain)

    def prepare_video(shard_rows):
        return (normed(shard_rows, video_key_gain), shard_rows)

    audio_state_cross = folding(as_heads(audio_queries), prepare_video)(
        start_state(audio_rows, head_count),
        lax.all_gather(video_self, "seq", axis=0, tiled=True),
        jnp.int32(0),
    )
    audio_cross = finish(audio_state_cross)
    video_mixed = (video_self.astype(jnp.float32) + video_cross).astype(jnp.bfloat16)
    audio_mixed = (audio_self.astype(jnp.float32) + audio_cross).astype(jnp.bfloat16)
    return (video_mixed, audio_mixed)


def solution(mesh):
    in_specs = (
        P(("clips", "seq"), "head"),
        P(("clips", "seq"), "head"),
        P(("clips", "seq"), "head"),
        P(("clips", "seq"), "head"),
        P(("clips", "seq"), "head"),
        P(("clips", "seq"), "head"),
        P("head"),
        P("head"),
        P("head"),
        P("head"),
    )
    out_specs = (P(("clips", "seq"), "head"), P(("clips", "seq"), "head"))
    return jax.shard_map(
        per_device, mesh=mesh, in_specs=in_specs, out_specs=out_specs, check_vma=False
    )
```

profile of v0, /device:TPU:0, one launch (start us, length us, event | category | flops | bytes accessed | tf_op | source)
XLA Modules:
  0.0 207.0 jit_solution(10102442533477169547)
XLA Ops:
  7.2 1.8 copy.72
  9.1 0.7 all-gather.6.cloned.1.call-update
  9.9 33.9 %all_gather.20 = bf16[256,1024]{1,0:T(8,128)(2,1)S(1)} all-gather(bf16[32,1024]{1,0:T(8,128)(2,1)} %param.14), channel_id=1, replica_groups=mesh['clips'=2,'seq'=8,'head'=2] {'seq'}, dimensions={0}, use_global_device_ids=true | all-gather | bytes 589824 | tf_op jit(solution)/shard_map/all_gather | solution.py:90
  44.0 23.1 %all-gather.4.cloned.1.call-done = bf16[1024,1024]{0,1:T(8,128)(2,1)} async-done(((bf16[128,1024]{0,1:T(8,128)(2,1)}), bf16[1024,1024]{0,1:T(8,128)(2,1)}) %all-gather.4.cloned.1.call-update) | async-done | bytes 2097168 | tf_op jit(solution)/shard_map/all_gather | solution.py:81
  67.2 2.4 %multiply_reduce_fusion = (f32[8,128]{1,0:T(8,128)S(1)}, f32[8,128,1024]{2,1,0:T(8,128)S(1)}) fusion(bf16[1024,8,128]{0,2,1:T(8,128)(2,1)} %bitcast.127, bf16[128,1024]{1,0:T(8,128)(2,1)S(1)} %copy-done), kind=kOutput, calls=%fused_computation.6 | convolution fusion | flops 270531584 | bytes 6557696 | tf_op jit(solution)/shard_map/qhd,khd->hqk/dot_general | solution.py:32
  69.5 1.9 copy-done.2
  71.4 0.9 fusion.2
  72.4 44.4 %all-gather.6.cloned.1.call-done = bf16[1024,1024]{1,0:T(8,128)(2,1)} async-done(((bf16[128,1024]{1,0:T(8,128)(2,1)}), bf16[1024,1024]{1,0:T(8,128)(2,1)}) %all-gather.6.cloned.1.call-update) | async-done | bytes 2097168 | tf_op jit(solution)/shard_map/all_gather | solution.py:82
  116.8 2.9 %copy.75 = bf16[1024,1024]{0,1:T(8,128)(2,1)S(1)} copy(bf16[1024,1024]{1,0:T(8,128)(2,1)} %all-gather.6.cloned.1.call-done) | data formatting | bytes 4194304 | tf_op jit(solution)/shard_map/all_gather | solution.py:82
  119.7 4.2 %fusion.35 = (f32[128,8]{0,1:T(8,128)S(1)}, bf16[128,8,128]{0,2,1:T(8,128)(2,1)}) fusion(f32[128,8]{0,1:T(8,128)S(1)} %bitcast.135, bf16[1024,8,128]{0,2,1:T(8,128)(2,1)S(1)} %bitcast.125, f32[8,128,1024]{2,1,0:T(8,128)} %copy-done.2, f32[8,128]{1,0:T(8,128)S(1)} %get-tuple-element.15, f32[128,8]{0,1:T(8,128)S(1)} %get-tuple-element.14), kind=kOutput, calls=%fused_computation.43 | convolution fusion | flops 272366592 | bytes 6569984 | tf_op jit(solution)/shard_map/hqk,khd->qhd/dot_general | solution.py:40
  123.9 32.3 %all_gather.21 = bf16[256,1024]{1,0:T(8,128)(2,1)S(1)} all-gather(bf16[32,1024]{1,0:T(8,128)(2,1)S(1)} %copy-done.4), channel_id=1, replica_groups=mesh['clips'=2,'seq'=8,'head'=2] {'seq'}, dimensions={0}, use_global_device_ids=true | all-gather | bytes 589824 | tf_op jit(solution)/shard_map/all_gather | solution.py:91
  156.8 0.4 fusion.54
  157.3 32.4 %all_gather.22 = bf16[256,1024]{1,0:T(8,128)(2,1)S(1)} all-gather(bf16[32,1024]{1,0:T(8,128)(2,1)S(1)} %copy_bitcast_fusion), channel_id=1, replica_groups=mesh['clips'=2,'seq'=8,'head'=2] {'seq'}, dimensions={0}, use_global_device_ids=true | all-gather | bytes 589824 | tf_op jit(solution)/shard_map/all_gather | solution.py:96
  190.2 0.3 reduce_sum.75
  190.8 0.3 mul.152
  191.2 0.7 fusion.67
  191.9 0.4 fusion.31
  192.3 0.4 fusion.12
  192.8 0.9 copy.90
  193.7 2.1 bitcast_reduce_fusion
  195.8 2.3 %fusion.1 = bf16[1024,1024]{0,1:T(8,128)(2,1)S(1)} fusion(bf16[1024,1024]{0,1:T(8,128)(2,1)} %all-gather.8.cloned.1.call-done, f32[1024]{0:T(1024)S(1)} %copy-done.8, f32[1024,8]{0,1:T(8,128)S(1)} %add_rsqrt_fusion), kind=kLoop, calls=%fused_computation.3 | loop fusion | flops 4194304 | bytes 4231168 | tf_op jit(solution)/shard_map/convert_element_type | solution.py:14
  198.0 0.5 fusion.68
  198.9 0.9 fusion.18
  199.8 0.7 fusion.58
  (45 shorter events, 2.3 us)
Async XLA Ops:
  7.2 60.0 %copy-start = (bf16[128,1024]{1,0:T(8,128)(2,1)S(1)}, bf16[128,1024]{1,0:T(8,128)(2,1)}, u32[]{:S(2)}) copy-start(bf16[128,1024]{1,0:T(8,128)(2,1)} %param.10) | copy-start | bytes 786436
  7.2 60.0 %all-gather.4.cloned.1.call-start = ((), (), s32[]{:S(2)}) async-start(), calls=%async_computation | async-start | bytes 2359296 | tf_op jit(solution)/shard_map/all_gather | solution.py:81
  9.1 107.7 %all-gather.6.cloned.1.call-start = ((), (), s32[]{:S(2)}) async-start(), calls=%async_computation.1 | async-start | bytes 2359296 | tf_op jit(solution)/shard_map/all_gather | solution.py:82
  9.8 183.8 %all-gather.8.cloned.1.call-start = ((), (), s32[]{:S(2)}) async-start(), calls=%async_computation.2 | async-start | bytes 2359296 | tf_op jit(solution)/shard_map/all_gather | solution.py:113
  69.5 1.9 copy-start.2
  119.6 4.2 %copy-start.4 = (bf16[32,1024]{1,0:T(8,128)(2,1)S(1)}, bf16[32,1024]{1,0:T(8,128)(2,1)}, u32[]{:S(2)}) copy-start(bf16[32,1024]{1,0:T(8,128)(2,1)} %param.15) | copy-start | bytes 196612
  119.7 36.7 %copy-start.5 = (bf16[32,1024]{1,0:T(8,128)(2,1)S(1)}, bf16[32,1024]{1,0:T(8,128)(2,1)}, u32[]{:S(2)}) copy-start(bf16[32,1024]{1,0:T(8,128)(2,1)} %param.13) | copy-start | bytes 196612
  157.3 33.9 %copy-start.3 = (bf16[128,8,128]{0,2,1:T(8,128)(2,1)S(1)}, bf16[128,8,128]{0,2,1:T(8,128)(2,1)}, u32[]{:S(2)}) copy-start(bf16[128,8,128]{0,2,1:T(8,128)(2,1)} %get-tuple-element.23) | copy-start | bytes 786436
  157.3 33.9 %copy-start.6 = (f32[1024]{0:T(1024)S(1)}, f32[1024]{0:T(1024)}, u32[]{:S(2)}) copy-start(f32[1024]{0:T(1024)} %param.16) | copy-start | bytes 12292
  157.3 33.9 %copy-start.7 = (f32[1024]{0:T(1024)S(1)}, f32[1024]{0:T(1024)}, u32[]{:S(2)}) copy-start(f32[1024]{0:T(1024)} %param.19) | copy-start | bytes 12292
  191.9 3.9 %copy-start.8 = (f32[1024]{0:T(1024)S(1)}, f32[1024]{0:T(1024)}, u32[]{:S(2)}) copy-start(f32[1024]{0:T(1024)} %param.17) | copy-start | bytes 12292
  192.7 5.3 %copy-start.9 = (f32[1024]{0:T(1024)S(1)}, f32[1024]{0:T(1024)}, u32[]{:S(2)}) copy-start(f32[1024]{0:T(1024)} %param.18) | copy-start | bytes 12292
  195.8 3.2 %copy-start.1 = (bf16[1024,1024]{0,1:T(8,128)(2,1)S(1)}, bf16[1024,1024]{0,1:T(8,128)(2,1)}, u32[]{:S(2)}) copy-start(bf16[1024,1024]{0,1:T(8,128)(2,1)} %all-gather.8.cloned.1.call-done) | copy-start | bytes 6291460
Sparse Core Ops, SparseCore 0:
  10.6 56.4 all-gather.3
  69.3 47.4 all-gather.5
  124.0 59.3 all-gather.7
where the time goes:
time: 207 us
  blocking collectives  98.6 us (48%)
  waiting for transfers between devices  68.3 us (33%)
  between operations  14.1 us (7%)
  matrix products  9.73 us (5%)
  local copies, waits for them, and re-layouts  8.84 us (4%)
  other arithmetic  7.39 us (4%)
    all_gather x1, waiting for transfers between devices, per_device(): lax.all_gather(video_v, 'seq', axis=0, tiled=True)  44.4 us
    all_gather x1, blocking collectives, per_device(): lax.all_gather(audio_k, 'seq', axis=0, tiled=True)  33.9 us
    all_gather x1, blocking collectives, per_device(): audio_whole = lax.all_gather(audio_self, 'seq', axis=0, tiled=True)  32.4 us
    all_gather x1, blocking collectives, per_device(): lax.all_gather(audio_v, 'seq', axis=0, tiled=True)  32.3 us
    all_gather x1, waiting for transfers between devices, per_device(): lax.all_gather(video_k, 'seq', axis=0, tiled=True)  23.1 us
    dot_general x4, matrix products, fold_step(): jnp.einsum('hqk,khd->qhd', weights.astype(jnp.bfloat16), values, preferre...  5.85 us
    unnamed x23, local copies, waits for them, and re-layouts  4.84 us
  transfers between devices with their start and end apart: 3, of which 2 were waited for; matrix products, arithmetic and copies ran while one was open for 4% of the time, Pallas kernels for 0%

commit v1 on v0

v1 whole, which is shorter than its diff:
```python
import functools
import math

import jax
import jax.numpy as jnp
from jax import lax
from jax.experimental import pallas as pl
from jax.experimental.pallas import tpu as pltpu
from jax.sharding import PartitionSpec as P

HEAD_DIM = 128
SCALE = HEAD_DIM ** (-0.5)
SCALE_LOG2 = SCALE * math.log2(math.e)
VMEM_LIMIT = 48 * 1024 * 1024
ROW_CHUNK = 256


def normed(tokens, gain_row):
    count = tokens.shape[0]
    head_count = tokens.shape[1] // HEAD_DIM
    entries = tokens.astype(jnp.float32).reshape(count, head_count, HEAD_DIM)
    scaled = entries * lax.rsqrt(jnp.mean(entries * entries, axis=2, keepdims=True) + 1e-06)
    return (scaled.reshape(count, head_count * HEAD_DIM) * gain_row).astype(jnp.bfloat16)


def as_heads(tokens):
    return tokens.reshape(tokens.shape[0], tokens.shape[1] // HEAD_DIM, HEAD_DIM)


def attend(queries, key_rows, values):
    queries, key_rows, values = as_heads(queries), as_heads(key_rows), as_heads(values)
    scores = SCALE * jnp.einsum("qhd,khd->hqk", queries, key_rows, preferred_element_type=jnp.float32)
    weights = jnp.exp(scores - jnp.max(scores, axis=2, keepdims=True))
    total = jnp.sum(weights, axis=2)
    result = jnp.einsum("hqk,khd->qhd", weights.astype(jnp.bfloat16), values, preferred_element_type=jnp.float32)
    result = result / total.T[:, :, None]
    return result.reshape(result.shape[0], result.shape[1] * HEAD_DIM)


def gather_plan(vq, vk, vv, aq, ak, av, vq_gain, vk_gain, aq_gain, ak_gain):
    whole = functools.partial(lax.all_gather, axis_name="seq", axis=0, tiled=True)
    video_self = attend(vq, whole(vk), whole(vv)).astype(jnp.bfloat16)
    audio_self = attend(aq, whole(ak), whole(av)).astype(jnp.bfloat16)
    video_all, audio_all = whole(video_self), whole(audio_self)
    video_cross = attend(normed(video_self, vq_gain), normed(audio_all, ak_gain), audio_all)
    audio_cross = attend(normed(audio_self, aq_gain), normed(video_all, vk_gain), video_all)
    return (
        (video_self.astype(jnp.float32) + video_cross).astype(jnp.bfloat16),
        (audio_self.astype(jnp.float32) + audio_cross).astype(jnp.bfloat16),
    )


def partners(size):
    if size & (size - 1) == 0:
        return [[(a, a ^ step) for a in range(size)] for step in range(size)]
    return [[(a, (a + step) % size) for a in range(size)] for step in range(size)]


def partner_of(me, step, size):
    return me ^ step if size & (size - 1) == 0 else lax.rem(me + step, size)


def pack_kernel(size, *refs):
    ins, outs = refs[:6], refs[6:]
    me = lax.axis_index("seq")
    width = ins[0].shape[1] // size
    for step, out in enumerate(outs):
        column = pl.multiple_of(partner_of(me, step, size) * width, HEAD_DIM)
        row = 0
        for ref in ins:
            out[pl.ds(row, ref.shape[0]), :] = ref[:, pl.ds(column, width)]
            row += ref.shape[0]


def unpack_kernel(size, rows, *refs):
    blocks, (video_out, audio_out) = refs[:-2], refs[-2:]
    me = lax.axis_index("seq")
    width = video_out.shape[1] // size
    for step, block in enumerate(blocks):
        column = pl.multiple_of(partner_of(me, step, size) * width, HEAD_DIM)
        video_out[:, pl.ds(column, width)] = block[pl.ds(0, rows), :]
        audio_out[:, pl.ds(column, width)] = block[pl.ds(rows, block.shape[0] - rows), :]


def dot_t(left, right):
    return lax.dot_general(left, right, (((1,), (1,)), ((), ())), preferred_element_type=jnp.float32)


def dot(left, right):
    return jnp.dot(left, right, preferred_element_type=jnp.float32)


def self_attend(queries, key_rows, values):
    scores = dot_t(queries, key_rows)
    top = jnp.max(scores, axis=1, keepdims=True)
    weights = jnp.exp2((scores - top) * SCALE_LOG2)
    total = jnp.sum(weights, axis=1, keepdims=True)
    return dot(weights.astype(jnp.bfloat16), values) * (1.0 / total)


def cross_attend(queries, key_rows, values):
    weights = jnp.exp2(dot_t(queries, key_rows) * SCALE_LOG2)
    total = jnp.sum(weights, axis=1, keepdims=True)
    return dot(weights.astype(jnp.bfloat16), values) * (1.0 / total)


def unit_rows(tokens):
    entries = tokens.astype(jnp.float32)
    return entries * lax.rsqrt(jnp.mean(entries * entries, axis=1, keepdims=True) + 1e-06)


def attention_kernel(size, video_rows, audio_rows, *refs):
    blocks = refs[:size]
    gains = refs[size : size + 4]
    outs = refs[size + 4 : 2 * size + 4]
    vk, vv, ak, av, aq, v_self, a_self, v_query, v_key = refs[2 * size + 4 :]
    me = lax.axis_index("seq")
    heads = blocks[0].shape[1] // HEAD_DIM
    rv, ra = video_rows, audio_rows
    for head in range(heads):
        cols = pl.ds(head * HEAD_DIM, HEAD_DIM)
        vq_gain, vk_gain, aq_gain, ak_gain = [gain[pl.ds(me * heads + head, 1), :] for gain in gains]
        for step, block in enumerate(blocks):
            v_at, a_at = pl.ds(step * rv, rv), pl.ds(step * ra, ra)
            vk[v_at, :] = block[pl.ds(rv, rv), cols]
            vv[v_at, :] = block[pl.ds(2 * rv, rv), cols]
            aq[a_at, :] = block[pl.ds(3 * rv, ra), cols]
            ak[a_at, :] = block[pl.ds(3 * rv + ra, ra), cols]
            av[a_at, :] = block[pl.ds(3 * rv + 2 * ra, ra), cols]
        a_result = self_attend(aq[...], ak[...], av[...]).astype(jnp.bfloat16)
        a_self[...] = a_result
        a_unit = unit_rows(a_result)
        a_query = (a_unit * aq_gain).astype(jnp.bfloat16)
        a_key = (a_unit * ak_gain).astype(jnp.bfloat16)
        for step, block in enumerate(blocks):
            v_at = pl.ds(step * rv, rv)
            result = self_attend(block[pl.ds(0, rv), cols], vk[...], vv[...]).astype(jnp.bfloat16)
            v_self[v_at, :] = result
            unit = unit_rows(result)
            v_key[v_at, :] = (unit * vk_gain).astype(jnp.bfloat16)
            cross = cross_attend((unit * vq_gain).astype(jnp.bfloat16), a_key, a_result)
            outs[step][pl.ds(0, rv), cols] = (result.astype(jnp.float32) + cross).astype(jnp.bfloat16)
        cross = cross_attend(a_query, v_key[...], v_self[...])
        mixed = (a_result.astype(jnp.float32) + cross).astype(jnp.bfloat16)
        for step in range(size):
            outs[step][pl.ds(rv, ra), cols] = mixed[step * ra : (step + 1) * ra, :]


def head_plan(size, vq, vk, vv, aq, ak, av, *gains):
    rv, columns = vq.shape
    ra = aq.shape[0]
    width = columns // size
    tall = 3 * (rv + ra)
    params = pltpu.CompilerParams(vmem_limit_bytes=VMEM_LIMIT)
    in_vmem = pl.BlockSpec(memory_space=pltpu.VMEM)
    moves = partners(size)

    sends = pl.pallas_call(
        functools.partial(pack_kernel, size),
        out_shape=[jax.ShapeDtypeStruct((tall, width), vq.dtype)] * size,
        in_specs=[in_vmem] * 6,
        out_specs=[in_vmem] * size,
        compiler_params=params,
        name="pack",
    )(vq, vk, vv, aq, ak, av)
    blocks = [sends[0]] + [lax.ppermute(sends[step], "seq", moves[step]) for step in range(1, size)]
    gains = [gain.reshape(columns // HEAD_DIM, HEAD_DIM) for gain in gains]
    tv, ta = rv * size, ra * size
    results = pl.pallas_call(
        functools.partial(attention_kernel, size, rv, ra),
        out_shape=[jax.ShapeDtypeStruct((rv + ra, width), vq.dtype)] * size,
        in_specs=[in_vmem] * (size + 4),
        out_specs=[in_vmem] * size,
        scratch_shapes=[
            pltpu.VMEM((rows, HEAD_DIM), jnp.bfloat16) for rows in (tv, tv, ta, ta, ta, tv, ta, tv, tv)
        ],
        compiler_params=params,
        cost_estimate=pl.CostEstimate(
            flops=4 * width * (tv * tv + ta * ta + 2 * tv * ta),
            bytes_accessed=8 * tv * width,
            transcendentals=(width // HEAD_DIM) * (tv * tv + ta * ta + 2 * tv * ta),
        ),
        name="attention",
    )(*blocks, *gains)
    back = [results[0]] + [
        lax.ppermute(results[step], "seq", [(b, a) for a, b in moves[step]]) for step in range(1, size)
    ]
    return tuple(
        pl.pallas_call(
            functools.partial(unpack_kernel, size, rv),
            out_shape=[
                jax.ShapeDtypeStruct((rv, columns), vq.dtype),
                jax.ShapeDtypeStruct((ra, columns), vq.dtype),
            ],
            in_specs=[in_vmem] * size,
            out_specs=[in_vmem] * 2,
            compiler_params=params,
            name="unpack",
        )(*back)
    )


def solution(mesh):
    size = mesh.shape["seq"]

    def per_device(*args):
        heads = args[0].shape[1] // HEAD_DIM
        if heads % size == 0:
            return head_plan(size, *args)
        return gather_plan(*args)

    tokens = P(("clips", "seq"), "head")
    return jax.shard_map(
        per_device,
        mesh=mesh,
        in_specs=(tokens,) * 6 + (P("head"),) * 4,
        out_specs=(tokens, tokens),
        check_vma=False,
    )
```

time: 207 us -> 59.2 us (0.29)
  blocking collectives: 98.6 us -> 0 us
  waiting for transfers between devices: 68.3 us -> 17.3 us
  starting transfers between devices: 0.12 us -> 27.6 us
  between operations: 14.1 us -> 0.7 us
  matrix products: 9.73 us -> 0 us
  other arithmetic: 7.39 us -> 0 us
  Pallas kernels: 0 us -> 7.22 us
  local copies, waits for them, and re-layouts: 8.84 us -> 6.04 us
    all_gather x3 -> x0, blocking collectives: 98.6 us -> none  [the longest x1 33.9 us: per_device(): lax.all_gather(audio_k, 'seq', axis=0, tiled=True)]
    all_gather x3 -> x0, waiting for transfers between devices: 67.5 us -> none  [the longest x1 44.4 us: per_device(): lax.all_gather(video_v, 'seq', axis=0, tiled=True)]
    ppermute x0 -> x14, starting transfers between devices: none -> 27.6 us  [the longest x7 14.5 us: head_plan(): lax.ppermute(results[step], 'seq', [(b, a) for a, b in moves[step]])]
    ppermute x0 -> x14, waiting for transfers between devices: none -> 17.3 us  [the longest x7 12.9 us: head_plan(): lax.ppermute(sends[step], 'seq', moves[step])]
    dot_general x8 -> x0, matrix products: 9.73 us -> none  [the longest x4 5.85 us: fold_step(): jnp.einsum('hqk,khd->qhd', weights.astype(jnp.bfloat16), values, preferre...]
    pallas_call x0 -> x3, Pallas kernels: none -> 7.22 us  [the longest x1 6.16 us: head_plan(): pl.pallas_call(functools.partial(attention_kernel, size, rv, ra), out_sha...]
    reduce_sum x6 -> x0, other arithmetic: 4.22 us -> none  [the longest x2 2.41 us: normed(): jnp.mean(entries * entries, axis=2, keepdims=True) + 1e-06]
    all_gather x4 -> x0, local copies, waits for them, and re-layouts: 3.46 us -> none  [the longest x1 2.85 us: per_device(): lax.all_gather(video_v, 'seq', axis=0, tiled=True)]
  transfers between devices with their start and end apart: 3 -> 14, of which waited for: 2 -> 6; matrix products, arithmetic and copies ran while one was open for 4% -> 0% of each run, Pallas kernels for 0% -> 0%
where the time goes in v1:
time: 59.2 us; the launch traced here: 58.8 us
  starting transfers between devices  27.6 us (47%)
  waiting for transfers between devices  17.3 us (29%)
  Pallas kernels  7.22 us (12%)
  local copies, waits for them, and re-layouts  6.04 us (10%)
  between operations  0.7 us (1%)
    ppermute x7, starting transfers between devices, head_plan(): lax.ppermute(results[step], 'seq', [(b, a) for a, b in moves[step]])  14.5 us
    ppermute x7, starting transfers between devices, head_plan(): lax.ppermute(sends[step], 'seq', moves[step])  13 us
    ppermute x7, waiting for transfers between devices, head_plan(): lax.ppermute(sends[step], 'seq', moves[step])  12.9 us
    pallas_call x1, Pallas kernels, head_plan(): pl.pallas_call(functools.partial(attention_kernel, size, rv, ra), out_sha...  6.16 us
    unnamed x20, local copies, waits for them, and re-layouts  6.04 us
    ppermute x7, waiting for transfers between devices, head_plan(): lax.ppermute(results[step], 'seq', [(b, a) for a, b in moves[step]])  4.34 us
  transfers between devices with their start and end apart: 14, of which 6 were waited for; matrix products, arithmetic and copies ran while one was open for 0% of the time, Pallas kernels for 0%

profile of v1, /device:TPU:0, one launch (start us, length us, event | category | flops | bytes accessed | tf_op | source)
XLA Modules:
  0.0 58.8 jit_solution(14186149509722438600)
XLA Ops:
  0.6 0.9 %copy-done = bf16[128,1024]{1,0:T(8,128)(2,1)S(1)} copy-done((bf16[128,1024]{1,0:T(8,128)(2,1)S(1)}, bf16[128,1024]{1,0:T(8,128)(2,1)}, u32[]{:S(2)}) %copy-start) | copy-done | bytes 262168
  1.6 0.9 %copy-done.1 = bf16[128,1024]{1,0:T(8,128)(2,1)S(1)} copy-done((bf16[128,1024]{1,0:T(8,128)(2,1)S(1)}, bf16[128,1024]{1,0:T(8,128)(2,1)}, u32[]{:S(2)}) %copy-start.1) | copy-done | bytes 262168
  2.5 0.9 %copy-done.2 = bf16[128,1024]{1,0:T(8,128)(2,1)S(1)} copy-done((bf16[128,1024]{1,0:T(8,128)(2,1)S(1)}, bf16[128,1024]{1,0:T(8,128)(2,1)}, u32[]{:S(2)}) %copy-start.2) | copy-done | bytes 262168
  3.5 0.8 %copy-done.3 = bf16[32,1024]{1,0:T(8,128)(2,1)S(1)} copy-done((bf16[32,1024]{1,0:T(8,128)(2,1)S(1)}, bf16[32,1024]{1,0:T(8,128)(2,1)}, u32[]{:S(2)}) %copy-start.3) | copy-done | bytes 65560
  4.3 0.8 %copy-done.4 = bf16[32,1024]{1,0:T(8,128)(2,1)S(1)} copy-done((bf16[32,1024]{1,0:T(8,128)(2,1)S(1)}, bf16[32,1024]{1,0:T(8,128)(2,1)}, u32[]{:S(2)}) %copy-start.4) | copy-done | bytes 65560
  5.2 0.8 %copy-done.5 = bf16[32,1024]{1,0:T(8,128)(2,1)S(1)} copy-done((bf16[32,1024]{1,0:T(8,128)(2,1)S(1)}, bf16[32,1024]{1,0:T(8,128)(2,1)}, u32[]{:S(2)}) %copy-start.5) | copy-done | bytes 65560
  6.3 3.0 %collective-permute-start = (bf16[480,128]{1,0:T(8,128)(2,1)S(1)}, bf16[480,128]{1,0:T(8,128)(2,1)S(1)}, u32[]{:S(2)}, u32[]{:S(2)}) collective-permute-start(bf16[480,128]{1,0:T(8,128)(2,1)S(1)} %get-tuple-element.19), channel_id=1, source_target_pairs={{0,2},{2,0},{4,6},{6,4},{8,10},{10,8},{12,14},{14,12},{1,3},{3,1},... | collective-permute-start | bytes 368648 | tf_op jit(solution)/shard_map/ppermute | solution.py:166
  9.3 1.6 %collective-permute-start.1 = (bf16[480,128]{1,0:T(8,128)(2,1)S(1)}, bf16[480,128]{1,0:T(8,128)(2,1)S(1)}, u32[]{:S(2)}, u32[]{:S(2)}) collective-permute-start(bf16[480,128]{1,0:T(8,128)(2,1)S(1)} %get-tuple-element.20), channel_id=1, source_target_pairs={{0,4},{2,6},{4,0},{6,2},{8,12},{10,14},{12,8},{14,10},{1,5},{3,7},... | collective-permute-start | bytes 368648 | tf_op jit(solution)/shard_map/ppermute | solution.py:166
  10.9 3.0 %collective-permute-start.3 = (bf16[480,128]{1,0:T(8,128)(2,1)S(1)}, bf16[480,128]{1,0:T(8,128)(2,1)S(1)}, u32[]{:S(2)}, u32[]{:S(2)}) collective-permute-start(bf16[480,128]{1,0:T(8,128)(2,1)S(1)} %get-tuple-element.22), channel_id=1, source_target_pairs={{0,8},{2,10},{4,12},{6,14},{8,0},{10,2},{12,4},{14,6},{1,9},{3,11}... | collective-permute-start | bytes 368648 | tf_op jit(solution)/shard_map/ppermute | solution.py:166
  13.9 1.3 %collective-permute-start.4 = (bf16[480,128]{1,0:T(8,128)(2,1)S(1)}, bf16[480,128]{1,0:T(8,128)(2,1)S(1)}, u32[]{:S(2)}, u32[]{:S(2)}) collective-permute-start(bf16[480,128]{1,0:T(8,128)(2,1)S(1)} %get-tuple-element.23), channel_id=1, source_target_pairs={{0,10},{2,8},{4,14},{6,12},{8,2},{10,0},{12,6},{14,4},{1,11},{3,9}... | collective-permute-start | bytes 368648 | tf_op jit(solution)/shard_map/ppermute | solution.py:166
  15.2 3.6 %collective-permute-start.5 = (bf16[480,128]{1,0:T(8,128)(2,1)S(1)}, bf16[480,128]{1,0:T(8,128)(2,1)S(1)}, u32[]{:S(2)}, u32[]{:S(2)}) collective-permute-start(bf16[480,128]{1,0:T(8,128)(2,1)S(1)} %get-tuple-element.24), channel_id=1, source_target_pairs={{0,12},{2,14},{4,8},{6,10},{8,4},{10,6},{12,0},{14,2},{1,13},{3,15... | collective-permute-start | bytes 368648 | tf_op jit(solution)/shard_map/ppermute | solution.py:166
  18.8 0.5 collective-permute-done.1.refs_2_
  20.0 12.3 %collective-permute-done.4.refs_5_ = bf16[480,128]{1,0:T(8,128)(2,1)S(1)} collective-permute-done((bf16[480,128]{1,0:T(8,128)(2,1)S(1)}, bf16[480,128]{1,0:T(8,128)(2,1)S(1)}, u32[]{:S(2)}, u32[]{:S(2)}) %collective-permute-start.4) | collective-permute-done | bytes 122912 | tf_op jit(solution)/shard_map/ppermute | solution.py:166
  32.3 0.7 %copy-done.7 = f32[1024]{0:T(1024)S(1)} copy-done((f32[1024]{0:T(1024)S(1)}, f32[1024]{0:T(1024)}, u32[]{:S(2)}) %copy-start.7) | copy-done | bytes 4120
  32.9 6.2 %attention.1 = (bf16[160,128]{1,0:T(8,128)(2,1)S(1)}, bf16[160,128]{1,0:T(8,128)(2,1)S(1)}, bf16[160,128]{1,0:T(8,128)(2,1)S(1)}, bf16[160,128]{1,0:T(8,128)(2,1...) custom-call(bf16[480,128]{1,0:T(8,128)(2,1)S(1)} %get-tuple-element., ...), custom_call_target="tpu_custom_call" | custom-call | flops 838860800 | bytes 1048576 | tf_op jit(solution)/shard_map/attention/pallas_call | solution.py:169
  39.1 0.8 %collective-permute-start.7 = (bf16[160,128]{1,0:T(8,128)(2,1)S(1)}, bf16[160,128]{1,0:T(8,128)(2,1)S(1)}, u32[]{:S(2)}, u32[]{:S(2)}) collective-permute-start(bf16[160,128]{1,0:T(8,128)(2,1)S(1)} %get-tuple-element.27), channel_id=1, source_target_pairs={{2,0},{0,2},{6,4},{4,6},{10,8},{8,10},{14,12},{12,14},{3,1},{1,3},... | collective-permute-start | bytes 122888 | tf_op jit(solution)/shard_map/ppermute | solution.py:186
  39.9 4.5 %collective-permute-start.8 = (bf16[160,128]{1,0:T(8,128)(2,1)S(1)}, bf16[160,128]{1,0:T(8,128)(2,1)S(1)}, u32[]{:S(2)}, u32[]{:S(2)}) collective-permute-start(bf16[160,128]{1,0:T(8,128)(2,1)S(1)} %get-tuple-element.28), channel_id=1, source_target_pairs={{4,0},{6,2},{0,4},{2,6},{12,8},{14,10},{8,12},{10,14},{5,1},{7,3},... | collective-permute-start | bytes 122888 | tf_op jit(solution)/shard_map/ppermute | solution.py:186
  44.4 1.0 %collective-permute-start.9 = (bf16[160,128]{1,0:T(8,128)(2,1)S(1)}, bf16[160,128]{1,0:T(8,128)(2,1)S(1)}, u32[]{:S(2)}, u32[]{:S(2)}) collective-permute-start(bf16[160,128]{1,0:T(8,128)(2,1)S(1)} %get-tuple-element.29), channel_id=1, source_target_pairs={{6,0},{4,2},{2,4},{0,6},{14,8},{12,10},{10,12},{8,14},{7,1},{5,3},... | collective-permute-start | bytes 122888 | tf_op jit(solution)/shard_map/ppermute | solution.py:186
  45.4 3.5 %collective-permute-start.10 = (bf16[160,128]{1,0:T(8,128)(2,1)S(1)}, bf16[160,128]{1,0:T(8,128)(2,1)S(1)}, u32[]{:S(2)}, u32[]{:S(2)}) collective-permute-start(bf16[160,128]{1,0:T(8,128)(2,1)S(1)} %get-tuple-element.30), channel_id=1, source_target_pairs={{8,0},{10,2},{12,4},{14,6},{0,8},{2,10},{4,12},{6,14},{9,1},{11,3}... | collective-permute-start | bytes 122888 | tf_op jit(solution)/shard_map/ppermute | solution.py:186
  48.9 2.4 %collective-permute-start.12 = (bf16[160,128]{1,0:T(8,128)(2,1)S(1)}, bf16[160,128]{1,0:T(8,128)(2,1)S(1)}, u32[]{:S(2)}, u32[]{:S(2)}) collective-permute-start(bf16[160,128]{1,0:T(8,128)(2,1)S(1)} %get-tuple-element.32), channel_id=1, source_target_pairs={{12,0},{14,2},{8,4},{10,6},{4,8},{6,10},{0,12},{2,14},{13,1},{15,3... | collective-permute-start | bytes 122888 | tf_op jit(solution)/shard_map/ppermute | solution.py:186
  51.3 2.4 %collective-permute-start.13 = (bf16[160,128]{1,0:T(8,128)(2,1)S(1)}, bf16[160,128]{1,0:T(8,128)(2,1)S(1)}, u32[]{:S(2)}, u32[]{:S(2)}) collective-permute-start(bf16[160,128]{1,0:T(8,128)(2,1)S(1)} %get-tuple-element.33), channel_id=1, source_target_pairs={{14,0},{12,2},{10,4},{8,6},{6,8},{4,10},{2,12},{0,14},{15,1},{13,3... | collective-permute-start | bytes 122888 | tf_op jit(solution)/shard_map/ppermute | solution.py:186
  53.6 1.4 %collective-permute-done.11.refs_5_ = bf16[160,128]{1,0:T(8,128)(2,1)S(1)} collective-permute-done((bf16[160,128]{1,0:T(8,128)(2,1)S(1)}, bf16[160,128]{1,0:T(8,128)(2,1)S(1)}, u32[]{:S(2)}, u32[]{:S(2)}) %collective-permute-start.11) | collective-permute-done | bytes 40992 | tf_op jit(solution)/shard_map/ppermute | solution.py:186
  55.1 2.9 %collective-permute-done.13.refs_7_ = bf16[160,128]{1,0:T(8,128)(2,1)S(1)} collective-permute-done((bf16[160,128]{1,0:T(8,128)(2,1)S(1)}, bf16[160,128]{1,0:T(8,128)(2,1)S(1)}, u32[]{:S(2)}, u32[]{:S(2)}) %collective-permute-start.13) | collective-permute-done | bytes 40992 | tf_op jit(solution)/shard_map/ppermute | solution.py:186
  58.0 0.8 %unpack.1 = (bf16[128,1024]{1,0:T(8,128)(2,1)}, bf16[32,1024]{1,0:T(8,128)(2,1)}) custom-call(bf16[160,128]{1,0:T(8,128)(2,1)S(1)} %get-tuple-element.26.refs_0_, bf16[160,128]{1,0:T(8,128)(2,1)S(1)} %collective-permute-done.7.refs_1_, bf16[160,128]{1,0:T(8,128)(2,1)S(1)} %collective-permute-done.8.refs_2_, ...), custom_call_target="tpu_custom_call" | custom-call | tf_op jit(solution)/shard_map/unpack/pallas_call | solution.py:189
  (27 shorter events, 1.0 us)
Async XLA Ops:
  0.6 1.0 %copy-start = (bf16[128,1024]{1,0:T(8,128)(2,1)S(1)}, bf16[128,1024]{1,0:T(8,128)(2,1)}, u32[]{:S(2)}) copy-start(bf16[128,1024]{1,0:T(8,128)(2,1)} %refs_0_.1) | copy-start | bytes 786436
  1.6 0.9 %copy-start.1 = (bf16[128,1024]{1,0:T(8,128)(2,1)S(1)}, bf16[128,1024]{1,0:T(8,128)(2,1)}, u32[]{:S(2)}) copy-start(bf16[128,1024]{1,0:T(8,128)(2,1)} %refs_1_.1) | copy-start | bytes 786436
  2.5 0.9 %copy-start.2 = (bf16[128,1024]{1,0:T(8,128)(2,1)S(1)}, bf16[128,1024]{1,0:T(8,128)(2,1)}, u32[]{:S(2)}) copy-start(bf16[128,1024]{1,0:T(8,128)(2,1)} %refs_2_.1) | copy-start | bytes 786436
  3.5 0.8 %copy-start.3 = (bf16[32,1024]{1,0:T(8,128)(2,1)S(1)}, bf16[32,1024]{1,0:T(8,128)(2,1)}, u32[]{:S(2)}) copy-start(bf16[32,1024]{1,0:T(8,128)(2,1)} %refs_3_.1) | copy-start | bytes 196612
  4.3 0.8 %copy-start.4 = (bf16[32,1024]{1,0:T(8,128)(2,1)S(1)}, bf16[32,1024]{1,0:T(8,128)(2,1)}, u32[]{:S(2)}) copy-start(bf16[32,1024]{1,0:T(8,128)(2,1)} %refs_4_.1) | copy-start | bytes 196612
  5.2 0.8 %copy-start.5 = (bf16[32,1024]{1,0:T(8,128)(2,1)S(1)}, bf16[32,1024]{1,0:T(8,128)(2,1)}, u32[]{:S(2)}) copy-start(bf16[32,1024]{1,0:T(8,128)(2,1)} %refs_5_.1) | copy-start | bytes 196612
  6.3 8.9 %collective-permute-start = (bf16[480,128]{1,0:T(8,128)(2,1)S(1)}, bf16[480,128]{1,0:T(8,128)(2,1)S(1)}, u32[]{:S(2)}, u32[]{:S(2)}) collective-permute-start(bf16[480,128]{1,0:T(8,128)(2,1)S(1)} %get-tuple-element.19), channel_id=1, source_target_pairs={{0,2},{2,0},{4,6},{6,4},{8,10},{10,8},{12,14},{14,12},{1,3},{3,1},... | collective-permute-start | bytes 368648 | tf_op jit(solution)/shard_map/ppermute | solution.py:166
  9.3 22.9 %copy-start.8 = (f32[1024]{0:T(1024)S(1)}, f32[1024]{0:T(1024)}, u32[]{:S(2)}) copy-start(f32[1024]{0:T(1024)} %param.18) | copy-start | bytes 12292
  9.3 22.9 %copy-start.9 = (f32[1024]{0:T(1024)S(1)}, f32[1024]{0:T(1024)}, u32[]{:S(2)}) copy-start(f32[1024]{0:T(1024)} %param.19) | copy-start | bytes 12292
  9.3 10.0 %collective-permute-start.1 = (bf16[480,128]{1,0:T(8,128)(2,1)S(1)}, bf16[480,128]{1,0:T(8,128)(2,1)S(1)}, u32[]{:S(2)}, u32[]{:S(2)}) collective-permute-start(bf16[480,128]{1,0:T(8,128)(2,1)S(1)} %get-tuple-element.20), channel_id=1, source_target_pairs={{0,4},{2,6},{4,0},{6,2},{8,12},{10,14},{12,8},{14,10},{1,5},{3,7},... | collective-permute-start | bytes 368648 | tf_op jit(solution)/shard_map/ppermute | solution.py:166
  10.9 8.9 %collective-permute-start.2 = (bf16[480,128]{1,0:T(8,128)(2,1)S(1)}, bf16[480,128]{1,0:T(8,128)(2,1)S(1)}, u32[]{:S(2)}, u32[]{:S(2)}) collective-permute-start(bf16[480,128]{1,0:T(8,128)(2,1)S(1)} %get-tuple-element.21), channel_id=1, source_target_pairs={{0,6},{2,4},{4,2},{6,0},{8,14},{10,12},{12,10},{14,8},{1,7},{3,5},... | collective-permute-start | bytes 368648 | tf_op jit(solution)/shard_map/ppermute | solution.py:166
  10.9 9.1 %collective-permute-start.3 = (bf16[480,128]{1,0:T(8,128)(2,1)S(1)}, bf16[480,128]{1,0:T(8,128)(2,1)S(1)}, u32[]{:S(2)}, u32[]{:S(2)}) collective-permute-start(bf16[480,128]{1,0:T(8,128)(2,1)S(1)} %get-tuple-element.22), channel_id=1, source_target_pairs={{0,8},{2,10},{4,12},{6,14},{8,0},{10,2},{12,4},{14,6},{1,9},{3,11}... | collective-permute-start | bytes 368648 | tf_op jit(solution)/shard_map/ppermute | solution.py:166
  13.9 18.3 %collective-permute-start.4 = (bf16[480,128]{1,0:T(8,128)(2,1)S(1)}, bf16[480,128]{1,0:T(8,128)(2,1)S(1)}, u32[]{:S(2)}, u32[]{:S(2)}) collective-permute-start(bf16[480,128]{1,0:T(8,128)(2,1)S(1)} %get-tuple-element.23), channel_id=1, source_target_pairs={{0,10},{2,8},{4,14},{6,12},{8,2},{10,0},{12,6},{14,4},{1,11},{3,9}... | collective-permute-start | bytes 368648 | tf_op jit(solution)/shard_map/ppermute | solution.py:166
  15.2 17.1 %collective-permute-start.5 = (bf16[480,128]{1,0:T(8,128)(2,1)S(1)}, bf16[480,128]{1,0:T(8,128)(2,1)S(1)}, u32[]{:S(2)}, u32[]{:S(2)}) collective-permute-start(bf16[480,128]{1,0:T(8,128)(2,1)S(1)} %get-tuple-element.24), channel_id=1, source_target_pairs={{0,12},{2,14},{4,8},{6,10},{8,4},{10,6},{12,0},{14,2},{1,13},{3,15... | collective-permute-start | bytes 368648 | tf_op jit(solution)/shard_map/ppermute | solution.py:166
  19.3 12.9 %collective-permute-start.6 = (bf16[480,128]{1,0:T(8,128)(2,1)S(1)}, bf16[480,128]{1,0:T(8,128)(2,1)S(1)}, u32[]{:S(2)}, u32[]{:S(2)}) collective-permute-start(bf16[480,128]{1,0:T(8,128)(2,1)S(1)} %get-tuple-element.25), channel_id=1, source_target_pairs={{0,14},{2,12},{4,10},{6,8},{8,6},{10,4},{12,2},{14,0},{1,15},{3,13... | collective-permute-start | bytes 368648 | tf_op jit(solution)/shard_map/ppermute | solution.py:166
  32.2 0.7 %copy-start.7 = (f32[1024]{0:T(1024)S(1)}, f32[1024]{0:T(1024)}, u32[]{:S(2)}) copy-start(f32[1024]{0:T(1024)} %param.17) | copy-start | bytes 12292
  32.2 0.7 %copy-start.6 = (f32[1024]{0:T(1024)S(1)}, f32[1024]{0:T(1024)}, u32[]{:S(2)}) copy-start(f32[1024]{0:T(1024)} %param.16) | copy-start | bytes 12292
  39.1 9.8 %collective-permute-start.7 = (bf16[160,128]{1,0:T(8,128)(2,1)S(1)}, bf16[160,128]{1,0:T(8,128)(2,1)S(1)}, u32[]{:S(2)}, u32[]{:S(2)}) collective-permute-start(bf16[160,128]{1,0:T(8,128)(2,1)S(1)} %get-tuple-element.27), channel_id=1, source_target_pairs={{2,0},{0,2},{6,4},{4,6},{10,8},{8,10},{14,12},{12,14},{3,1},{1,3},... | collective-permute-start | bytes 122888 | tf_op jit(solution)/shard_map/ppermute | solution.py:186
  39.9 11.4 %collective-permute-start.8 = (bf16[160,128]{1,0:T(8,128)(2,1)S(1)}, bf16[160,128]{1,0:T(8,128)(2,1)S(1)}, u32[]{:S(2)}, u32[]{:S(2)}) collective-permute-start(bf16[160,128]{1,0:T(8,128)(2,1)S(1)} %get-tuple-element.28), channel_id=1, source_target_pairs={{4,0},{6,2},{0,4},{2,6},{12,8},{14,10},{8,12},{10,14},{5,1},{7,3},... | collective-permute-start | bytes 122888 | tf_op jit(solution)/shard_map/ppermute | solution.py:186
  44.4 9.2 %collective-permute-start.9 = (bf16[160,128]{1,0:T(8,128)(2,1)S(1)}, bf16[160,128]{1,0:T(8,128)(2,1)S(1)}, u32[]{:S(2)}, u32[]{:S(2)}) collective-permute-start(bf16[160,128]{1,0:T(8,128)(2,1)S(1)} %get-tuple-element.29), channel_id=1, source_target_pairs={{6,0},{4,2},{2,4},{0,6},{14,8},{12,10},{10,12},{8,14},{7,1},{5,3},... | collective-permute-start | bytes 122888 | tf_op jit(solution)/shard_map/ppermute | solution.py:186
  45.4 8.2 %collective-permute-start.10 = (bf16[160,128]{1,0:T(8,128)(2,1)S(1)}, bf16[160,128]{1,0:T(8,128)(2,1)S(1)}, u32[]{:S(2)}, u32[]{:S(2)}) collective-permute-start(bf16[160,128]{1,0:T(8,128)(2,1)S(1)} %get-tuple-element.30), channel_id=1, source_target_pairs={{8,0},{10,2},{12,4},{14,6},{0,8},{2,10},{4,12},{6,14},{9,1},{11,3}... | collective-permute-start | bytes 122888 | tf_op jit(solution)/shard_map/ppermute | solution.py:186
  48.9 6.1 %collective-permute-start.11 = (bf16[160,128]{1,0:T(8,128)(2,1)S(1)}, bf16[160,128]{1,0:T(8,128)(2,1)S(1)}, u32[]{:S(2)}, u32[]{:S(2)}) collective-permute-start(bf16[160,128]{1,0:T(8,128)(2,1)S(1)} %get-tuple-element.31), channel_id=1, source_target_pairs={{10,0},{8,2},{14,4},{12,6},{2,8},{0,10},{6,12},{4,14},{11,1},{9,3}... | collective-permute-start | bytes 122888 | tf_op jit(solution)/shard_map/ppermute | solution.py:186
  48.9 6.2 %collective-permute-start.12 = (bf16[160,128]{1,0:T(8,128)(2,1)S(1)}, bf16[160,128]{1,0:T(8,128)(2,1)S(1)}, u32[]{:S(2)}, u32[]{:S(2)}) collective-permute-start(bf16[160,128]{1,0:T(8,128)(2,1)S(1)} %get-tuple-element.32), channel_id=1, source_target_pairs={{12,0},{14,2},{8,4},{10,6},{4,8},{6,10},{0,12},{2,14},{13,1},{15,3... | collective-permute-start | bytes 122888 | tf_op jit(solution)/shard_map/ppermute | solution.py:186
  51.3 6.7 %collective-permute-start.13 = (bf16[160,128]{1,0:T(8,128)(2,1)S(1)}, bf16[160,128]{1,0:T(8,128)(2,1)S(1)}, u32[]{:S(2)}, u32[]{:S(2)}) collective-permute-start(bf16[160,128]{1,0:T(8,128)(2,1)S(1)} %get-tuple-element.33), channel_id=1, source_target_pairs={{14,0},{12,2},{10,4},{8,6},{6,8},{4,10},{2,12},{0,14},{15,1},{13,3... | collective-permute-start | bytes 122888 | tf_op jit(solution)/shard_map/ppermute | solution.py:186

commit v2 on v1

--- a/solution.py
+++ b/solution.py
@@ -60,23 +60,46 @@
     return me ^ step if size & (size - 1) == 0 else lax.rem(me + step, size)
 
 
+def send_order(size):
+    middle = size // 2
+    return sorted(range(1, size), key=lambda step: (step & (step - 1) and 1 + (step < middle), step))
+
+
+def return_order(size):
+    return range(size - 1, 0, -1)
+
+
+def exchange(blocks, moves, order):
+    return [blocks[0]] + [lax.ppermute(blocks[step], "seq", moves[step]) for step in order]
+
+
 def pack_kernel(size, *refs):
-    ins, outs = refs[:6], refs[6:]
+    ins, outs, sem = refs[:6], refs[6:-1], refs[-1]
     me = lax.axis_index("seq")
     width = ins[0].shape[1] // size
+    copies = []
     for step, out in enumerate(outs):
         column = pl.multiple_of(partner_of(me, step, size) * width, HEAD_DIM)
         row = 0
         for ref in ins:
-            out[pl.ds(row, ref.shape[0]), :] = ref[:, pl.ds(column, width)]
-            row += ref.shape[0]
+            rows = ref.shape[0]
+            copies.append(
+                pltpu.make_async_copy(
+                    ref.at[:, pl.ds(column, width)], out.at[pl.ds(row, rows), :], sem.at[len(copies)]
+                )
+            )
+            row += rows
+    for copy in copies:
+        copy.start()
+    for copy in copies:
+        copy.wait()
 
 
 def unpack_kernel(size, rows, *refs):
     blocks, (video_out, audio_out) = refs[:-2], refs[-2:]
     me = lax.axis_index("seq")
     width = video_out.shape[1] // size
-    for step, block in enumerate(blocks):
+    for step, block in zip((0, *return_order(size)), blocks):
         column = pl.multiple_of(partner_of(me, step, size) * width, HEAD_DIM)
         video_out[:, pl.ds(column, width)] = block[pl.ds(0, rows), :]
         audio_out[:, pl.ds(column, width)] = block[pl.ds(rows, block.shape[0] - rows), :]
@@ -112,7 +135,8 @@
 def attention_kernel(size, video_rows, audio_rows, *refs):
     blocks = refs[:size]
     gains = refs[size : size + 4]
-    outs = refs[size + 4 : 2 * size + 4]
+    by_step = refs[size + 4 : 2 * size + 4]
+    outs = [by_step[step] for step in (0, *send_order(size))]
     vk, vv, ak, av, aq, v_self, a_self, v_query, v_key = refs[2 * size + 4 :]
     me = lax.axis_index("seq")
     heads = blocks[0].shape[1] // HEAD_DIM
@@ -158,12 +182,13 @@
     sends = pl.pallas_call(
         functools.partial(pack_kernel, size),
         out_shape=[jax.ShapeDtypeStruct((tall, width), vq.dtype)] * size,
-        in_specs=[in_vmem] * 6,
+        in_specs=[pl.BlockSpec(memory_space=pltpu.HBM)] * 6,
         out_specs=[in_vmem] * size,
+        scratch_shapes=[pltpu.SemaphoreType.DMA((6 * size,))],
         compiler_params=params,
         name="pack",
-    )(vq, vk, vv, aq, ak, av)
-    blocks = [sends[0]] + [lax.ppermute(sends[step], "seq", moves[step]) for step in range(1, size)]
+    )(*[pltpu.with_memory_space_constraint(x, pltpu.HBM) for x in (vq, vk, vv, aq, ak, av)])
+    blocks = exchange(sends, moves, send_order(size))
     gains = [gain.reshape(columns // HEAD_DIM, HEAD_DIM) for gain in gains]
     tv, ta = rv * size, ra * size
     results = pl.pallas_call(
@@ -182,9 +207,7 @@
         ),
         name="attention",
     )(*blocks, *gains)
-    back = [results[0]] + [
-        lax.ppermute(results[step], "seq", [(b, a) for a, b in moves[step]]) for step in range(1, size)
-    ]
+    back = exchange(results, [[(b, a) for a, b in move] for move in moves], return_order(size))
     return tuple(
         pl.pallas_call(
             functools.partial(unpack_kernel, size, rv),

time: 59.2 us -> 50.3 us (0.85)
  local copies, waits for them, and re-layouts: 6.04 us -> 0.7 us
  starting transfers between devices: 27.6 us -> 24.4 us
  waiting for transfers between devices: 17.3 us -> 15.7 us
  Pallas kernels: 7.22 us -> 8.63 us
    unnamed x20 -> x8, local copies, waits for them, and re-layouts: 6.04 us -> 0.7 us
    ppermute x14, starting transfers between devices: 27.6 us -> 24.4 us  [exchange(): lax.ppermute(blocks[step], 'seq', moves[step])]
    ppermute x14, waiting for transfers between devices: 17.3 us -> 15.7 us  [exchange(): lax.ppermute(blocks[step], 'seq', moves[step])]
    pallas_call x1, Pallas kernels: 0.26 us -> 1.66 us  [head_plan(): pl.pallas_call(functools.partial(pack_kernel, size), out_shape=[jax.Shape...]
  transfers between devices with their start and end apart: 14 -> 14, of which waited for: 6 -> 7; matrix products, arithmetic and copies ran while one was open for 0% -> 0% of each run, Pallas kernels for 0% -> 0%
where the time goes in v2:
time: 50.3 us; the launch traced here: 50 us
  starting transfers between devices  24.4 us (49%)
  waiting for transfers between devices  15.7 us (31%)
  Pallas kernels  8.63 us (17%)
  local copies, waits for them, and re-layouts  0.7 us (1%)
  between operations  0.67 us (1%)
    ppermute x14, starting transfers between devices, exchange(): lax.ppermute(blocks[step], 'seq', moves[step])  24.4 us
    ppermute x14, waiting for transfers between devices, exchange(): lax.ppermute(blocks[step], 'seq', moves[step])  15.7 us
    pallas_call x1, Pallas kernels, head_plan(): pl.pallas_call(functools.partial(attention_kernel, size, rv, ra), out_sha...  6.16 us
    pallas_call x1, Pallas kernels, head_plan(): pl.pallas_call(functools.partial(pack_kernel, size), out_shape=[jax.Shape...  1.66 us
  transfers between devices with their start and end apart: 14, of which 7 were waited for; matrix products, arithmetic and copies ran while one was open for 0% of the time, Pallas kernels for 0%

profile of v2, /device:TPU:0, one launch (start us, length us, event | category | flops | bytes accessed | tf_op | source)
XLA Modules:
  0.0 50.0 jit_solution(3785091532825374069)
XLA Ops:
  0.6 1.7 %pack.1 = (bf16[480,128]{1,0:T(8,128)(2,1)S(1)}, bf16[480,128]{1,0:T(8,128)(2,1)S(1)}, bf16[480,128]{1,0:T(8,128)(2,1)S(1)}, bf16[480,128]{1,0:T(8,128)(2,1)S(1)...) custom-call(bf16[128,1024]{1,0:T(8,128)(2,1)} %refs_0_.1, ...), custom_call_target="tpu_custom_call" | custom-call | tf_op jit(solution)/shard_map/pack/pallas_call | solution.py:182
  2.3 3.0 %collective-permute-start = (bf16[480,128]{1,0:T(8,128)(2,1)S(1)}, bf16[480,128]{1,0:T(8,128)(2,1)S(1)}, u32[]{:S(2)}, u32[]{:S(2)}) collective-permute-start(bf16[480,128]{1,0:T(8,128)(2,1)S(1)} %get-tuple-element.19), channel_id=1, source_target_pairs={{0,2},{2,0},{4,6},{6,4},{8,10},{10,8},{12,14},{14,12},{1,3},{3,1},... | collective-permute-start | bytes 368648 | tf_op jit(solution)/shard_map/ppermute | solution.py:73
  5.3 1.6 %collective-permute-start.1 = (bf16[480,128]{1,0:T(8,128)(2,1)S(1)}, bf16[480,128]{1,0:T(8,128)(2,1)S(1)}, u32[]{:S(2)}, u32[]{:S(2)}) collective-permute-start(bf16[480,128]{1,0:T(8,128)(2,1)S(1)} %get-tuple-element.20), channel_id=1, source_target_pairs={{0,4},{2,6},{4,0},{6,2},{8,12},{10,14},{12,8},{14,10},{1,5},{3,7},... | collective-permute-start | bytes 368648 | tf_op jit(solution)/shard_map/ppermute | solution.py:73
  6.9 2.6 %collective-permute-start.2 = (bf16[480,128]{1,0:T(8,128)(2,1)S(1)}, bf16[480,128]{1,0:T(8,128)(2,1)S(1)}, u32[]{:S(2)}, u32[]{:S(2)}) collective-permute-start(bf16[480,128]{1,0:T(8,128)(2,1)S(1)} %get-tuple-element.21), channel_id=1, source_target_pairs={{0,8},{2,10},{4,12},{6,14},{8,0},{10,2},{12,4},{14,6},{1,9},{3,11}... | collective-permute-start | bytes 368648 | tf_op jit(solution)/shard_map/ppermute | solution.py:73
  9.5 0.3 collective-permute-start.3
  9.8 2.5 %collective-permute-start.4 = (bf16[480,128]{1,0:T(8,128)(2,1)S(1)}, bf16[480,128]{1,0:T(8,128)(2,1)S(1)}, u32[]{:S(2)}, u32[]{:S(2)}) collective-permute-start(bf16[480,128]{1,0:T(8,128)(2,1)S(1)} %get-tuple-element.23), channel_id=1, source_target_pairs={{0,12},{2,14},{4,8},{6,10},{8,4},{10,6},{12,0},{14,2},{1,13},{3,15... | collective-permute-start | bytes 368648 | tf_op jit(solution)/shard_map/ppermute | solution.py:73
  12.3 2.3 %collective-permute-start.5 = (bf16[480,128]{1,0:T(8,128)(2,1)S(1)}, bf16[480,128]{1,0:T(8,128)(2,1)S(1)}, u32[]{:S(2)}, u32[]{:S(2)}) collective-permute-start(bf16[480,128]{1,0:T(8,128)(2,1)S(1)} %get-tuple-element.24), channel_id=1, source_target_pairs={{0,14},{2,12},{4,10},{6,8},{8,6},{10,4},{12,2},{14,0},{1,15},{3,13... | collective-permute-start | bytes 368648 | tf_op jit(solution)/shard_map/ppermute | solution.py:73
  14.6 9.3 %collective-permute-done.2.refs_3_ = bf16[480,128]{1,0:T(8,128)(2,1)S(1)} collective-permute-done((bf16[480,128]{1,0:T(8,128)(2,1)S(1)}, bf16[480,128]{1,0:T(8,128)(2,1)S(1)}, u32[]{:S(2)}, u32[]{:S(2)}) %collective-permute-start.2) | collective-permute-done | bytes 122912 | tf_op jit(solution)/shard_map/ppermute | solution.py:73
  23.9 2.1 %collective-permute-done.3.refs_4_ = bf16[480,128]{1,0:T(8,128)(2,1)S(1)} collective-permute-done((bf16[480,128]{1,0:T(8,128)(2,1)S(1)}, bf16[480,128]{1,0:T(8,128)(2,1)S(1)}, u32[]{:S(2)}, u32[]{:S(2)}) %collective-permute-start.3) | collective-permute-done | bytes 122912 | tf_op jit(solution)/shard_map/ppermute | solution.py:73
  26.0 0.8 %collective-permute-done.6.refs_7_ = bf16[480,128]{1,0:T(8,128)(2,1)S(1)} collective-permute-done((bf16[480,128]{1,0:T(8,128)(2,1)S(1)}, bf16[480,128]{1,0:T(8,128)(2,1)S(1)}, u32[]{:S(2)}, u32[]{:S(2)}) %collective-permute-start.6) | collective-permute-done | bytes 122912 | tf_op jit(solution)/shard_map/ppermute | solution.py:73
  26.8 0.7 %copy-done.1 = f32[1024]{0:T(1024)S(1)} copy-done((f32[1024]{0:T(1024)S(1)}, f32[1024]{0:T(1024)}, u32[]{:S(2)}) %copy-start.1) | copy-done | bytes 4120
  27.5 6.2 %attention.1 = (bf16[160,128]{1,0:T(8,128)(2,1)S(1)}, bf16[160,128]{1,0:T(8,128)(2,1)S(1)}, bf16[160,128]{1,0:T(8,128)(2,1)S(1)}, bf16[160,128]{1,0:T(8,128)(2,1...) custom-call(bf16[480,128]{1,0:T(8,128)(2,1)S(1)} %get-tuple-element., ...), custom_call_target="tpu_custom_call" | custom-call | flops 838860800 | bytes 1048576 | tf_op jit(solution)/shard_map/attention/pallas_call | solution.py:194
  33.7 3.6 %collective-permute-start.7 = (bf16[160,128]{1,0:T(8,128)(2,1)S(1)}, bf16[160,128]{1,0:T(8,128)(2,1)S(1)}, u32[]{:S(2)}, u32[]{:S(2)}) collective-permute-start(bf16[160,128]{1,0:T(8,128)(2,1)S(1)} %get-tuple-element.27), channel_id=1, source_target_pairs={{14,0},{12,2},{10,4},{8,6},{6,8},{4,10},{2,12},{0,14},{15,1},{13,3... | collective-permute-start | bytes 122888 | tf_op jit(solution)/shard_map/ppermute | solution.py:73
  37.3 1.0 %collective-permute-start.8 = (bf16[160,128]{1,0:T(8,128)(2,1)S(1)}, bf16[160,128]{1,0:T(8,128)(2,1)S(1)}, u32[]{:S(2)}, u32[]{:S(2)}) collective-permute-start(bf16[160,128]{1,0:T(8,128)(2,1)S(1)} %get-tuple-element.28), channel_id=1, source_target_pairs={{12,0},{14,2},{8,4},{10,6},{4,8},{6,10},{0,12},{2,14},{13,1},{15,3... | collective-permute-start | bytes 122888 | tf_op jit(solution)/shard_map/ppermute | solution.py:73
  38.3 3.9 %collective-permute-start.9 = (bf16[160,128]{1,0:T(8,128)(2,1)S(1)}, bf16[160,128]{1,0:T(8,128)(2,1)S(1)}, u32[]{:S(2)}, u32[]{:S(2)}) collective-permute-start(bf16[160,128]{1,0:T(8,128)(2,1)S(1)} %get-tuple-element.29), channel_id=1, source_target_pairs={{10,0},{8,2},{14,4},{12,6},{2,8},{0,10},{6,12},{4,14},{11,1},{9,3}... | collective-permute-start | bytes 122888 | tf_op jit(solution)/shard_map/ppermute | solution.py:73
  42.2 0.1 collective-permute-start.10
  42.3 2.8 %collective-permute-start.11 = (bf16[160,128]{1,0:T(8,128)(2,1)S(1)}, bf16[160,128]{1,0:T(8,128)(2,1)S(1)}, u32[]{:S(2)}, u32[]{:S(2)}) collective-permute-start(bf16[160,128]{1,0:T(8,128)(2,1)S(1)} %get-tuple-element.31), channel_id=1, source_target_pairs={{6,0},{4,2},{2,4},{0,6},{14,8},{12,10},{10,12},{8,14},{7,1},{5,3},... | collective-permute-start | bytes 122888 | tf_op jit(solution)/shard_map/ppermute | solution.py:73
  45.1 0.1 collective-permute-start.12
  45.2 0.6 %collective-permute-start.13 = (bf16[160,128]{1,0:T(8,128)(2,1)S(1)}, bf16[160,128]{1,0:T(8,128)(2,1)S(1)}, u32[]{:S(2)}, u32[]{:S(2)}) collective-permute-start(bf16[160,128]{1,0:T(8,128)(2,1)S(1)} %get-tuple-element.33), channel_id=1, source_target_pairs={{2,0},{0,2},{6,4},{4,6},{10,8},{8,10},{14,12},{12,14},{3,1},{1,3},... | collective-permute-start | bytes 122888 | tf_op jit(solution)/shard_map/ppermute | solution.py:73
  45.8 0.1 collective-permute-done.9.refs_3_
  45.8 1.4 %collective-permute-done.10.refs_4_ = bf16[160,128]{1,0:T(8,128)(2,1)S(1)} collective-permute-done((bf16[160,128]{1,0:T(8,128)(2,1)S(1)}, bf16[160,128]{1,0:T(8,128)(2,1)S(1)}, u32[]{:S(2)}, u32[]{:S(2)}) %collective-permute-start.10) | collective-permute-done | bytes 40992 | tf_op jit(solution)/shard_map/ppermute | solution.py:73
  47.3 1.8 %collective-permute-done.12.refs_6_ = bf16[160,128]{1,0:T(8,128)(2,1)S(1)} collective-permute-done((bf16[160,128]{1,0:T(8,128)(2,1)S(1)}, bf16[160,128]{1,0:T(8,128)(2,1)S(1)}, u32[]{:S(2)}, u32[]{:S(2)}) %collective-permute-start.12) | collective-permute-done | bytes 40992 | tf_op jit(solution)/shard_map/ppermute | solution.py:73
  49.1 0.1 collective-permute-done.13.refs_7_
  49.2 0.8 %unpack.1 = (bf16[128,1024]{1,0:T(8,128)(2,1)}, bf16[32,1024]{1,0:T(8,128)(2,1)}) custom-call(bf16[160,128]{1,0:T(8,128)(2,1)S(1)} %get-tuple-element.26.refs_0_, bf16[160,128]{1,0:T(8,128)(2,1)S(1)} %collective-permute-done.7.refs_1_, bf16[160,128]{1,0:T(8,128)(2,1)S(1)} %collective-permute-done.8.refs_2_, ...), custom_call_target="tpu_custom_call" | custom-call | tf_op jit(solution)/shard_map/unpack/pallas_call | solution.py:212
  (15 shorter events, 0.0 us)
Async XLA Ops:
  2.3 10.0 %collective-permute-start = (bf16[480,128]{1,0:T(8,128)(2,1)S(1)}, bf16[480,128]{1,0:T(8,128)(2,1)S(1)}, u32[]{:S(2)}, u32[]{:S(2)}) collective-permute-start(bf16[480,128]{1,0:T(8,128)(2,1)S(1)} %get-tuple-element.19), channel_id=1, source_target_pairs={{0,2},{2,0},{4,6},{6,4},{8,10},{10,8},{12,14},{14,12},{1,3},{3,1},... | collective-permute-start | bytes 368648 | tf_op jit(solution)/shard_map/ppermute | solution.py:73
  5.3 21.5 %copy-start.2 = (f32[1024]{0:T(1024)S(1)}, f32[1024]{0:T(1024)}, u32[]{:S(2)}) copy-start(f32[1024]{0:T(1024)} %param.18) | copy-start | bytes 12292
  5.3 21.5 %copy-start.3 = (f32[1024]{0:T(1024)S(1)}, f32[1024]{0:T(1024)}, u32[]{:S(2)}) copy-start(f32[1024]{0:T(1024)} %param.19) | copy-start | bytes 12292
  5.3 9.2 %collective-permute-start.1 = (bf16[480,128]{1,0:T(8,128)(2,1)S(1)}, bf16[480,128]{1,0:T(8,128)(2,1)S(1)}, u32[]{:S(2)}, u32[]{:S(2)}) collective-permute-start(bf16[480,128]{1,0:T(8,128)(2,1)S(1)} %get-tuple-element.20), channel_id=1, source_target_pairs={{0,4},{2,6},{4,0},{6,2},{8,12},{10,14},{12,8},{14,10},{1,5},{3,7},... | collective-permute-start | bytes 368648 | tf_op jit(solution)/shard_map/ppermute | solution.py:73
  6.9 17.0 %collective-permute-start.2 = (bf16[480,128]{1,0:T(8,128)(2,1)S(1)}, bf16[480,128]{1,0:T(8,128)(2,1)S(1)}, u32[]{:S(2)}, u32[]{:S(2)}) collective-permute-start(bf16[480,128]{1,0:T(8,128)(2,1)S(1)} %get-tuple-element.21), channel_id=1, source_target_pairs={{0,8},{2,10},{4,12},{6,14},{8,0},{10,2},{12,4},{14,6},{1,9},{3,11}... | collective-permute-start | bytes 368648 | tf_op jit(solution)/shard_map/ppermute | solution.py:73
  9.5 16.5 %collective-permute-start.3 = (bf16[480,128]{1,0:T(8,128)(2,1)S(1)}, bf16[480,128]{1,0:T(8,128)(2,1)S(1)}, u32[]{:S(2)}, u32[]{:S(2)}) collective-permute-start(bf16[480,128]{1,0:T(8,128)(2,1)S(1)} %get-tuple-element.22), channel_id=1, source_target_pairs={{0,10},{2,8},{4,14},{6,12},{8,2},{10,0},{12,6},{14,4},{1,11},{3,9}... | collective-permute-start | bytes 368648 | tf_op jit(solution)/shard_map/ppermute | solution.py:73
  9.8 16.2 %collective-permute-start.4 = (bf16[480,128]{1,0:T(8,128)(2,1)S(1)}, bf16[480,128]{1,0:T(8,128)(2,1)S(1)}, u32[]{:S(2)}, u32[]{:S(2)}) collective-permute-start(bf16[480,128]{1,0:T(8,128)(2,1)S(1)} %get-tuple-element.23), channel_id=1, source_target_pairs={{0,12},{2,14},{4,8},{6,10},{8,4},{10,6},{12,0},{14,2},{1,13},{3,15... | collective-permute-start | bytes 368648 | tf_op jit(solution)/shard_map/ppermute | solution.py:73
  12.3 13.7 %collective-permute-start.5 = (bf16[480,128]{1,0:T(8,128)(2,1)S(1)}, bf16[480,128]{1,0:T(8,128)(2,1)S(1)}, u32[]{:S(2)}, u32[]{:S(2)}) collective-permute-start(bf16[480,128]{1,0:T(8,128)(2,1)S(1)} %get-tuple-element.24), channel_id=1, source_target_pairs={{0,14},{2,12},{4,10},{6,8},{8,6},{10,4},{12,2},{14,0},{1,15},{3,13... | collective-permute-start | bytes 368648 | tf_op jit(solution)/shard_map/ppermute | solution.py:73
  14.6 12.2 %collective-permute-start.6 = (bf16[480,128]{1,0:T(8,128)(2,1)S(1)}, bf16[480,128]{1,0:T(8,128)(2,1)S(1)}, u32[]{:S(2)}, u32[]{:S(2)}) collective-permute-start(bf16[480,128]{1,0:T(8,128)(2,1)S(1)} %get-tuple-element.25), channel_id=1, source_target_pairs={{0,6},{2,4},{4,2},{6,0},{8,14},{10,12},{12,10},{14,8},{1,7},{3,5},... | collective-permute-start | bytes 368648 | tf_op jit(solution)/shard_map/ppermute | solution.py:73
  26.8 0.7 %copy-start.1 = (f32[1024]{0:T(1024)S(1)}, f32[1024]{0:T(1024)}, u32[]{:S(2)}) copy-start(f32[1024]{0:T(1024)} %param.17) | copy-start | bytes 12292
  26.8 0.7 %copy-start = (f32[1024]{0:T(1024)S(1)}, f32[1024]{0:T(1024)}, u32[]{:S(2)}) copy-start(f32[1024]{0:T(1024)} %param.16) | copy-start | bytes 12292
  33.7 11.4 %collective-permute-start.7 = (bf16[160,128]{1,0:T(8,128)(2,1)S(1)}, bf16[160,128]{1,0:T(8,128)(2,1)S(1)}, u32[]{:S(2)}, u32[]{:S(2)}) collective-permute-start(bf16[160,128]{1,0:T(8,128)(2,1)S(1)} %get-tuple-element.27), channel_id=1, source_target_pairs={{14,0},{12,2},{10,4},{8,6},{6,8},{4,10},{2,12},{0,14},{15,1},{13,3... | collective-permute-start | bytes 122888 | tf_op jit(solution)/shard_map/ppermute | solution.py:73
  37.3 7.9 %collective-permute-start.8 = (bf16[160,128]{1,0:T(8,128)(2,1)S(1)}, bf16[160,128]{1,0:T(8,128)(2,1)S(1)}, u32[]{:S(2)}, u32[]{:S(2)}) collective-permute-start(bf16[160,128]{1,0:T(8,128)(2,1)S(1)} %get-tuple-element.28), channel_id=1, source_target_pairs={{12,0},{14,2},{8,4},{10,6},{4,8},{6,10},{0,12},{2,14},{13,1},{15,3... | collective-permute-start | bytes 122888 | tf_op jit(solution)/shard_map/ppermute | solution.py:73
  38.3 7.5 %collective-permute-start.9 = (bf16[160,128]{1,0:T(8,128)(2,1)S(1)}, bf16[160,128]{1,0:T(8,128)(2,1)S(1)}, u32[]{:S(2)}, u32[]{:S(2)}) collective-permute-start(bf16[160,128]{1,0:T(8,128)(2,1)S(1)} %get-tuple-element.29), channel_id=1, source_target_pairs={{10,0},{8,2},{14,4},{12,6},{2,8},{0,10},{6,12},{4,14},{11,1},{9,3}... | collective-permute-start | bytes 122888 | tf_op jit(solution)/shard_map/ppermute | solution.py:73
  42.2 5.1 %collective-permute-start.10 = (bf16[160,128]{1,0:T(8,128)(2,1)S(1)}, bf16[160,128]{1,0:T(8,128)(2,1)S(1)}, u32[]{:S(2)}, u32[]{:S(2)}) collective-permute-start(bf16[160,128]{1,0:T(8,128)(2,1)S(1)} %get-tuple-element.30), channel_id=1, source_target_pairs={{8,0},{10,2},{12,4},{14,6},{0,8},{2,10},{4,12},{6,14},{9,1},{11,3}... | collective-permute-start | bytes 122888 | tf_op jit(solution)/shard_map/ppermute | solution.py:73
  42.3 5.0 %collective-permute-start.11 = (bf16[160,128]{1,0:T(8,128)(2,1)S(1)}, bf16[160,128]{1,0:T(8,128)(2,1)S(1)}, u32[]{:S(2)}, u32[]{:S(2)}) collective-permute-start(bf16[160,128]{1,0:T(8,128)(2,1)S(1)} %get-tuple-element.31), channel_id=1, source_target_pairs={{6,0},{4,2},{2,4},{0,6},{14,8},{12,10},{10,12},{8,14},{7,1},{5,3},... | collective-permute-start | bytes 122888 | tf_op jit(solution)/shard_map/ppermute | solution.py:73
  45.1 4.0 %collective-permute-start.12 = (bf16[160,128]{1,0:T(8,128)(2,1)S(1)}, bf16[160,128]{1,0:T(8,128)(2,1)S(1)}, u32[]{:S(2)}, u32[]{:S(2)}) collective-permute-start(bf16[160,128]{1,0:T(8,128)(2,1)S(1)} %get-tuple-element.32), channel_id=1, source_target_pairs={{4,0},{6,2},{0,4},{2,6},{12,8},{14,10},{8,12},{10,14},{5,1},{7,3},... | collective-permute-start | bytes 122888 | tf_op jit(solution)/shard_map/ppermute | solution.py:73
  45.2 4.0 %collective-permute-start.13 = (bf16[160,128]{1,0:T(8,128)(2,1)S(1)}, bf16[160,128]{1,0:T(8,128)(2,1)S(1)}, u32[]{:S(2)}, u32[]{:S(2)}) collective-permute-start(bf16[160,128]{1,0:T(8,128)(2,1)S(1)} %get-tuple-element.33), channel_id=1, source_target_pairs={{2,0},{0,2},{6,4},{4,6},{10,8},{8,10},{14,12},{12,14},{3,1},{1,3},... | collective-permute-start | bytes 122888 | tf_op jit(solution)/shard_map/ppermute | solution.py:73

commit v3 on v2

v3 whole, which is shorter than its diff:
```python
import functools
import math

import jax
import jax.numpy as jnp
from jax import lax
from jax.experimental import pallas as pl
from jax.experimental.pallas import tpu as pltpu
from jax.sharding import PartitionSpec as P

HEAD_DIM = 128
SCALE = HEAD_DIM ** (-0.5)
SCALE_LOG2 = SCALE * math.log2(math.e)
VMEM_LIMIT = 48 * 1024 * 1024
PACK_VMEM = 16 * 1024 * 1024


def normed(tokens, gain_row):
    count = tokens.shape[0]
    head_count = tokens.shape[1] // HEAD_DIM
    entries = tokens.astype(jnp.float32).reshape(count, head_count, HEAD_DIM)
    scaled = entries * lax.rsqrt(jnp.mean(entries * entries, axis=2, keepdims=True) + 1e-06)
    return (scaled.reshape(count, head_count * HEAD_DIM) * gain_row).astype(jnp.bfloat16)


def as_heads(tokens):
    return tokens.reshape(tokens.shape[0], tokens.shape[1] // HEAD_DIM, HEAD_DIM)


def attend(queries, key_rows, values):
    queries, key_rows, values = as_heads(queries), as_heads(key_rows), as_heads(values)
    scores = SCALE * jnp.einsum("qhd,khd->hqk", queries, key_rows, preferred_element_type=jnp.float32)
    weights = jnp.exp(scores - jnp.max(scores, axis=2, keepdims=True))
    total = jnp.sum(weights, axis=2)
    result = jnp.einsum("hqk,khd->qhd", weights.astype(jnp.bfloat16), values, preferred_element_type=jnp.float32)
    result = result / total.T[:, :, None]
    return result.reshape(result.shape[0], result.shape[1] * HEAD_DIM)


def gather_plan(vq, vk, vv, aq, ak, av, vq_gain, vk_gain, aq_gain, ak_gain):
    whole = functools.partial(lax.all_gather, axis_name="seq", axis=0, tiled=True)
    video_self = attend(vq, whole(vk), whole(vv)).astype(jnp.bfloat16)
    audio_self = attend(aq, whole(ak), whole(av)).astype(jnp.bfloat16)
    video_all, audio_all = whole(video_self), whole(audio_self)
    video_cross = attend(normed(video_self, vq_gain), normed(audio_all, ak_gain), audio_all)
    audio_cross = attend(normed(audio_self, aq_gain), normed(video_all, vk_gain), video_all)
    return (
        (video_self.astype(jnp.float32) + video_cross).astype(jnp.bfloat16),
        (audio_self.astype(jnp.float32) + audio_cross).astype(jnp.bfloat16),
    )


def partners(size):
    if size & (size - 1) == 0:
        return [[(a, a ^ step) for a in range(size)] for step in range(size)]
    return [[(a, (a + step) % size) for a in range(size)] for step in range(size)]


def partner_of(me, step, size):
    return me ^ step if size & (size - 1) == 0 else lax.rem(me + step, size)


def send_order(size):
    middle = size // 2

    def rank(step):
        return (step != middle, step & (step - 1) and 1 + (step < middle), step)

    return sorted(range(1, size), key=rank)


def exchange(blocks, moves, steps):
    return {step: lax.ppermute(blocks[step], "seq", moves[step]) for step in steps}


def pack_kernel(size, steps, *refs):
    ins, outs, sem = refs[:6], refs[-1 - len(steps) : -1], refs[-1]
    me = lax.axis_index("seq")
    width = ins[0].shape[1] // size
    copies = []
    for step, out in zip(steps, outs):
        column = pl.multiple_of(partner_of(me, step, size) * width, HEAD_DIM)
        row = 0
        for ref in ins:
            rows = ref.shape[0]
            copies.append(
                pltpu.make_async_copy(
                    ref.at[:, pl.ds(column, width)], out.at[pl.ds(row, rows), :], sem.at[len(copies)]
                )
            )
            row += rows
    for copy in copies:
        copy.start()
    for copy in copies:
        copy.wait()


def unpack_kernel(size, rows, steps, *refs):
    blocks, (video_out, audio_out) = refs[:-2], refs[-2:]
    me = lax.axis_index("seq")
    width = video_out.shape[1] // size
    for step, block in zip(steps, blocks):
        column = pl.multiple_of(partner_of(me, step, size) * width, HEAD_DIM)
        video_out[:, pl.ds(column, width)] = block[pl.ds(0, rows), :]
        audio_out[:, pl.ds(column, width)] = block[pl.ds(rows, block.shape[0] - rows), :]


def dot_t(left, right):
    return lax.dot_general(left, right, (((1,), (1,)), ((), ())), preferred_element_type=jnp.float32)


def weighed(weights, values_and_ones):
    product = jnp.dot(weights.astype(jnp.bfloat16), values_and_ones, preferred_element_type=jnp.float32)
    return product[:, :HEAD_DIM] * (1.0 / product[:, HEAD_DIM:])


def self_attend(queries, key_rows, values_and_ones):
    scores = dot_t(queries, key_rows)
    top = jnp.max(scores, axis=1, keepdims=True)
    return weighed(jnp.exp2((scores - top) * SCALE_LOG2), values_and_ones)


def cross_attend(queries, key_rows, values_and_ones):
    return weighed(jnp.exp2(dot_t(queries, key_rows) * SCALE_LOG2), values_and_ones)


def unit_rows(tokens):
    entries = tokens.astype(jnp.float32)
    return entries * lax.rsqrt(jnp.mean(entries * entries, axis=1, keepdims=True) + 1e-06)


def attention_kernel(size, video_rows, audio_rows, *refs):
    blocks = refs[:size]
    gain_refs = refs[size : size + 4]
    outs = refs[size + 4 : 2 * size + 4]
    vq, vk, vv, aq, ak, av, v_self, a_self, gains, sem = refs[2 * size + 4 :]
    me = lax.axis_index("seq")
    heads = blocks[0].shape[1] // HEAD_DIM
    rv, ra = video_rows, audio_rows
    copies = [
        pltpu.make_async_copy(ref, gains.at[at], sem.at[at]) for at, ref in enumerate(gain_refs)
    ]
    for copy in copies:
        copy.start()
    for values in (vv, av, v_self, a_self):
        values[:, HEAD_DIM:] = jnp.ones((values.shape[0], HEAD_DIM), jnp.bfloat16)
    for head in range(heads):
        cols = pl.ds(head * HEAD_DIM, HEAD_DIM)
        for at, block in enumerate(blocks):
            row = 0
            for whole, rows in ((vq, rv), (vk, rv), (vv, rv), (aq, ra), (ak, ra), (av, ra)):
                whole[pl.ds(at * rows, rows), :HEAD_DIM] = block[pl.ds(row, rows), cols]
                row += rows
        a_result = self_attend(aq[...], ak[...], av[...]).astype(jnp.bfloat16)
        v_result = self_attend(vq[...], vk[...], vv[...]).astype(jnp.bfloat16)
        a_self[:, :HEAD_DIM] = a_result
        v_self[:, :HEAD_DIM] = v_result
        if head == 0:
            for copy in copies:
                copy.wait()
        vq_gain, vk_gain, aq_gain, ak_gain = [gains[at, pl.ds(me * heads + head, 1), :] for at in range(4)]
        a_unit, v_unit = unit_rows(a_result), unit_rows(v_result)
        a_query, a_key = (a_unit * aq_gain).astype(jnp.bfloat16), (a_unit * ak_gain).astype(jnp.bfloat16)
        v_query, v_key = (v_unit * vq_gain).astype(jnp.bfloat16), (v_unit * vk_gain).astype(jnp.bfloat16)
        v_mixed = v_result.astype(jnp.float32) + cross_attend(v_query, a_key, a_self[...])
        a_mixed = a_result.astype(jnp.float32) + cross_attend(a_query, v_key, v_self[...])
        v_mixed, a_mixed = v_mixed.astype(jnp.bfloat16), a_mixed.astype(jnp.bfloat16)
        for at, out in enumerate(outs):
            out[pl.ds(0, rv), cols] = v_mixed[at * rv : (at + 1) * rv, :]
            out[pl.ds(rv, ra), cols] = a_mixed[at * ra : (at + 1) * ra, :]


def head_plan(size, vq, vk, vv, aq, ak, av, *gains):
    rv, columns = vq.shape
    ra = aq.shape[0]
    width = columns // size
    in_vmem = pl.BlockSpec(memory_space=pltpu.VMEM)
    in_hbm = pl.BlockSpec(memory_space=pltpu.HBM)
    moves = partners(size)

    arrays = [pltpu.with_memory_space_constraint(x, pltpu.HBM) for x in (vq, vk, vv, aq, ak, av)]
    order = [0, *send_order(size)]
    sends = pl.pallas_call(
        functools.partial(pack_kernel, size, order),
        out_shape=[jax.ShapeDtypeStruct((3 * (rv + ra), width), vq.dtype)] * size,
        in_specs=[in_hbm] * 6,
        out_specs=[in_vmem] * size,
        scratch_shapes=[pltpu.SemaphoreType.DMA((6 * size,))],
        compiler_params=pltpu.CompilerParams(vmem_limit_bytes=PACK_VMEM),
        name="pack",
    )(*arrays)
    sends = dict(zip(order, sends))
    blocks = {0: sends[0], **exchange(sends, moves, order[1:])}

    gains = [
        pltpu.with_memory_space_constraint(gain.reshape(columns // HEAD_DIM, HEAD_DIM), pltpu.HBM)
        for gain in gains
    ]
    tv, ta = rv * size, ra * size
    results = pl.pallas_call(
        functools.partial(attention_kernel, size, rv, ra),
        out_shape=[jax.ShapeDtypeStruct((rv + ra, width), vq.dtype)] * size,
        in_specs=[in_vmem] * size + [in_hbm] * 4,
        out_specs=[in_vmem] * size,
        scratch_shapes=[
            pltpu.VMEM((rows, parts * HEAD_DIM), jnp.bfloat16)
            for rows, parts in ((tv, 1), (tv, 1), (tv, 2), (ta, 1), (ta, 1), (ta, 2), (tv, 2), (ta, 2))
        ]
        + [pltpu.VMEM((4, columns // HEAD_DIM, HEAD_DIM), jnp.float32), pltpu.SemaphoreType.DMA((4,))],
        compiler_params=pltpu.CompilerParams(vmem_limit_bytes=VMEM_LIMIT),
        cost_estimate=pl.CostEstimate(
            flops=4 * width * (tv * tv + ta * ta + 2 * tv * ta),
            bytes_accessed=8 * tv * width,
            transcendentals=(width // HEAD_DIM) * (tv * tv + ta * ta + 2 * tv * ta),
        ),
        name="attention",
    )(*[blocks[step] for step in order], *gains)
    results = dict(zip(order, results))
    inverse = [[(b, a) for a, b in move] for move in moves]
    farthest_first = range(size - 1, 0, -1)
    back = [results[0], *exchange(results, inverse, farthest_first).values()]
    return tuple(
        pl.pallas_call(
            functools.partial(unpack_kernel, size, rv, (0, *farthest_first)),
            out_shape=[
                jax.ShapeDtypeStruct((rv, columns), vq.dtype),
                jax.ShapeDtypeStruct((ra, columns), vq.dtype),
            ],
            in_specs=[in_vmem] * size,
            out_specs=[in_vmem] * 2,
            compiler_params=pltpu.CompilerParams(vmem_limit_bytes=PACK_VMEM),
            name="unpack",
        )(*back)
    )


def solution(mesh):
    size = mesh.shape["seq"]

    def per_device(*args):
        heads = args[0].shape[1] // HEAD_DIM
        if heads % size == 0:
            return head_plan(size, *args)
        return gather_plan(*args)

    tokens = P(("clips", "seq"), "head")
    return jax.shard_map(
        per_device,
        mesh=mesh,
        in_specs=(tokens,) * 6 + (P("head"),) * 4,
        out_specs=(tokens, tokens),
        check_vma=False,
    )
```

time: 50.3 us -> 46.3 us (0.920)
  waiting for transfers between devices: 15.7 us -> 9.02 us
  starting transfers between devices: 24.4 us -> 30.4 us
  Pallas kernels: 8.63 us -> 6.02 us
  local copies, waits for them, and re-layouts: 0.7 us -> 0 us
    ppermute x14, waiting for transfers between devices: 15.7 us -> 9.02 us  [exchange(): lax.ppermute(blocks[step], 'seq', moves[step])]
    ppermute x14, starting transfers between devices: 24.4 us -> 30.4 us  [exchange(): lax.ppermute(blocks[step], 'seq', moves[step])]
    pallas_call x1, Pallas kernels: 6.16 us -> 3.55 us  [head_plan(): pl.pallas_call(functools.partial(attention_kernel, size, rv, ra), out_sha...]
    unnamed x8 -> x0, local copies, waits for them, and re-layouts: 0.7 us -> none
where the time goes in v3:
time: 46.3 us; the launch traced here: 46.1 us
  starting transfers between devices  30.4 us (66%)
  waiting for transfers between devices  9.02 us (19%)
  Pallas kernels  6.02 us (13%)
  between operations  0.66 us (1%)
    ppermute x14, starting transfers between devices, exchange(): lax.ppermute(blocks[step], 'seq', moves[step])  30.4 us
    ppermute x14, waiting for transfers between devices, exchange(): lax.ppermute(blocks[step], 'seq', moves[step])  9.02 us
    pallas_call x1, Pallas kernels, head_plan(): pl.pallas_call(functools.partial(attention_kernel, size, rv, ra), out_sha...  3.55 us
    pallas_call x1, Pallas kernels, head_plan(): pl.pallas_call(functools.partial(pack_kernel, size, order), out_shape=[ja...  1.66 us
  transfers between devices with their start and end apart: 14, of which 7 were waited for; matrix products, arithmetic and copies ran while one was open for 0% of the time, Pallas kernels for 0%

profile of v3, /device:TPU:0, one launch (start us, length us, event | category | flops | bytes accessed | tf_op | source)
XLA Modules:
  0.0 46.1 jit_solution(5653079545865471515)
XLA Ops:
  0.6 1.7 %pack.1 = (bf16[480,128]{1,0:T(8,128)(2,1)S(1)}, bf16[480,128]{1,0:T(8,128)(2,1)S(1)}, bf16[480,128]{1,0:T(8,128)(2,1)S(1)}, bf16[480,128]{1,0:T(8,128)(2,1)S(1)...) custom-call(bf16[128,1024]{1,0:T(8,128)(2,1)} %refs_0_.1, ...), custom_call_target="tpu_custom_call" | custom-call | tf_op jit(solution)/shard_map/pack/pallas_call | solution.py:183
  2.3 4.1 %collective-permute-start = (bf16[480,128]{1,0:T(8,128)(2,1)S(1)}, bf16[480,128]{1,0:T(8,128)(2,1)S(1)}, u32[]{:S(2)}, u32[]{:S(2)}) collective-permute-start(bf16[480,128]{1,0:T(8,128)(2,1)S(1)} %get-tuple-element.19), channel_id=1, source_target_pairs={{0,8},{2,10},{4,12},{6,14},{8,0},{10,2},{12,4},{14,6},{1,9},{3,11}... | collective-permute-start | bytes 368648 | tf_op jit(solution)/shard_map/ppermute | solution.py:73
  6.4 1.5 %collective-permute-start.1 = (bf16[480,128]{1,0:T(8,128)(2,1)S(1)}, bf16[480,128]{1,0:T(8,128)(2,1)S(1)}, u32[]{:S(2)}, u32[]{:S(2)}) collective-permute-start(bf16[480,128]{1,0:T(8,128)(2,1)S(1)} %get-tuple-element.20), channel_id=1, source_target_pairs={{0,2},{2,0},{4,6},{6,4},{8,10},{10,8},{12,14},{14,12},{1,3},{3,1},... | collective-permute-start | bytes 368648 | tf_op jit(solution)/shard_map/ppermute | solution.py:73
  7.9 1.6 %collective-permute-start.2 = (bf16[480,128]{1,0:T(8,128)(2,1)S(1)}, bf16[480,128]{1,0:T(8,128)(2,1)S(1)}, u32[]{:S(2)}, u32[]{:S(2)}) collective-permute-start(bf16[480,128]{1,0:T(8,128)(2,1)S(1)} %get-tuple-element.21), channel_id=1, source_target_pairs={{0,4},{2,6},{4,0},{6,2},{8,12},{10,14},{12,8},{14,10},{1,5},{3,7},... | collective-permute-start | bytes 368648 | tf_op jit(solution)/shard_map/ppermute | solution.py:73
  9.5 0.3 collective-permute-start.3
  9.8 2.5 %collective-permute-start.4 = (bf16[480,128]{1,0:T(8,128)(2,1)S(1)}, bf16[480,128]{1,0:T(8,128)(2,1)S(1)}, u32[]{:S(2)}, u32[]{:S(2)}) collective-permute-start(bf16[480,128]{1,0:T(8,128)(2,1)S(1)} %get-tuple-element.23), channel_id=1, source_target_pairs={{0,12},{2,14},{4,8},{6,10},{8,4},{10,6},{12,0},{14,2},{1,13},{3,15... | collective-permute-start | bytes 368648 | tf_op jit(solution)/shard_map/ppermute | solution.py:73
  12.2 0.8 %collective-permute-done.refs_1_ = bf16[480,128]{1,0:T(8,128)(2,1)S(1)} collective-permute-done((bf16[480,128]{1,0:T(8,128)(2,1)S(1)}, bf16[480,128]{1,0:T(8,128)(2,1)S(1)}, u32[]{:S(2)}, u32[]{:S(2)}) %collective-permute-start) | collective-permute-done | bytes 122912 | tf_op jit(solution)/shard_map/ppermute | solution.py:73
  13.1 9.2 %collective-permute-start.5 = (bf16[480,128]{1,0:T(8,128)(2,1)S(1)}, bf16[480,128]{1,0:T(8,128)(2,1)S(1)}, u32[]{:S(2)}, u32[]{:S(2)}) collective-permute-start(bf16[480,128]{1,0:T(8,128)(2,1)S(1)} %get-tuple-element.24), channel_id=1, source_target_pairs={{0,14},{2,12},{4,10},{6,8},{8,6},{10,4},{12,2},{14,0},{1,15},{3,13... | collective-permute-start | bytes 368648 | tf_op jit(solution)/shard_map/ppermute | solution.py:73
  22.3 1.0 %collective-permute-done.3.refs_4_ = bf16[480,128]{1,0:T(8,128)(2,1)S(1)} collective-permute-done((bf16[480,128]{1,0:T(8,128)(2,1)S(1)}, bf16[480,128]{1,0:T(8,128)(2,1)S(1)}, u32[]{:S(2)}, u32[]{:S(2)}) %collective-permute-start.3) | collective-permute-done | bytes 122912 | tf_op jit(solution)/shard_map/ppermute | solution.py:73
  23.4 1.9 %collective-permute-done.5.refs_6_ = bf16[480,128]{1,0:T(8,128)(2,1)S(1)} collective-permute-done((bf16[480,128]{1,0:T(8,128)(2,1)S(1)}, bf16[480,128]{1,0:T(8,128)(2,1)S(1)}, u32[]{:S(2)}, u32[]{:S(2)}) %collective-permute-start.5) | collective-permute-done | bytes 122912 | tf_op jit(solution)/shard_map/ppermute | solution.py:73
  25.3 2.8 %collective-permute-done.6.refs_7_ = bf16[480,128]{1,0:T(8,128)(2,1)S(1)} collective-permute-done((bf16[480,128]{1,0:T(8,128)(2,1)S(1)}, bf16[480,128]{1,0:T(8,128)(2,1)S(1)}, u32[]{:S(2)}, u32[]{:S(2)}) %collective-permute-start.6) | collective-permute-done | bytes 122912 | tf_op jit(solution)/shard_map/ppermute | solution.py:73
  28.1 3.6 %attention.1 = (bf16[160,128]{1,0:T(8,128)(2,1)S(1)}, bf16[160,128]{1,0:T(8,128)(2,1)S(1)}, bf16[160,128]{1,0:T(8,128)(2,1)S(1)}, bf16[160,128]{1,0:T(8,128)(2,1...) custom-call(bf16[480,128]{1,0:T(8,128)(2,1)S(1)} %get-tuple-element., ...), custom_call_target="tpu_custom_call" | custom-call | flops 838860800 | bytes 1048576 | tf_op jit(solution)/shard_map/attention/pallas_call | solution.py:200
  31.6 2.0 %collective-permute-start.7 = (bf16[160,128]{1,0:T(8,128)(2,1)S(1)}, bf16[160,128]{1,0:T(8,128)(2,1)S(1)}, u32[]{:S(2)}, u32[]{:S(2)}) collective-permute-start(bf16[160,128]{1,0:T(8,128)(2,1)S(1)} %get-tuple-element.27), channel_id=1, source_target_pairs={{14,0},{12,2},{10,4},{8,6},{6,8},{4,10},{2,12},{0,14},{15,1},{13,3... | collective-permute-start | bytes 122888 | tf_op jit(solution)/shard_map/ppermute | solution.py:73
  33.6 1.8 %collective-permute-start.8 = (bf16[160,128]{1,0:T(8,128)(2,1)S(1)}, bf16[160,128]{1,0:T(8,128)(2,1)S(1)}, u32[]{:S(2)}, u32[]{:S(2)}) collective-permute-start(bf16[160,128]{1,0:T(8,128)(2,1)S(1)} %get-tuple-element.28), channel_id=1, source_target_pairs={{12,0},{14,2},{8,4},{10,6},{4,8},{6,10},{0,12},{2,14},{13,1},{15,3... | collective-permute-start | bytes 122888 | tf_op jit(solution)/shard_map/ppermute | solution.py:73
  35.4 2.9 %collective-permute-start.9 = (bf16[160,128]{1,0:T(8,128)(2,1)S(1)}, bf16[160,128]{1,0:T(8,128)(2,1)S(1)}, u32[]{:S(2)}, u32[]{:S(2)}) collective-permute-start(bf16[160,128]{1,0:T(8,128)(2,1)S(1)} %get-tuple-element.29), channel_id=1, source_target_pairs={{10,0},{8,2},{14,4},{12,6},{2,8},{0,10},{6,12},{4,14},{11,1},{9,3}... | collective-permute-start | bytes 122888 | tf_op jit(solution)/shard_map/ppermute | solution.py:73
  38.3 1.0 %collective-permute-start.10 = (bf16[160,128]{1,0:T(8,128)(2,1)S(1)}, bf16[160,128]{1,0:T(8,128)(2,1)S(1)}, u32[]{:S(2)}, u32[]{:S(2)}) collective-permute-start(bf16[160,128]{1,0:T(8,128)(2,1)S(1)} %get-tuple-element.30), channel_id=1, source_target_pairs={{8,0},{10,2},{12,4},{14,6},{0,8},{2,10},{4,12},{6,14},{9,1},{11,3}... | collective-permute-start | bytes 122888 | tf_op jit(solution)/shard_map/ppermute | solution.py:73
  39.4 1.0 %collective-permute-start.11 = (bf16[160,128]{1,0:T(8,128)(2,1)S(1)}, bf16[160,128]{1,0:T(8,128)(2,1)S(1)}, u32[]{:S(2)}, u32[]{:S(2)}) collective-permute-start(bf16[160,128]{1,0:T(8,128)(2,1)S(1)} %get-tuple-element.31), channel_id=1, source_target_pairs={{6,0},{4,2},{2,4},{0,6},{14,8},{12,10},{10,12},{8,14},{7,1},{5,3},... | collective-permute-start | bytes 122888 | tf_op jit(solution)/shard_map/ppermute | solution.py:73
  40.4 0.9 %collective-permute-start.12 = (bf16[160,128]{1,0:T(8,128)(2,1)S(1)}, bf16[160,128]{1,0:T(8,128)(2,1)S(1)}, u32[]{:S(2)}, u32[]{:S(2)}) collective-permute-start(bf16[160,128]{1,0:T(8,128)(2,1)S(1)} %get-tuple-element.32), channel_id=1, source_target_pairs={{4,0},{6,2},{0,4},{2,6},{12,8},{14,10},{8,12},{10,14},{5,1},{7,3},... | collective-permute-start | bytes 122888 | tf_op jit(solution)/shard_map/ppermute | solution.py:73
  41.3 1.6 %collective-permute-start.13 = (bf16[160,128]{1,0:T(8,128)(2,1)S(1)}, bf16[160,128]{1,0:T(8,128)(2,1)S(1)}, u32[]{:S(2)}, u32[]{:S(2)}) collective-permute-start(bf16[160,128]{1,0:T(8,128)(2,1)S(1)} %get-tuple-element.33), channel_id=1, source_target_pairs={{2,0},{0,2},{6,4},{4,6},{10,8},{8,10},{14,12},{12,14},{3,1},{1,3},... | collective-permute-start | bytes 122888 | tf_op jit(solution)/shard_map/ppermute | solution.py:73
  42.9 0.8 %collective-permute-done.9.refs_3_ = bf16[160,128]{1,0:T(8,128)(2,1)S(1)} collective-permute-done((bf16[160,128]{1,0:T(8,128)(2,1)S(1)}, bf16[160,128]{1,0:T(8,128)(2,1)S(1)}, u32[]{:S(2)}, u32[]{:S(2)}) %collective-permute-start.9) | collective-permute-done | bytes 40992 | tf_op jit(solution)/shard_map/ppermute | solution.py:73
  43.7 0.0 collective-permute-done.10.refs_4_
  43.7 0.9 %collective-permute-done.11.refs_5_ = bf16[160,128]{1,0:T(8,128)(2,1)S(1)} collective-permute-done((bf16[160,128]{1,0:T(8,128)(2,1)S(1)}, bf16[160,128]{1,0:T(8,128)(2,1)S(1)}, u32[]{:S(2)}, u32[]{:S(2)}) %collective-permute-start.11) | collective-permute-done | bytes 40992 | tf_op jit(solution)/shard_map/ppermute | solution.py:73
  44.6 0.7 %collective-permute-done.13.refs_7_ = bf16[160,128]{1,0:T(8,128)(2,1)S(1)} collective-permute-done((bf16[160,128]{1,0:T(8,128)(2,1)S(1)}, bf16[160,128]{1,0:T(8,128)(2,1)S(1)}, u32[]{:S(2)}, u32[]{:S(2)}) %collective-permute-start.13) | collective-permute-done | bytes 40992 | tf_op jit(solution)/shard_map/ppermute | solution.py:73
  45.3 0.8 %unpack.1 = (bf16[128,1024]{1,0:T(8,128)(2,1)}, bf16[32,1024]{1,0:T(8,128)(2,1)}) custom-call(bf16[160,128]{1,0:T(8,128)(2,1)S(1)} %get-tuple-element.26.refs_0_, bf16[160,128]{1,0:T(8,128)(2,1)S(1)} %collective-permute-done.7.refs_1_, bf16[160,128]{1,0:T(8,128)(2,1)S(1)} %collective-permute-done.8.refs_2_, ...), custom_call_target="tpu_custom_call" | custom-call | tf_op jit(solution)/shard_map/unpack/pallas_call | solution.py:223
  (7 shorter events, 0.0 us)
Async XLA Ops:
  2.3 10.8 %collective-permute-start = (bf16[480,128]{1,0:T(8,128)(2,1)S(1)}, bf16[480,128]{1,0:T(8,128)(2,1)S(1)}, u32[]{:S(2)}, u32[]{:S(2)}) collective-permute-start(bf16[480,128]{1,0:T(8,128)(2,1)S(1)} %get-tuple-element.19), channel_id=1, source_target_pairs={{0,8},{2,10},{4,12},{6,14},{8,0},{10,2},{12,4},{14,6},{1,9},{3,11}... | collective-permute-start | bytes 368648 | tf_op jit(solution)/shard_map/ppermute | solution.py:73
  6.4 15.9 %collective-permute-start.1 = (bf16[480,128]{1,0:T(8,128)(2,1)S(1)}, bf16[480,128]{1,0:T(8,128)(2,1)S(1)}, u32[]{:S(2)}, u32[]{:S(2)}) collective-permute-start(bf16[480,128]{1,0:T(8,128)(2,1)S(1)} %get-tuple-element.20), channel_id=1, source_target_pairs={{0,2},{2,0},{4,6},{6,4},{8,10},{10,8},{12,14},{14,12},{1,3},{3,1},... | collective-permute-start | bytes 368648 | tf_op jit(solution)/shard_map/ppermute | solution.py:73
  7.9 14.4 %collective-permute-start.2 = (bf16[480,128]{1,0:T(8,128)(2,1)S(1)}, bf16[480,128]{1,0:T(8,128)(2,1)S(1)}, u32[]{:S(2)}, u32[]{:S(2)}) collective-permute-start(bf16[480,128]{1,0:T(8,128)(2,1)S(1)} %get-tuple-element.21), channel_id=1, source_target_pairs={{0,4},{2,6},{4,0},{6,2},{8,12},{10,14},{12,8},{14,10},{1,5},{3,7},... | collective-permute-start | bytes 368648 | tf_op jit(solution)/shard_map/ppermute | solution.py:73
  9.5 13.9 %collective-permute-start.3 = (bf16[480,128]{1,0:T(8,128)(2,1)S(1)}, bf16[480,128]{1,0:T(8,128)(2,1)S(1)}, u32[]{:S(2)}, u32[]{:S(2)}) collective-permute-start(bf16[480,128]{1,0:T(8,128)(2,1)S(1)} %get-tuple-element.22), channel_id=1, source_target_pairs={{0,10},{2,8},{4,14},{6,12},{8,2},{10,0},{12,6},{14,4},{1,11},{3,9}... | collective-permute-start | bytes 368648 | tf_op jit(solution)/shard_map/ppermute | solution.py:73
  9.8 13.6 %collective-permute-start.4 = (bf16[480,128]{1,0:T(8,128)(2,1)S(1)}, bf16[480,128]{1,0:T(8,128)(2,1)S(1)}, u32[]{:S(2)}, u32[]{:S(2)}) collective-permute-start(bf16[480,128]{1,0:T(8,128)(2,1)S(1)} %get-tuple-element.23), channel_id=1, source_target_pairs={{0,12},{2,14},{4,8},{6,10},{8,4},{10,6},{12,0},{14,2},{1,13},{3,15... | collective-permute-start | bytes 368648 | tf_op jit(solution)/shard_map/ppermute | solution.py:73
  13.1 12.2 %collective-permute-start.5 = (bf16[480,128]{1,0:T(8,128)(2,1)S(1)}, bf16[480,128]{1,0:T(8,128)(2,1)S(1)}, u32[]{:S(2)}, u32[]{:S(2)}) collective-permute-start(bf16[480,128]{1,0:T(8,128)(2,1)S(1)} %get-tuple-element.24), channel_id=1, source_target_pairs={{0,14},{2,12},{4,10},{6,8},{8,6},{10,4},{12,2},{14,0},{1,15},{3,13... | collective-permute-start | bytes 368648 | tf_op jit(solution)/shard_map/ppermute | solution.py:73
  22.3 5.8 %collective-permute-start.6 = (bf16[480,128]{1,0:T(8,128)(2,1)S(1)}, bf16[480,128]{1,0:T(8,128)(2,1)S(1)}, u32[]{:S(2)}, u32[]{:S(2)}) collective-permute-start(bf16[480,128]{1,0:T(8,128)(2,1)S(1)} %get-tuple-element.25), channel_id=1, source_target_pairs={{0,6},{2,4},{4,2},{6,0},{8,14},{10,12},{12,10},{14,8},{1,7},{3,5},... | collective-permute-start | bytes 368648 | tf_op jit(solution)/shard_map/ppermute | solution.py:73
  31.6 8.8 %collective-permute-start.7 = (bf16[160,128]{1,0:T(8,128)(2,1)S(1)}, bf16[160,128]{1,0:T(8,128)(2,1)S(1)}, u32[]{:S(2)}, u32[]{:S(2)}) collective-permute-start(bf16[160,128]{1,0:T(8,128)(2,1)S(1)} %get-tuple-element.27), channel_id=1, source_target_pairs={{14,0},{12,2},{10,4},{8,6},{6,8},{4,10},{2,12},{0,14},{15,1},{13,3... | collective-permute-start | bytes 122888 | tf_op jit(solution)/shard_map/ppermute | solution.py:73
  33.6 7.7 %collective-permute-start.8 = (bf16[160,128]{1,0:T(8,128)(2,1)S(1)}, bf16[160,128]{1,0:T(8,128)(2,1)S(1)}, u32[]{:S(2)}, u32[]{:S(2)}) collective-permute-start(bf16[160,128]{1,0:T(8,128)(2,1)S(1)} %get-tuple-element.28), channel_id=1, source_target_pairs={{12,0},{14,2},{8,4},{10,6},{4,8},{6,10},{0,12},{2,14},{13,1},{15,3... | collective-permute-start | bytes 122888 | tf_op jit(solution)/shard_map/ppermute | solution.py:73
  35.4 8.3 %collective-permute-start.9 = (bf16[160,128]{1,0:T(8,128)(2,1)S(1)}, bf16[160,128]{1,0:T(8,128)(2,1)S(1)}, u32[]{:S(2)}, u32[]{:S(2)}) collective-permute-start(bf16[160,128]{1,0:T(8,128)(2,1)S(1)} %get-tuple-element.29), channel_id=1, source_target_pairs={{10,0},{8,2},{14,4},{12,6},{2,8},{0,10},{6,12},{4,14},{11,1},{9,3}... | collective-permute-start | bytes 122888 | tf_op jit(solution)/shard_map/ppermute | solution.py:73
  38.3 5.3 %collective-permute-start.10 = (bf16[160,128]{1,0:T(8,128)(2,1)S(1)}, bf16[160,128]{1,0:T(8,128)(2,1)S(1)}, u32[]{:S(2)}, u32[]{:S(2)}) collective-permute-start(bf16[160,128]{1,0:T(8,128)(2,1)S(1)} %get-tuple-element.30), channel_id=1, source_target_pairs={{8,0},{10,2},{12,4},{14,6},{0,8},{2,10},{4,12},{6,14},{9,1},{11,3}... | collective-permute-start | bytes 122888 | tf_op jit(solution)/shard_map/ppermute | solution.py:73
  39.4 5.2 %collective-permute-start.11 = (bf16[160,128]{1,0:T(8,128)(2,1)S(1)}, bf16[160,128]{1,0:T(8,128)(2,1)S(1)}, u32[]{:S(2)}, u32[]{:S(2)}) collective-permute-start(bf16[160,128]{1,0:T(8,128)(2,1)S(1)} %get-tuple-element.31), channel_id=1, source_target_pairs={{6,0},{4,2},{2,4},{0,6},{14,8},{12,10},{10,12},{8,14},{7,1},{5,3},... | collective-permute-start | bytes 122888 | tf_op jit(solution)/shard_map/ppermute | solution.py:73
  40.4 4.1 %collective-permute-start.12 = (bf16[160,128]{1,0:T(8,128)(2,1)S(1)}, bf16[160,128]{1,0:T(8,128)(2,1)S(1)}, u32[]{:S(2)}, u32[]{:S(2)}) collective-permute-start(bf16[160,128]{1,0:T(8,128)(2,1)S(1)} %get-tuple-element.32), channel_id=1, source_target_pairs={{4,0},{6,2},{0,4},{2,6},{12,8},{14,10},{8,12},{10,14},{5,1},{7,3},... | collective-permute-start | bytes 122888 | tf_op jit(solution)/shard_map/ppermute | solution.py:73
  41.3 4.0 %collective-permute-start.13 = (bf16[160,128]{1,0:T(8,128)(2,1)S(1)}, bf16[160,128]{1,0:T(8,128)(2,1)S(1)}, u32[]{:S(2)}, u32[]{:S(2)}) collective-permute-start(bf16[160,128]{1,0:T(8,128)(2,1)S(1)} %get-tuple-element.33), channel_id=1, source_target_pairs={{2,0},{0,2},{6,4},{4,6},{10,8},{8,10},{14,12},{12,14},{3,1},{1,3},... | collective-permute-start | bytes 122888 | tf_op jit(solution)/shard_map/ppermute | solution.py:73

commit v4 on v3

--- a/solution.py
+++ b/solution.py
@@ -64,9 +64,13 @@
     middle = size // 2
 
     def rank(step):
-        return (step != middle, step & (step - 1) and 1 + (step < middle), step)
+        return (step == size - 1, step != middle, step & (step - 1) and 1 + (step < middle), step)
 
     return sorted(range(1, size), key=rank)
+
+
+def return_order(size):
+    return range(size - 1, 0, -1)
 
 
 def exchange(blocks, moves, steps):
@@ -109,19 +113,29 @@
     return lax.dot_general(left, right, (((1,), (1,)), ((), ())), preferred_element_type=jnp.float32)
 
 
-def weighed(weights, values_and_ones):
-    product = jnp.dot(weights.astype(jnp.bfloat16), values_and_ones, preferred_element_type=jnp.float32)
+def times(weights, values_and_ones):
+    return jnp.dot(weights.astype(jnp.bfloat16), values_and_ones, preferred_element_type=jnp.float32)
+
+
+def weighed(product):
     return product[:, :HEAD_DIM] * (1.0 / product[:, HEAD_DIM:])
 
 
-def self_attend(queries, key_rows, values_and_ones):
+def start_attend(queries, key_rows, values_and_ones):
     scores = dot_t(queries, key_rows)
     top = jnp.max(scores, axis=1, keepdims=True)
-    return weighed(jnp.exp2((scores - top) * SCALE_LOG2), values_and_ones)
+    return top, times(jnp.exp2((scores - top) * SCALE_LOG2), values_and_ones)
+
+
+def more_attend(top, product, queries, key_rows, values_and_ones):
+    scores = dot_t(queries, key_rows)
+    new_top = jnp.maximum(top, jnp.max(scores, axis=1, keepdims=True))
+    product = product * jnp.exp2((top - new_top) * SCALE_LOG2)
+    return product + times(jnp.exp2((scores - new_top) * SCALE_LOG2), values_and_ones)
 
 
 def cross_attend(queries, key_rows, values_and_ones):
-    return weighed(jnp.exp2(dot_t(queries, key_rows) * SCALE_LOG2), values_and_ones)
+    return weighed(times(jnp.exp2(dot_t(queries, key_rows) * SCALE_LOG2), values_and_ones))
 
 
 def unit_rows(tokens):
@@ -129,36 +143,58 @@
     return entries * lax.rsqrt(jnp.mean(entries * entries, axis=1, keepdims=True) + 1e-06)
 
 
-def attention_kernel(size, video_rows, audio_rows, *refs):
-    blocks = refs[:size]
-    gain_refs = refs[size : size + 4]
-    outs = refs[size + 4 : 2 * size + 4]
-    vq, vk, vv, aq, ak, av, v_self, a_self, gains, sem = refs[2 * size + 4 :]
+def assemble(blocks, cols, wholes):
+    for at, block in enumerate(blocks):
+        row = 0
+        for whole, rows in wholes:
+            if whole is not None:
+                whole[pl.ds(at * rows, rows), :HEAD_DIM] = block[pl.ds(row, rows), cols]
+            row += rows
+
+
+def fill_ones(*arrays):
+    for values in arrays:
+        values[:, HEAD_DIM:] = jnp.ones((values.shape[0], HEAD_DIM), jnp.bfloat16)
+
+
+def early_kernel(rv, *refs):
+    blocks, (tops, products, vq, vk, vv) = refs[:-5], refs[-5:]
+    fill_ones(vv)
+    for head in range(tops.shape[0]):
+        assemble(blocks, pl.ds(head * HEAD_DIM, HEAD_DIM), ((vq, rv), (vk, rv), (vv, rv)))
+        top, products[head] = start_attend(vq[...], vk[...], vv[...])
+        tops[head] = jnp.broadcast_to(top, tops.shape[1:])
+
+
+def attention_kernel(size, rv, ra, *refs):
+    blocks, tops, products, gain_refs = refs[:size], refs[size], refs[size + 1], refs[size + 2 : size + 6]
+    outs = refs[size + 6 : 2 * size + 6]
+    vq, vk, vv, aq, ak, av, v_self, a_self, gains, sem = refs[2 * size + 6 :]
     me = lax.axis_index("seq")
-    heads = blocks[0].shape[1] // HEAD_DIM
-    rv, ra = video_rows, audio_rows
+    early, late = pl.ds(0, (size - 1) * rv), pl.ds((size - 1) * rv, rv)
     copies = [
         pltpu.make_async_copy(ref, gains.at[at], sem.at[at]) for at, ref in enumerate(gain_refs)
     ]
     for copy in copies:
         copy.start()
-    for values in (vv, av, v_self, a_self):
-        values[:, HEAD_DIM:] = jnp.ones((values.shape[0], HEAD_DIM), jnp.bfloat16)
-    for head in range(heads):
+    fill_ones(vv, av, v_self, a_self)
+    for head in range(tops.shape[0]):
         cols = pl.ds(head * HEAD_DIM, HEAD_DIM)
-        for at, block in enumerate(blocks):
-            row = 0
-            for whole, rows in ((vq, rv), (vk, rv), (vv, rv), (aq, ra), (ak, ra), (av, ra)):
-                whole[pl.ds(at * rows, rows), :HEAD_DIM] = block[pl.ds(row, rows), cols]
-                row += rows
-        a_result = self_attend(aq[...], ak[...], av[...]).astype(jnp.bfloat16)
-        v_result = self_attend(vq[...], vk[...], vv[...]).astype(jnp.bfloat16)
+        assemble(blocks, cols, ((vq, rv), (vk, rv), (vv, rv), (aq, ra), (ak, ra), (av, ra)))
+        _, product = start_attend(aq[...], ak[...], av[...])
+        a_result = weighed(product).astype(jnp.bfloat16)
         a_self[:, :HEAD_DIM] = a_result
-        v_self[:, :HEAD_DIM] = v_result
+        product = more_attend(tops[head, :, :1], products[head], vq[early, :], vk[late, :], vv[late, :])
+        v_self[early, :HEAD_DIM] = weighed(product).astype(jnp.bfloat16)
+        _, product = start_attend(vq[late, :], vk[...], vv[...])
+        v_self[late, :HEAD_DIM] = weighed(product).astype(jnp.bfloat16)
+        v_result = v_self[:, :HEAD_DIM]
         if head == 0:
             for copy in copies:
                 copy.wait()
-        vq_gain, vk_gain, aq_gain, ak_gain = [gains[at, pl.ds(me * heads + head, 1), :] for at in range(4)]
+        vq_gain, vk_gain, aq_gain, ak_gain = [
+            gains[at, pl.ds(me * tops.shape[0] + head, 1), :] for at in range(4)
+        ]
         a_unit, v_unit = unit_rows(a_result), unit_rows(v_result)
         a_query, a_key = (a_unit * aq_gain).astype(jnp.bfloat16), (a_unit * ak_gain).astype(jnp.bfloat16)
         v_query, v_key = (v_unit * vq_gain).astype(jnp.bfloat16), (v_unit * vk_gain).astype(jnp.bfloat16)
@@ -196,11 +232,28 @@
         pltpu.with_memory_space_constraint(gain.reshape(columns // HEAD_DIM, HEAD_DIM), pltpu.HBM)
         for gain in gains
     ]
-    tv, ta = rv * size, ra * size
+    tv, ta, te, heads = rv * size, ra * size, rv * (size - 1), width // HEAD_DIM
+    arrival = order
+    arrived = [blocks[step] for step in arrival]
+    tops, products = pl.pallas_call(
+        functools.partial(early_kernel, rv),
+        out_shape=[
+            jax.ShapeDtypeStruct((heads, te, HEAD_DIM), jnp.float32),
+            jax.ShapeDtypeStruct((heads, te, 2 * HEAD_DIM), jnp.float32),
+        ],
+        in_specs=[in_vmem] * (size - 1),
+        out_specs=[in_vmem] * 2,
+        scratch_shapes=[pltpu.VMEM((te, parts * HEAD_DIM), jnp.bfloat16) for parts in (1, 1, 2)],
+        compiler_params=pltpu.CompilerParams(vmem_limit_bytes=VMEM_LIMIT),
+        cost_estimate=pl.CostEstimate(
+            flops=4 * width * te * te, bytes_accessed=8 * te * width, transcendentals=heads * te * te
+        ),
+        name="early",
+    )(*arrived[:-1])
     results = pl.pallas_call(
         functools.partial(attention_kernel, size, rv, ra),
         out_shape=[jax.ShapeDtypeStruct((rv + ra, width), vq.dtype)] * size,
-        in_specs=[in_vmem] * size + [in_hbm] * 4,
+        in_specs=[in_vmem] * (size + 2) + [in_hbm] * 4,
         out_specs=[in_vmem] * size,
         scratch_shapes=[
             pltpu.VMEM((rows, parts * HEAD_DIM), jnp.bfloat16)
@@ -209,19 +262,18 @@
         + [pltpu.VMEM((4, columns // HEAD_DIM, HEAD_DIM), jnp.float32), pltpu.SemaphoreType.DMA((4,))],
         compiler_params=pltpu.CompilerParams(vmem_limit_bytes=VMEM_LIMIT),
         cost_estimate=pl.CostEstimate(
-            flops=4 * width * (tv * tv + ta * ta + 2 * tv * ta),
+            flops=4 * width * (2 * tv * rv + ta * ta + 2 * tv * ta),
             bytes_accessed=8 * tv * width,
-            transcendentals=(width // HEAD_DIM) * (tv * tv + ta * ta + 2 * tv * ta),
+            transcendentals=heads * (2 * tv * rv + ta * ta + 2 * tv * ta),
         ),
         name="attention",
-    )(*[blocks[step] for step in order], *gains)
-    results = dict(zip(order, results))
+    )(*arrived, tops, products, *gains)
+    results = dict(zip(arrival, results))
     inverse = [[(b, a) for a, b in move] for move in moves]
-    farthest_first = range(size - 1, 0, -1)
-    back = [results[0], *exchange(results, inverse, farthest_first).values()]
+    back = [results[0], *exchange(results, inverse, return_order(size)).values()]
     return tuple(
         pl.pallas_call(
-            functools.partial(unpack_kernel, size, rv, (0, *farthest_first)),
+            functools.partial(unpack_kernel, size, rv, (0, *return_order(size))),
             out_shape=[
                 jax.ShapeDtypeStruct((rv, columns), vq.dtype),
                 jax.ShapeDtypeStruct((ra, columns), vq.dtype),
@@ -239,7 +291,7 @@
 
     def per_device(*args):
         heads = args[0].shape[1] // HEAD_DIM
-        if heads % size == 0:
+        if size > 1 and heads % size == 0:
             return head_plan(size, *args)
         return gather_plan(*args)
 

time: 46.3 us -> 46 us (level)
  waiting for transfers between devices: 9.02 us -> 5.84 us
  starting transfers between devices: 30.4 us -> 31.9 us
  Pallas kernels: 6.02 us -> 7.31 us
    ppermute x14, waiting for transfers between devices: 9.02 us -> 5.84 us  [exchange(): lax.ppermute(blocks[step], 'seq', moves[step])]
    pallas_call x1 -> x2, Pallas kernels: 0.81 us -> 2.81 us  [the longest x1 2.01 us: head_plan(): pl.pallas_call(functools.partial(early_kernel, rv), out_shape=[jax.ShapeD...]
    ppermute x14, starting transfers between devices: 30.4 us -> 31.9 us  [exchange(): lax.ppermute(blocks[step], 'seq', moves[step])]
    pallas_call x1, Pallas kernels: 3.55 us -> 2.84 us  [head_plan(): pl.pallas_call(functools.partial(attention_kernel, size, rv, ra), out_sha...]
  transfers between devices with their start and end apart: 14 -> 14, of which waited for: 7 -> 6; matrix products, arithmetic and copies ran while one was open for 0% -> 0% of each run, Pallas kernels for 0% -> 4%
where the time goes in v4:
time: 46 us; the launch traced here: 45.7 us
  starting transfers between devices  31.9 us (69%)
  Pallas kernels  7.31 us (16%)
  waiting for transfers between devices  5.84 us (13%)
  between operations  0.67 us (1%)
    ppermute x14, starting transfers between devices, exchange(): lax.ppermute(blocks[step], 'seq', moves[step])  31.9 us
    ppermute x14, waiting for transfers between devices, exchange(): lax.ppermute(blocks[step], 'seq', moves[step])  5.84 us
    pallas_call x1, Pallas kernels, head_plan(): pl.pallas_call(functools.partial(attention_kernel, size, rv, ra), out_sha...  2.84 us
    pallas_call x1, Pallas kernels, head_plan(): pl.pallas_call(functools.partial(early_kernel, rv), out_shape=[jax.ShapeD...  2.01 us
    pallas_call x1, Pallas kernels, head_plan(): pl.pallas_call(functools.partial(pack_kernel, size, order), out_shape=[ja...  1.66 us
  transfers between devices with their start and end apart: 14, of which 6 were waited for; matrix products, arithmetic and copies ran while one was open for 0% of the time, Pallas kernels for 4%

profile of v4, /device:TPU:0, one launch (start us, length us, event | category | flops | bytes accessed | tf_op | source)
XLA Modules:
  0.0 45.7 jit_solution(5408871038450786116)
XLA Ops:
  0.6 1.7 %pack.1 = (bf16[480,128]{1,0:T(8,128)(2,1)S(1)}, bf16[480,128]{1,0:T(8,128)(2,1)S(1)}, bf16[480,128]{1,0:T(8,128)(2,1)S(1)}, bf16[480,128]{1,0:T(8,128)(2,1)S(1)...) custom-call(bf16[128,1024]{1,0:T(8,128)(2,1)} %refs_0_.1, ...), custom_call_target="tpu_custom_call" | custom-call | tf_op jit(solution)/shard_map/pack/pallas_call | solution.py:219
  2.3 4.1 %collective-permute-start = (bf16[480,128]{1,0:T(8,128)(2,1)S(1)}, bf16[480,128]{1,0:T(8,128)(2,1)S(1)}, u32[]{:S(2)}, u32[]{:S(2)}) collective-permute-start(bf16[480,128]{1,0:T(8,128)(2,1)S(1)} %get-tuple-element.21), channel_id=1, source_target_pairs={{0,8},{2,10},{4,12},{6,14},{8,0},{10,2},{12,4},{14,6},{1,9},{3,11}... | collective-permute-start | bytes 368648 | tf_op jit(solution)/shard_map/ppermute | solution.py:77
  6.4 1.5 %collective-permute-start.1 = (bf16[480,128]{1,0:T(8,128)(2,1)S(1)}, bf16[480,128]{1,0:T(8,128)(2,1)S(1)}, u32[]{:S(2)}, u32[]{:S(2)}) collective-permute-start(bf16[480,128]{1,0:T(8,128)(2,1)S(1)} %get-tuple-element.22), channel_id=1, source_target_pairs={{0,2},{2,0},{4,6},{6,4},{8,10},{10,8},{12,14},{14,12},{1,3},{3,1},... | collective-permute-start | bytes 368648 | tf_op jit(solution)/shard_map/ppermute | solution.py:77
  7.9 1.6 %collective-permute-start.2 = (bf16[480,128]{1,0:T(8,128)(2,1)S(1)}, bf16[480,128]{1,0:T(8,128)(2,1)S(1)}, u32[]{:S(2)}, u32[]{:S(2)}) collective-permute-start(bf16[480,128]{1,0:T(8,128)(2,1)S(1)} %get-tuple-element.23), channel_id=1, source_target_pairs={{0,4},{2,6},{4,0},{6,2},{8,12},{10,14},{12,8},{14,10},{1,5},{3,7},... | collective-permute-start | bytes 368648 | tf_op jit(solution)/shard_map/ppermute | solution.py:77
  9.5 0.3 collective-permute-start.3
  9.8 2.5 %collective-permute-start.4 = (bf16[480,128]{1,0:T(8,128)(2,1)S(1)}, bf16[480,128]{1,0:T(8,128)(2,1)S(1)}, u32[]{:S(2)}, u32[]{:S(2)}) collective-permute-start(bf16[480,128]{1,0:T(8,128)(2,1)S(1)} %get-tuple-element.25), channel_id=1, source_target_pairs={{0,12},{2,14},{4,8},{6,10},{8,4},{10,6},{12,0},{14,2},{1,13},{3,15... | collective-permute-start | bytes 368648 | tf_op jit(solution)/shard_map/ppermute | solution.py:77
  12.2 0.8 %collective-permute-done.refs_1_ = bf16[480,128]{1,0:T(8,128)(2,1)S(1)} collective-permute-done((bf16[480,128]{1,0:T(8,128)(2,1)S(1)}, bf16[480,128]{1,0:T(8,128)(2,1)S(1)}, u32[]{:S(2)}, u32[]{:S(2)}) %collective-permute-start) | collective-permute-done | bytes 122912 | tf_op jit(solution)/shard_map/ppermute | solution.py:77
  13.1 1.9 %collective-permute-start.5 = (bf16[480,128]{1,0:T(8,128)(2,1)S(1)}, bf16[480,128]{1,0:T(8,128)(2,1)S(1)}, u32[]{:S(2)}, u32[]{:S(2)}) collective-permute-start(bf16[480,128]{1,0:T(8,128)(2,1)S(1)} %get-tuple-element.26), channel_id=1, source_target_pairs={{0,6},{2,4},{4,2},{6,0},{8,14},{10,12},{12,10},{14,8},{1,7},{3,5},... | collective-permute-start | bytes 368648 | tf_op jit(solution)/shard_map/ppermute | solution.py:77
  15.0 6.2 %collective-permute-start.6 = (bf16[480,128]{1,0:T(8,128)(2,1)S(1)}, bf16[480,128]{1,0:T(8,128)(2,1)S(1)}, u32[]{:S(2)}, u32[]{:S(2)}) collective-permute-start(bf16[480,128]{1,0:T(8,128)(2,1)S(1)} %get-tuple-element.27), channel_id=1, source_target_pairs={{0,14},{2,12},{4,10},{6,8},{8,6},{10,4},{12,2},{14,0},{1,15},{3,13... | collective-permute-start | bytes 368648 | tf_op jit(solution)/shard_map/ppermute | solution.py:77
  21.2 2.1 %collective-permute-done.3.refs_4_ = bf16[480,128]{1,0:T(8,128)(2,1)S(1)} collective-permute-done((bf16[480,128]{1,0:T(8,128)(2,1)S(1)}, bf16[480,128]{1,0:T(8,128)(2,1)S(1)}, u32[]{:S(2)}, u32[]{:S(2)}) %collective-permute-start.3) | collective-permute-done | bytes 122912 | tf_op jit(solution)/shard_map/ppermute | solution.py:77
  23.4 0.3 collective-permute-done.5.refs_6_
  23.6 2.0 %early.1 = (f32[1,896,128]{2,1,0:T(8,128)S(1)}, f32[1,896,256]{2,1,0:T(8,128)S(1)}) custom-call(bf16[480,128]{1,0:T(8,128)(2,1)S(1)} %get-tuple-element.20.refs_0_, bf16[480,128]{1,0:T(8,128)(2,1)S(1)} %collective-permute-done.refs_1_, bf16[480,128]{1,0:T(8,128)(2,1)S(1)} %collective-permute-done.1.refs_2_, ...), custom_call_target="tpu_custom_call" | custom-call | flops 411041792 | bytes 917504 | tf_op jit(solution)/shard_map/early/pallas_call | solution.py:238
  25.6 2.8 %attention.1 = (bf16[160,128]{1,0:T(8,128)(2,1)S(1)}, bf16[160,128]{1,0:T(8,128)(2,1)S(1)}, bf16[160,128]{1,0:T(8,128)(2,1)S(1)}, bf16[160,128]{1,0:T(8,128)(2,1...) custom-call(bf16[480,128]{1,0:T(8,128)(2,1)S(1)} %get-tuple-element., ...), custom_call_target="tpu_custom_call" | custom-call | flops 436207616 | bytes 1048576 | tf_op jit(solution)/shard_map/attention/pallas_call | solution.py:253
  28.5 6.4 %collective-permute-start.7 = (bf16[160,128]{1,0:T(8,128)(2,1)S(1)}, bf16[160,128]{1,0:T(8,128)(2,1)S(1)}, u32[]{:S(2)}, u32[]{:S(2)}) collective-permute-start(bf16[160,128]{1,0:T(8,128)(2,1)S(1)} %get-tuple-element.31), channel_id=1, source_target_pairs={{14,0},{12,2},{10,4},{8,6},{6,8},{4,10},{2,12},{0,14},{15,1},{13,3... | collective-permute-start | bytes 122888 | tf_op jit(solution)/shard_map/ppermute | solution.py:77
  34.9 0.1 collective-permute-start.8
  35.0 2.6 %collective-permute-start.9 = (bf16[160,128]{1,0:T(8,128)(2,1)S(1)}, bf16[160,128]{1,0:T(8,128)(2,1)S(1)}, u32[]{:S(2)}, u32[]{:S(2)}) collective-permute-start(bf16[160,128]{1,0:T(8,128)(2,1)S(1)} %get-tuple-element.33), channel_id=1, source_target_pairs={{10,0},{8,2},{14,4},{12,6},{2,8},{0,10},{6,12},{4,14},{11,1},{9,3}... | collective-permute-start | bytes 122888 | tf_op jit(solution)/shard_map/ppermute | solution.py:77
  37.6 1.1 %collective-permute-start.10 = (bf16[160,128]{1,0:T(8,128)(2,1)S(1)}, bf16[160,128]{1,0:T(8,128)(2,1)S(1)}, u32[]{:S(2)}, u32[]{:S(2)}) collective-permute-start(bf16[160,128]{1,0:T(8,128)(2,1)S(1)} %get-tuple-element.34), channel_id=1, source_target_pairs={{8,0},{10,2},{12,4},{14,6},{0,8},{2,10},{4,12},{6,14},{9,1},{11,3}... | collective-permute-start | bytes 122888 | tf_op jit(solution)/shard_map/ppermute | solution.py:77
  38.8 1.5 %collective-permute-start.11 = (bf16[160,128]{1,0:T(8,128)(2,1)S(1)}, bf16[160,128]{1,0:T(8,128)(2,1)S(1)}, u32[]{:S(2)}, u32[]{:S(2)}) collective-permute-start(bf16[160,128]{1,0:T(8,128)(2,1)S(1)} %get-tuple-element.35), channel_id=1, source_target_pairs={{6,0},{4,2},{2,4},{0,6},{14,8},{12,10},{10,12},{8,14},{7,1},{5,3},... | collective-permute-start | bytes 122888 | tf_op jit(solution)/shard_map/ppermute | solution.py:77
  40.2 0.6 %collective-permute-start.12 = (bf16[160,128]{1,0:T(8,128)(2,1)S(1)}, bf16[160,128]{1,0:T(8,128)(2,1)S(1)}, u32[]{:S(2)}, u32[]{:S(2)}) collective-permute-start(bf16[160,128]{1,0:T(8,128)(2,1)S(1)} %get-tuple-element.36), channel_id=1, source_target_pairs={{4,0},{6,2},{0,4},{2,6},{12,8},{14,10},{8,12},{10,14},{5,1},{7,3},... | collective-permute-start | bytes 122888 | tf_op jit(solution)/shard_map/ppermute | solution.py:77
  40.9 1.4 %collective-permute-start.13 = (bf16[160,128]{1,0:T(8,128)(2,1)S(1)}, bf16[160,128]{1,0:T(8,128)(2,1)S(1)}, u32[]{:S(2)}, u32[]{:S(2)}) collective-permute-start(bf16[160,128]{1,0:T(8,128)(2,1)S(1)} %get-tuple-element.37), channel_id=1, source_target_pairs={{2,0},{0,2},{6,4},{4,6},{10,8},{8,10},{14,12},{12,14},{3,1},{1,3},... | collective-permute-start | bytes 122888 | tf_op jit(solution)/shard_map/ppermute | solution.py:77
  42.3 0.9 %collective-permute-done.9.refs_3_ = bf16[160,128]{1,0:T(8,128)(2,1)S(1)} collective-permute-done((bf16[160,128]{1,0:T(8,128)(2,1)S(1)}, bf16[160,128]{1,0:T(8,128)(2,1)S(1)}, u32[]{:S(2)}, u32[]{:S(2)}) %collective-permute-start.9) | collective-permute-done | bytes 40992 | tf_op jit(solution)/shard_map/ppermute | solution.py:77
  43.1 1.1 %collective-permute-done.11.refs_5_ = bf16[160,128]{1,0:T(8,128)(2,1)S(1)} collective-permute-done((bf16[160,128]{1,0:T(8,128)(2,1)S(1)}, bf16[160,128]{1,0:T(8,128)(2,1)S(1)}, u32[]{:S(2)}, u32[]{:S(2)}) %collective-permute-start.11) | collective-permute-done | bytes 40992 | tf_op jit(solution)/shard_map/ppermute | solution.py:77
  44.2 0.6 %collective-permute-done.13.refs_7_ = bf16[160,128]{1,0:T(8,128)(2,1)S(1)} collective-permute-done((bf16[160,128]{1,0:T(8,128)(2,1)S(1)}, bf16[160,128]{1,0:T(8,128)(2,1)S(1)}, u32[]{:S(2)}, u32[]{:S(2)}) %collective-permute-start.13) | collective-permute-done | bytes 40992 | tf_op jit(solution)/shard_map/ppermute | solution.py:77
  44.9 0.8 %unpack.1 = (bf16[128,1024]{1,0:T(8,128)(2,1)}, bf16[32,1024]{1,0:T(8,128)(2,1)}) custom-call(bf16[160,128]{1,0:T(8,128)(2,1)S(1)} %get-tuple-element.30.refs_0_, bf16[160,128]{1,0:T(8,128)(2,1)S(1)} %collective-permute-done.7.refs_1_, bf16[160,128]{1,0:T(8,128)(2,1)S(1)} %collective-permute-done.8.refs_2_, ...), custom_call_target="tpu_custom_call" | custom-call | tf_op jit(solution)/shard_map/unpack/pallas_call | solution.py:275
  (8 shorter events, 0.1 us)
Async XLA Ops:
  2.3 10.8 %collective-permute-start = (bf16[480,128]{1,0:T(8,128)(2,1)S(1)}, bf16[480,128]{1,0:T(8,128)(2,1)S(1)}, u32[]{:S(2)}, u32[]{:S(2)}) collective-permute-start(bf16[480,128]{1,0:T(8,128)(2,1)S(1)} %get-tuple-element.21), channel_id=1, source_target_pairs={{0,8},{2,10},{4,12},{6,14},{8,0},{10,2},{12,4},{14,6},{1,9},{3,11}... | collective-permute-start | bytes 368648 | tf_op jit(solution)/shard_map/ppermute | solution.py:77
  6.4 8.6 %collective-permute-start.1 = (bf16[480,128]{1,0:T(8,128)(2,1)S(1)}, bf16[480,128]{1,0:T(8,128)(2,1)S(1)}, u32[]{:S(2)}, u32[]{:S(2)}) collective-permute-start(bf16[480,128]{1,0:T(8,128)(2,1)S(1)} %get-tuple-element.22), channel_id=1, source_target_pairs={{0,2},{2,0},{4,6},{6,4},{8,10},{10,8},{12,14},{14,12},{1,3},{3,1},... | collective-permute-start | bytes 368648 | tf_op jit(solution)/shard_map/ppermute | solution.py:77
  7.9 13.3 %collective-permute-start.2 = (bf16[480,128]{1,0:T(8,128)(2,1)S(1)}, bf16[480,128]{1,0:T(8,128)(2,1)S(1)}, u32[]{:S(2)}, u32[]{:S(2)}) collective-permute-start(bf16[480,128]{1,0:T(8,128)(2,1)S(1)} %get-tuple-element.23), channel_id=1, source_target_pairs={{0,4},{2,6},{4,0},{6,2},{8,12},{10,14},{12,8},{14,10},{1,5},{3,7},... | collective-permute-start | bytes 368648 | tf_op jit(solution)/shard_map/ppermute | solution.py:77
  9.5 13.9 %collective-permute-start.3 = (bf16[480,128]{1,0:T(8,128)(2,1)S(1)}, bf16[480,128]{1,0:T(8,128)(2,1)S(1)}, u32[]{:S(2)}, u32[]{:S(2)}) collective-permute-start(bf16[480,128]{1,0:T(8,128)(2,1)S(1)} %get-tuple-element.24), channel_id=1, source_target_pairs={{0,10},{2,8},{4,14},{6,12},{8,2},{10,0},{12,6},{14,4},{1,11},{3,9}... | collective-permute-start | bytes 368648 | tf_op jit(solution)/shard_map/ppermute | solution.py:77
  9.8 13.6 %collective-permute-start.4 = (bf16[480,128]{1,0:T(8,128)(2,1)S(1)}, bf16[480,128]{1,0:T(8,128)(2,1)S(1)}, u32[]{:S(2)}, u32[]{:S(2)}) collective-permute-start(bf16[480,128]{1,0:T(8,128)(2,1)S(1)} %get-tuple-element.25), channel_id=1, source_target_pairs={{0,12},{2,14},{4,8},{6,10},{8,4},{10,6},{12,0},{14,2},{1,13},{3,15... | collective-permute-start | bytes 368648 | tf_op jit(solution)/shard_map/ppermute | solution.py:77
  13.1 10.6 %collective-permute-start.5 = (bf16[480,128]{1,0:T(8,128)(2,1)S(1)}, bf16[480,128]{1,0:T(8,128)(2,1)S(1)}, u32[]{:S(2)}, u32[]{:S(2)}) collective-permute-start(bf16[480,128]{1,0:T(8,128)(2,1)S(1)} %get-tuple-element.26), channel_id=1, source_target_pairs={{0,6},{2,4},{4,2},{6,0},{8,14},{10,12},{12,10},{14,8},{1,7},{3,5},... | collective-permute-start | bytes 368648 | tf_op jit(solution)/shard_map/ppermute | solution.py:77
  15.0 10.6 %collective-permute-start.6 = (bf16[480,128]{1,0:T(8,128)(2,1)S(1)}, bf16[480,128]{1,0:T(8,128)(2,1)S(1)}, u32[]{:S(2)}, u32[]{:S(2)}) collective-permute-start(bf16[480,128]{1,0:T(8,128)(2,1)S(1)} %get-tuple-element.27), channel_id=1, source_target_pairs={{0,14},{2,12},{4,10},{6,8},{8,6},{10,4},{12,2},{14,0},{1,15},{3,13... | collective-permute-start | bytes 368648 | tf_op jit(solution)/shard_map/ppermute | solution.py:77
  28.5 11.7 %collective-permute-start.7 = (bf16[160,128]{1,0:T(8,128)(2,1)S(1)}, bf16[160,128]{1,0:T(8,128)(2,1)S(1)}, u32[]{:S(2)}, u32[]{:S(2)}) collective-permute-start(bf16[160,128]{1,0:T(8,128)(2,1)S(1)} %get-tuple-element.31), channel_id=1, source_target_pairs={{14,0},{12,2},{10,4},{8,6},{6,8},{4,10},{2,12},{0,14},{15,1},{13,3... | collective-permute-start | bytes 122888 | tf_op jit(solution)/shard_map/ppermute | solution.py:77
  34.9 6.0 %collective-permute-start.8 = (bf16[160,128]{1,0:T(8,128)(2,1)S(1)}, bf16[160,128]{1,0:T(8,128)(2,1)S(1)}, u32[]{:S(2)}, u32[]{:S(2)}) collective-permute-start(bf16[160,128]{1,0:T(8,128)(2,1)S(1)} %get-tuple-element.32), channel_id=1, source_target_pairs={{12,0},{14,2},{8,4},{10,6},{4,8},{6,10},{0,12},{2,14},{13,1},{15,3... | collective-permute-start | bytes 122888 | tf_op jit(solution)/shard_map/ppermute | solution.py:77
  35.0 8.1 %collective-permute-start.9 = (bf16[160,128]{1,0:T(8,128)(2,1)S(1)}, bf16[160,128]{1,0:T(8,128)(2,1)S(1)}, u32[]{:S(2)}, u32[]{:S(2)}) collective-permute-start(bf16[160,128]{1,0:T(8,128)(2,1)S(1)} %get-tuple-element.33), channel_id=1, source_target_pairs={{10,0},{8,2},{14,4},{12,6},{2,8},{0,10},{6,12},{4,14},{11,1},{9,3}... | collective-permute-start | bytes 122888 | tf_op jit(solution)/shard_map/ppermute | solution.py:77
  37.6 5.5 %collective-permute-start.10 = (bf16[160,128]{1,0:T(8,128)(2,1)S(1)}, bf16[160,128]{1,0:T(8,128)(2,1)S(1)}, u32[]{:S(2)}, u32[]{:S(2)}) collective-permute-start(bf16[160,128]{1,0:T(8,128)(2,1)S(1)} %get-tuple-element.34), channel_id=1, source_target_pairs={{8,0},{10,2},{12,4},{14,6},{0,8},{2,10},{4,12},{6,14},{9,1},{11,3}... | collective-permute-start | bytes 122888 | tf_op jit(solution)/shard_map/ppermute | solution.py:77
  38.8 5.4 %collective-permute-start.11 = (bf16[160,128]{1,0:T(8,128)(2,1)S(1)}, bf16[160,128]{1,0:T(8,128)(2,1)S(1)}, u32[]{:S(2)}, u32[]{:S(2)}) collective-permute-start(bf16[160,128]{1,0:T(8,128)(2,1)S(1)} %get-tuple-element.35), channel_id=1, source_target_pairs={{6,0},{4,2},{2,4},{0,6},{14,8},{12,10},{10,12},{8,14},{7,1},{5,3},... | collective-permute-start | bytes 122888 | tf_op jit(solution)/shard_map/ppermute | solution.py:77
  40.2 4.0 %collective-permute-start.12 = (bf16[160,128]{1,0:T(8,128)(2,1)S(1)}, bf16[160,128]{1,0:T(8,128)(2,1)S(1)}, u32[]{:S(2)}, u32[]{:S(2)}) collective-permute-start(bf16[160,128]{1,0:T(8,128)(2,1)S(1)} %get-tuple-element.36), channel_id=1, source_target_pairs={{4,0},{6,2},{0,4},{2,6},{12,8},{14,10},{8,12},{10,14},{5,1},{7,3},... | collective-permute-start | bytes 122888 | tf_op jit(solution)/shard_map/ppermute | solution.py:77
  40.9 4.0 %collective-permute-start.13 = (bf16[160,128]{1,0:T(8,128)(2,1)S(1)}, bf16[160,128]{1,0:T(8,128)(2,1)S(1)}, u32[]{:S(2)}, u32[]{:S(2)}) collective-permute-start(bf16[160,128]{1,0:T(8,128)(2,1)S(1)} %get-tuple-element.37), channel_id=1, source_target_pairs={{2,0},{0,2},{6,4},{4,6},{10,8},{8,10},{14,12},{12,14},{3,1},{1,3},... | collective-permute-start | bytes 122888 | tf_op jit(solution)/shard_map/ppermute | solution.py:77

commit v5 on v4

--- a/solution.py
+++ b/solution.py
@@ -64,7 +64,13 @@
     middle = size // 2
 
     def rank(step):
-        return (step == size - 1, step != middle, step & (step - 1) and 1 + (step < middle), step)
+        return (
+            step == size - 1,
+            step != middle // 2,
+            step != middle,
+            step & (step - 1) and 1 + (step < middle),
+            step,
+        )
 
     return sorted(range(1, size), key=rank)
 
@@ -158,25 +164,25 @@
 
 
 def early_kernel(rv, *refs):
-    blocks, (tops, products, vq, vk, vv) = refs[:-5], refs[-5:]
+    blocks, gain_refs, (tops, products, gains, vq, vk, vv, sem) = refs[:-11], refs[-11:-7], refs[-7:]
+    copies = [pltpu.make_async_copy(ref, gains.at[at], sem.at[at]) for at, ref in enumerate(gain_refs)]
+    for copy in copies:
+        copy.start()
     fill_ones(vv)
     for head in range(tops.shape[0]):
         assemble(blocks, pl.ds(head * HEAD_DIM, HEAD_DIM), ((vq, rv), (vk, rv), (vv, rv)))
         top, products[head] = start_attend(vq[...], vk[...], vv[...])
         tops[head] = jnp.broadcast_to(top, tops.shape[1:])
+    for copy in copies:
+        copy.wait()
 
 
 def attention_kernel(size, rv, ra, *refs):
-    blocks, tops, products, gain_refs = refs[:size], refs[size], refs[size + 1], refs[size + 2 : size + 6]
-    outs = refs[size + 6 : 2 * size + 6]
-    vq, vk, vv, aq, ak, av, v_self, a_self, gains, sem = refs[2 * size + 6 :]
+    blocks, tops, products, gains = refs[:size], *refs[size : size + 3]
+    outs = refs[size + 3 : 2 * size + 3]
+    vq, vk, vv, aq, ak, av, v_self, a_self = refs[2 * size + 3 :]
     me = lax.axis_index("seq")
     early, late = pl.ds(0, (size - 1) * rv), pl.ds((size - 1) * rv, rv)
-    copies = [
-        pltpu.make_async_copy(ref, gains.at[at], sem.at[at]) for at, ref in enumerate(gain_refs)
-    ]
-    for copy in copies:
-        copy.start()
     fill_ones(vv, av, v_self, a_self)
     for head in range(tops.shape[0]):
         cols = pl.ds(head * HEAD_DIM, HEAD_DIM)
@@ -189,9 +195,6 @@
         _, product = start_attend(vq[late, :], vk[...], vv[...])
         v_self[late, :HEAD_DIM] = weighed(product).astype(jnp.bfloat16)
         v_result = v_self[:, :HEAD_DIM]
-        if head == 0:
-            for copy in copies:
-                copy.wait()
         vq_gain, vk_gain, aq_gain, ak_gain = [
             gains[at, pl.ds(me * tops.shape[0] + head, 1), :] for at in range(4)
         ]
@@ -233,33 +236,33 @@
         for gain in gains
     ]
     tv, ta, te, heads = rv * size, ra * size, rv * (size - 1), width // HEAD_DIM
-    arrival = order
-    arrived = [blocks[step] for step in arrival]
-    tops, products = pl.pallas_call(
+    arrived = [blocks[step] for step in order]
+    tops, products, gains = pl.pallas_call(
         functools.partial(early_kernel, rv),
         out_shape=[
             jax.ShapeDtypeStruct((heads, te, HEAD_DIM), jnp.float32),
             jax.ShapeDtypeStruct((heads, te, 2 * HEAD_DIM), jnp.float32),
+            jax.ShapeDtypeStruct((4, *gains[0].shape), jnp.float32),
         ],
-        in_specs=[in_vmem] * (size - 1),
-        out_specs=[in_vmem] * 2,
-        scratch_shapes=[pltpu.VMEM((te, parts * HEAD_DIM), jnp.bfloat16) for parts in (1, 1, 2)],
+        in_specs=[in_vmem] * (size - 1) + [in_hbm] * 4,
+        out_specs=[in_vmem] * 3,
+        scratch_shapes=[pltpu.VMEM((te, parts * HEAD_DIM), jnp.bfloat16) for parts in (1, 1, 2)]
+        + [pltpu.SemaphoreType.DMA((4,))],
         compiler_params=pltpu.CompilerParams(vmem_limit_bytes=VMEM_LIMIT),
         cost_estimate=pl.CostEstimate(
             flops=4 * width * te * te, bytes_accessed=8 * te * width, transcendentals=heads * te * te
         ),
         name="early",
-    )(*arrived[:-1])
+    )(*arrived[:-1], *gains)
     results = pl.pallas_call(
         functools.partial(attention_kernel, size, rv, ra),
         out_shape=[jax.ShapeDtypeStruct((rv + ra, width), vq.dtype)] * size,
-        in_specs=[in_vmem] * (size + 2) + [in_hbm] * 4,
+        in_specs=[in_vmem] * (size + 3),
         out_specs=[in_vmem] * size,
         scratch_shapes=[
             pltpu.VMEM((rows, parts * HEAD_DIM), jnp.bfloat16)
             for rows, parts in ((tv, 1), (tv, 1), (tv, 2), (ta, 1), (ta, 1), (ta, 2), (tv, 2), (ta, 2))
-        ]
-        + [pltpu.VMEM((4, columns // HEAD_DIM, HEAD_DIM), jnp.float32), pltpu.SemaphoreType.DMA((4,))],
+        ],
         compiler_params=pltpu.CompilerParams(vmem_limit_bytes=VMEM_LIMIT),
         cost_estimate=pl.CostEstimate(
             flops=4 * width * (2 * tv * rv + ta * ta + 2 * tv * ta),
@@ -267,8 +270,8 @@
             transcendentals=heads * (2 * tv * rv + ta * ta + 2 * tv * ta),
         ),
         name="attention",
-    )(*arrived, tops, products, *gains)
-    results = dict(zip(arrival, results))
+    )(*arrived, tops, products, gains)
+    results = dict(zip(order, results))
     inverse = [[(b, a) for a, b in move] for move in moves]
     back = [results[0], *exchange(results, inverse, return_order(size)).values()]
     return tuple(

time: 46 us -> 45.3 us (0.985)
  starting transfers between devices: 31.9 us -> 28.6 us
  waiting for transfers between devices: 5.84 us -> 8.84 us
    ppermute x14, starting transfers between devices: 31.9 us -> 28.6 us  [exchange(): lax.ppermute(blocks[step], 'seq', moves[step])]
    ppermute x14, waiting for transfers between devices: 5.84 us -> 8.84 us  [exchange(): lax.ppermute(blocks[step], 'seq', moves[step])]
  transfers between devices with their start and end apart: 14 -> 14, of which waited for: 6 -> 8; matrix products, arithmetic and copies ran while one was open for 0% -> 0% of each run, Pallas kernels for 4% -> 5%
where the time goes in v5:
time: 45.3 us; the launch traced here: 45.1 us
  starting transfers between devices  28.6 us (63%)
  waiting for transfers between devices  8.84 us (20%)
  Pallas kernels  6.93 us (15%)
  between operations  0.67 us (1%)
    ppermute x14, starting transfers between devices, exchange(): lax.ppermute(blocks[step], 'seq', moves[step])  28.6 us
    ppermute x14, waiting for transfers between devices, exchange(): lax.ppermute(blocks[step], 'seq', moves[step])  8.84 us
    pallas_call x1, Pallas kernels, head_plan(): pl.pallas_call(functools.partial(attention_kernel, size, rv, ra), out_sha...  2.41 us
    pallas_call x1, Pallas kernels, head_plan(): pl.pallas_call(functools.partial(early_kernel, rv), out_shape=[jax.ShapeD...  2.06 us
    pallas_call x1, Pallas kernels, head_plan(): pl.pallas_call(functools.partial(pack_kernel, size, order), out_shape=[ja...  1.66 us
  transfers between devices with their start and end apart: 14, of which 8 were waited for; matrix products, arithmetic and copies ran while one was open for 0% of the time, Pallas kernels for 5%

profile of v5, /device:TPU:0, one launch (start us, length us, event | category | flops | bytes accessed | tf_op | source)
XLA Modules:
  0.0 45.1 jit_solution(4330693084313504055)
XLA Ops:
  0.6 1.7 %pack.1 = (bf16[480,128]{1,0:T(8,128)(2,1)S(1)}, bf16[480,128]{1,0:T(8,128)(2,1)S(1)}, bf16[480,128]{1,0:T(8,128)(2,1)S(1)}, bf16[480,128]{1,0:T(8,128)(2,1)S(1)...) custom-call(bf16[128,1024]{1,0:T(8,128)(2,1)} %refs_0_.1, ...), custom_call_target="tpu_custom_call" | custom-call | tf_op jit(solution)/shard_map/pack/pallas_call | solution.py:222
  2.3 3.1 %collective-permute-start = (bf16[480,128]{1,0:T(8,128)(2,1)S(1)}, bf16[480,128]{1,0:T(8,128)(2,1)S(1)}, u32[]{:S(2)}, u32[]{:S(2)}) collective-permute-start(bf16[480,128]{1,0:T(8,128)(2,1)S(1)} %get-tuple-element.22), channel_id=1, source_target_pairs={{0,4},{2,6},{4,0},{6,2},{8,12},{10,14},{12,8},{14,10},{1,5},{3,7},... | collective-permute-start | bytes 368648 | tf_op jit(solution)/shard_map/ppermute | solution.py:83
  5.4 2.6 %collective-permute-start.1 = (bf16[480,128]{1,0:T(8,128)(2,1)S(1)}, bf16[480,128]{1,0:T(8,128)(2,1)S(1)}, u32[]{:S(2)}, u32[]{:S(2)}) collective-permute-start(bf16[480,128]{1,0:T(8,128)(2,1)S(1)} %get-tuple-element.23), channel_id=1, source_target_pairs={{0,8},{2,10},{4,12},{6,14},{8,0},{10,2},{12,4},{14,6},{1,9},{3,11}... | collective-permute-start | bytes 368648 | tf_op jit(solution)/shard_map/ppermute | solution.py:83
  8.0 1.5 %collective-permute-start.2 = (bf16[480,128]{1,0:T(8,128)(2,1)S(1)}, bf16[480,128]{1,0:T(8,128)(2,1)S(1)}, u32[]{:S(2)}, u32[]{:S(2)}) collective-permute-start(bf16[480,128]{1,0:T(8,128)(2,1)S(1)} %get-tuple-element.24), channel_id=1, source_target_pairs={{0,2},{2,0},{4,6},{6,4},{8,10},{10,8},{12,14},{14,12},{1,3},{3,1},... | collective-permute-start | bytes 368648 | tf_op jit(solution)/shard_map/ppermute | solution.py:83
  9.5 0.3 collective-permute-start.3
  9.8 2.5 %collective-permute-start.4 = (bf16[480,128]{1,0:T(8,128)(2,1)S(1)}, bf16[480,128]{1,0:T(8,128)(2,1)S(1)}, u32[]{:S(2)}, u32[]{:S(2)}) collective-permute-start(bf16[480,128]{1,0:T(8,128)(2,1)S(1)} %get-tuple-element.26), channel_id=1, source_target_pairs={{0,12},{2,14},{4,8},{6,10},{8,4},{10,6},{12,0},{14,2},{1,13},{3,15... | collective-permute-start | bytes 368648 | tf_op jit(solution)/shard_map/ppermute | solution.py:83
  12.3 1.6 %collective-permute-start.5 = (bf16[480,128]{1,0:T(8,128)(2,1)S(1)}, bf16[480,128]{1,0:T(8,128)(2,1)S(1)}, u32[]{:S(2)}, u32[]{:S(2)}) collective-permute-start(bf16[480,128]{1,0:T(8,128)(2,1)S(1)} %get-tuple-element.27), channel_id=1, source_target_pairs={{0,6},{2,4},{4,2},{6,0},{8,14},{10,12},{12,10},{14,8},{1,7},{3,5},... | collective-permute-start | bytes 368648 | tf_op jit(solution)/shard_map/ppermute | solution.py:83
  13.9 4.7 %collective-permute-done.1.refs_2_ = bf16[480,128]{1,0:T(8,128)(2,1)S(1)} collective-permute-done((bf16[480,128]{1,0:T(8,128)(2,1)S(1)}, bf16[480,128]{1,0:T(8,128)(2,1)S(1)}, u32[]{:S(2)}, u32[]{:S(2)}) %collective-permute-start.1) | collective-permute-done | bytes 122912 | tf_op jit(solution)/shard_map/ppermute | solution.py:83
  18.6 5.2 %collective-permute-start.6 = (bf16[480,128]{1,0:T(8,128)(2,1)S(1)}, bf16[480,128]{1,0:T(8,128)(2,1)S(1)}, u32[]{:S(2)}, u32[]{:S(2)}) collective-permute-start(bf16[480,128]{1,0:T(8,128)(2,1)S(1)} %get-tuple-element.28), channel_id=1, source_target_pairs={{0,14},{2,12},{4,10},{6,8},{8,6},{10,4},{12,2},{14,0},{1,15},{3,13... | collective-permute-start | bytes 368648 | tf_op jit(solution)/shard_map/ppermute | solution.py:83
  23.8 0.4 collective-permute-done.3.refs_4_
  24.2 0.2 collective-permute-done.5.refs_6_
  24.4 2.1 %early.1 = (f32[1,896,128]{2,1,0:T(8,128)S(1)}, f32[1,896,256]{2,1,0:T(8,128)S(1)}, f32[4,8,128]{2,1,0:T(8,128)S(1)}) custom-call(bf16[480,128]{1,0:T(8,128)(2,1)S(1)} %get-tuple-element.21.refs_0_, bf16[480,128]{1,0:T(8,128)(2,1)S(1)} %collective-permute-done.refs_1_, bf16[480,128]{1,0:T(8,128)(2,1)S(1)} %collective-permute-done.1.refs_2_, ...), custom_call_target="tpu_custom_call" | custom-call | flops 411041792 | bytes 917504 | tf_op jit(solution)/shard_map/early/pallas_call | solution.py:240
  26.5 0.3 collective-permute-done.6.refs_7_
  26.7 2.4 %attention.1 = (bf16[160,128]{1,0:T(8,128)(2,1)S(1)}, bf16[160,128]{1,0:T(8,128)(2,1)S(1)}, bf16[160,128]{1,0:T(8,128)(2,1)S(1)}, bf16[160,128]{1,0:T(8,128)(2,1...) custom-call(bf16[480,128]{1,0:T(8,128)(2,1)S(1)} %get-tuple-element., ...), custom_call_target="tpu_custom_call" | custom-call | flops 436207616 | bytes 1048576 | tf_op jit(solution)/shard_map/attention/pallas_call | solution.py:257
  29.1 4.8 %collective-permute-start.7 = (bf16[160,128]{1,0:T(8,128)(2,1)S(1)}, bf16[160,128]{1,0:T(8,128)(2,1)S(1)}, u32[]{:S(2)}, u32[]{:S(2)}) collective-permute-start(bf16[160,128]{1,0:T(8,128)(2,1)S(1)} %get-tuple-element.33), channel_id=1, source_target_pairs={{14,0},{12,2},{10,4},{8,6},{6,8},{4,10},{2,12},{0,14},{15,1},{13,3... | collective-permute-start | bytes 122888 | tf_op jit(solution)/shard_map/ppermute | solution.py:83
  33.9 3.6 %collective-permute-start.9 = (bf16[160,128]{1,0:T(8,128)(2,1)S(1)}, bf16[160,128]{1,0:T(8,128)(2,1)S(1)}, u32[]{:S(2)}, u32[]{:S(2)}) collective-permute-start(bf16[160,128]{1,0:T(8,128)(2,1)S(1)} %get-tuple-element.35), channel_id=1, source_target_pairs={{10,0},{8,2},{14,4},{12,6},{2,8},{0,10},{6,12},{4,14},{11,1},{9,3}... | collective-permute-start | bytes 122888 | tf_op jit(solution)/shard_map/ppermute | solution.py:83
  37.5 2.1 %collective-permute-start.11 = (bf16[160,128]{1,0:T(8,128)(2,1)S(1)}, bf16[160,128]{1,0:T(8,128)(2,1)S(1)}, u32[]{:S(2)}, u32[]{:S(2)}) collective-permute-start(bf16[160,128]{1,0:T(8,128)(2,1)S(1)} %get-tuple-element.37), channel_id=1, source_target_pairs={{6,0},{4,2},{2,4},{0,6},{14,8},{12,10},{10,12},{8,14},{7,1},{5,3},... | collective-permute-start | bytes 122888 | tf_op jit(solution)/shard_map/ppermute | solution.py:83
  39.7 0.6 %collective-permute-start.12 = (bf16[160,128]{1,0:T(8,128)(2,1)S(1)}, bf16[160,128]{1,0:T(8,128)(2,1)S(1)}, u32[]{:S(2)}, u32[]{:S(2)}) collective-permute-start(bf16[160,128]{1,0:T(8,128)(2,1)S(1)} %get-tuple-element.38), channel_id=1, source_target_pairs={{4,0},{6,2},{0,4},{2,6},{12,8},{14,10},{8,12},{10,14},{5,1},{7,3},... | collective-permute-start | bytes 122888 | tf_op jit(solution)/shard_map/ppermute | solution.py:83
  40.2 0.8 %collective-permute-start.13 = (bf16[160,128]{1,0:T(8,128)(2,1)S(1)}, bf16[160,128]{1,0:T(8,128)(2,1)S(1)}, u32[]{:S(2)}, u32[]{:S(2)}) collective-permute-start(bf16[160,128]{1,0:T(8,128)(2,1)S(1)} %get-tuple-element.39), channel_id=1, source_target_pairs={{2,0},{0,2},{6,4},{4,6},{10,8},{8,10},{14,12},{12,14},{3,1},{1,3},... | collective-permute-start | bytes 122888 | tf_op jit(solution)/shard_map/ppermute | solution.py:83
  41.0 0.8 %collective-permute-done.9.refs_3_ = bf16[160,128]{1,0:T(8,128)(2,1)S(1)} collective-permute-done((bf16[160,128]{1,0:T(8,128)(2,1)S(1)}, bf16[160,128]{1,0:T(8,128)(2,1)S(1)}, u32[]{:S(2)}, u32[]{:S(2)}) %collective-permute-start.9) | collective-permute-done | bytes 40992 | tf_op jit(solution)/shard_map/ppermute | solution.py:83
  41.8 1.0 %collective-permute-done.10.refs_4_ = bf16[160,128]{1,0:T(8,128)(2,1)S(1)} collective-permute-done((bf16[160,128]{1,0:T(8,128)(2,1)S(1)}, bf16[160,128]{1,0:T(8,128)(2,1)S(1)}, u32[]{:S(2)}, u32[]{:S(2)}) %collective-permute-start.10) | collective-permute-done | bytes 40992 | tf_op jit(solution)/shard_map/ppermute | solution.py:83
  42.9 0.8 %collective-permute-done.12.refs_6_ = bf16[160,128]{1,0:T(8,128)(2,1)S(1)} collective-permute-done((bf16[160,128]{1,0:T(8,128)(2,1)S(1)}, bf16[160,128]{1,0:T(8,128)(2,1)S(1)}, u32[]{:S(2)}, u32[]{:S(2)}) %collective-permute-start.12) | collective-permute-done | bytes 40992 | tf_op jit(solution)/shard_map/ppermute | solution.py:83
  43.7 0.6 %collective-permute-done.13.refs_7_ = bf16[160,128]{1,0:T(8,128)(2,1)S(1)} collective-permute-done((bf16[160,128]{1,0:T(8,128)(2,1)S(1)}, bf16[160,128]{1,0:T(8,128)(2,1)S(1)}, u32[]{:S(2)}, u32[]{:S(2)}) %collective-permute-start.13) | collective-permute-done | bytes 40992 | tf_op jit(solution)/shard_map/ppermute | solution.py:83
  44.2 0.8 %unpack.1 = (bf16[128,1024]{1,0:T(8,128)(2,1)}, bf16[32,1024]{1,0:T(8,128)(2,1)}) custom-call(bf16[160,128]{1,0:T(8,128)(2,1)S(1)} %get-tuple-element.32.refs_0_, bf16[160,128]{1,0:T(8,128)(2,1)S(1)} %collective-permute-done.7.refs_1_, bf16[160,128]{1,0:T(8,128)(2,1)S(1)} %collective-permute-done.8.refs_2_, ...), custom_call_target="tpu_custom_call" | custom-call | tf_op jit(solution)/shard_map/unpack/pallas_call | solution.py:278
  (8 shorter events, 0.0 us)
Async XLA Ops:
  2.3 10.0 %collective-permute-start = (bf16[480,128]{1,0:T(8,128)(2,1)S(1)}, bf16[480,128]{1,0:T(8,128)(2,1)S(1)}, u32[]{:S(2)}, u32[]{:S(2)}) collective-permute-start(bf16[480,128]{1,0:T(8,128)(2,1)S(1)} %get-tuple-element.22), channel_id=1, source_target_pairs={{0,4},{2,6},{4,0},{6,2},{8,12},{10,14},{12,8},{14,10},{1,5},{3,7},... | collective-permute-start | bytes 368648 | tf_op jit(solution)/shard_map/ppermute | solution.py:83
  5.4 13.2 %collective-permute-start.1 = (bf16[480,128]{1,0:T(8,128)(2,1)S(1)}, bf16[480,128]{1,0:T(8,128)(2,1)S(1)}, u32[]{:S(2)}, u32[]{:S(2)}) collective-permute-start(bf16[480,128]{1,0:T(8,128)(2,1)S(1)} %get-tuple-element.23), channel_id=1, source_target_pairs={{0,8},{2,10},{4,12},{6,14},{8,0},{10,2},{12,4},{14,6},{1,9},{3,11}... | collective-permute-start | bytes 368648 | tf_op jit(solution)/shard_map/ppermute | solution.py:83
  8.0 15.8 %collective-permute-start.2 = (bf16[480,128]{1,0:T(8,128)(2,1)S(1)}, bf16[480,128]{1,0:T(8,128)(2,1)S(1)}, u32[]{:S(2)}, u32[]{:S(2)}) collective-permute-start(bf16[480,128]{1,0:T(8,128)(2,1)S(1)} %get-tuple-element.24), channel_id=1, source_target_pairs={{0,2},{2,0},{4,6},{6,4},{8,10},{10,8},{12,14},{14,12},{1,3},{3,1},... | collective-permute-start | bytes 368648 | tf_op jit(solution)/shard_map/ppermute | solution.py:83
  9.5 14.7 %collective-permute-start.3 = (bf16[480,128]{1,0:T(8,128)(2,1)S(1)}, bf16[480,128]{1,0:T(8,128)(2,1)S(1)}, u32[]{:S(2)}, u32[]{:S(2)}) collective-permute-start(bf16[480,128]{1,0:T(8,128)(2,1)S(1)} %get-tuple-element.25), channel_id=1, source_target_pairs={{0,10},{2,8},{4,14},{6,12},{8,2},{10,0},{12,6},{14,4},{1,11},{3,9}... | collective-permute-start | bytes 368648 | tf_op jit(solution)/shard_map/ppermute | solution.py:83
  9.8 14.4 %collective-permute-start.4 = (bf16[480,128]{1,0:T(8,128)(2,1)S(1)}, bf16[480,128]{1,0:T(8,128)(2,1)S(1)}, u32[]{:S(2)}, u32[]{:S(2)}) collective-permute-start(bf16[480,128]{1,0:T(8,128)(2,1)S(1)} %get-tuple-element.26), channel_id=1, source_target_pairs={{0,12},{2,14},{4,8},{6,10},{8,4},{10,6},{12,0},{14,2},{1,13},{3,15... | collective-permute-start | bytes 368648 | tf_op jit(solution)/shard_map/ppermute | solution.py:83
  12.3 12.2 %collective-permute-start.5 = (bf16[480,128]{1,0:T(8,128)(2,1)S(1)}, bf16[480,128]{1,0:T(8,128)(2,1)S(1)}, u32[]{:S(2)}, u32[]{:S(2)}) collective-permute-start(bf16[480,128]{1,0:T(8,128)(2,1)S(1)} %get-tuple-element.27), channel_id=1, source_target_pairs={{0,6},{2,4},{4,2},{6,0},{8,14},{10,12},{12,10},{14,8},{1,7},{3,5},... | collective-permute-start | bytes 368648 | tf_op jit(solution)/shard_map/ppermute | solution.py:83
  18.6 8.1 %collective-permute-start.6 = (bf16[480,128]{1,0:T(8,128)(2,1)S(1)}, bf16[480,128]{1,0:T(8,128)(2,1)S(1)}, u32[]{:S(2)}, u32[]{:S(2)}) collective-permute-start(bf16[480,128]{1,0:T(8,128)(2,1)S(1)} %get-tuple-element.28), channel_id=1, source_target_pairs={{0,14},{2,12},{4,10},{6,8},{8,6},{10,4},{12,2},{14,0},{1,15},{3,13... | collective-permute-start | bytes 368648 | tf_op jit(solution)/shard_map/ppermute | solution.py:83
  29.1 10.5 %collective-permute-start.7 = (bf16[160,128]{1,0:T(8,128)(2,1)S(1)}, bf16[160,128]{1,0:T(8,128)(2,1)S(1)}, u32[]{:S(2)}, u32[]{:S(2)}) collective-permute-start(bf16[160,128]{1,0:T(8,128)(2,1)S(1)} %get-tuple-element.33), channel_id=1, source_target_pairs={{14,0},{12,2},{10,4},{8,6},{6,8},{4,10},{2,12},{0,14},{15,1},{13,3... | collective-permute-start | bytes 122888 | tf_op jit(solution)/shard_map/ppermute | solution.py:83
  33.9 6.3 %collective-permute-start.8 = (bf16[160,128]{1,0:T(8,128)(2,1)S(1)}, bf16[160,128]{1,0:T(8,128)(2,1)S(1)}, u32[]{:S(2)}, u32[]{:S(2)}) collective-permute-start(bf16[160,128]{1,0:T(8,128)(2,1)S(1)} %get-tuple-element.34), channel_id=1, source_target_pairs={{12,0},{14,2},{8,4},{10,6},{4,8},{6,10},{0,12},{2,14},{13,1},{15,3... | collective-permute-start | bytes 122888 | tf_op jit(solution)/shard_map/ppermute | solution.py:83
  33.9 7.9 %collective-permute-start.9 = (bf16[160,128]{1,0:T(8,128)(2,1)S(1)}, bf16[160,128]{1,0:T(8,128)(2,1)S(1)}, u32[]{:S(2)}, u32[]{:S(2)}) collective-permute-start(bf16[160,128]{1,0:T(8,128)(2,1)S(1)} %get-tuple-element.35), channel_id=1, source_target_pairs={{10,0},{8,2},{14,4},{12,6},{2,8},{0,10},{6,12},{4,14},{11,1},{9,3}... | collective-permute-start | bytes 122888 | tf_op jit(solution)/shard_map/ppermute | solution.py:83
  37.5 5.3 %collective-permute-start.10 = (bf16[160,128]{1,0:T(8,128)(2,1)S(1)}, bf16[160,128]{1,0:T(8,128)(2,1)S(1)}, u32[]{:S(2)}, u32[]{:S(2)}) collective-permute-start(bf16[160,128]{1,0:T(8,128)(2,1)S(1)} %get-tuple-element.36), channel_id=1, source_target_pairs={{8,0},{10,2},{12,4},{14,6},{0,8},{2,10},{4,12},{6,14},{9,1},{11,3}... | collective-permute-start | bytes 122888 | tf_op jit(solution)/shard_map/ppermute | solution.py:83
  37.5 5.3 %collective-permute-start.11 = (bf16[160,128]{1,0:T(8,128)(2,1)S(1)}, bf16[160,128]{1,0:T(8,128)(2,1)S(1)}, u32[]{:S(2)}, u32[]{:S(2)}) collective-permute-start(bf16[160,128]{1,0:T(8,128)(2,1)S(1)} %get-tuple-element.37), channel_id=1, source_target_pairs={{6,0},{4,2},{2,4},{0,6},{14,8},{12,10},{10,12},{8,14},{7,1},{5,3},... | collective-permute-start | bytes 122888 | tf_op jit(solution)/shard_map/ppermute | solution.py:83
  39.7 4.0 %collective-permute-start.12 = (bf16[160,128]{1,0:T(8,128)(2,1)S(1)}, bf16[160,128]{1,0:T(8,128)(2,1)S(1)}, u32[]{:S(2)}, u32[]{:S(2)}) collective-permute-start(bf16[160,128]{1,0:T(8,128)(2,1)S(1)} %get-tuple-element.38), channel_id=1, source_target_pairs={{4,0},{6,2},{0,4},{2,6},{12,8},{14,10},{8,12},{10,14},{5,1},{7,3},... | collective-permute-start | bytes 122888 | tf_op jit(solution)/shard_map/ppermute | solution.py:83
  40.2 4.0 %collective-permute-start.13 = (bf16[160,128]{1,0:T(8,128)(2,1)S(1)}, bf16[160,128]{1,0:T(8,128)(2,1)S(1)}, u32[]{:S(2)}, u32[]{:S(2)}) collective-permute-start(bf16[160,128]{1,0:T(8,128)(2,1)S(1)} %get-tuple-element.39), channel_id=1, source_target_pairs={{2,0},{0,2},{6,4},{4,6},{10,8},{8,10},{14,12},{12,14},{3,1},{1,3},... | collective-permute-start | bytes 122888 | tf_op jit(solution)/shard_map/ppermute | solution.py:83

commit v6 on v5

--- a/solution.py
+++ b/solution.py
@@ -133,11 +133,18 @@
     return top, times(jnp.exp2((scores - top) * SCALE_LOG2), values_and_ones)
 
 
+def across(column, width):
+    if column.shape[1] == 1:
+        return jnp.broadcast_to(column, (column.shape[0], width))
+    return jnp.concatenate([column] * pl.cdiv(width, column.shape[1]), axis=1)[:, :width]
+
+
 def more_attend(top, product, queries, key_rows, values_and_ones):
     scores = dot_t(queries, key_rows)
-    new_top = jnp.maximum(top, jnp.max(scores, axis=1, keepdims=True))
-    product = product * jnp.exp2((top - new_top) * SCALE_LOG2)
-    return product + times(jnp.exp2((scores - new_top) * SCALE_LOG2), values_and_ones)
+    new_top = jnp.maximum(top, across(jnp.max(scores, axis=1, keepdims=True), top.shape[1]))
+    weights = jnp.exp2((scores - across(new_top, scores.shape[1])) * SCALE_LOG2)
+    product = product * across(jnp.exp2((top - new_top) * SCALE_LOG2), product.shape[1])
+    return product + times(weights, values_and_ones)
 
 
 def cross_attend(queries, key_rows, values_and_ones):
@@ -190,7 +197,7 @@
         _, product = start_attend(aq[...], ak[...], av[...])
         a_result = weighed(product).astype(jnp.bfloat16)
         a_self[:, :HEAD_DIM] = a_result
-        product = more_attend(tops[head, :, :1], products[head], vq[early, :], vk[late, :], vv[late, :])
+        product = more_attend(tops[head], products[head], vq[early, :], vk[late, :], vv[late, :])
         v_self[early, :HEAD_DIM] = weighed(product).astype(jnp.bfloat16)
         _, product = start_attend(vq[late, :], vk[...], vv[...])
         v_self[late, :HEAD_DIM] = weighed(product).astype(jnp.bfloat16)

time: 45.3 us -> 44.7 us (0.987)
  Pallas kernels: 6.93 us -> 6.36 us
    pallas_call x1, Pallas kernels: 2.41 us -> 1.84 us  [head_plan(): pl.pallas_call(functools.partial(attention_kernel, size, rv, ra), out_sha...]
where the time goes in v6:
time: 44.7 us; the launch traced here: 44.5 us
  starting transfers between devices  28.6 us (64%)
  waiting for transfers between devices  8.84 us (20%)
  Pallas kernels  6.36 us (14%)
  between operations  0.67 us (1%)
    ppermute x14, starting transfers between devices, exchange(): lax.ppermute(blocks[step], 'seq', moves[step])  28.6 us
    ppermute x14, waiting for transfers between devices, exchange(): lax.ppermute(blocks[step], 'seq', moves[step])  8.84 us
    pallas_call x1, Pallas kernels, head_plan(): pl.pallas_call(functools.partial(early_kernel, rv), out_shape=[jax.ShapeD...  2.06 us
    pallas_call x1, Pallas kernels, head_plan(): pl.pallas_call(functools.partial(attention_kernel, size, rv, ra), out_sha...  1.84 us
    pallas_call x1, Pallas kernels, head_plan(): pl.pallas_call(functools.partial(pack_kernel, size, order), out_shape=[ja...  1.66 us
  transfers between devices with their start and end apart: 14, of which 8 were waited for; matrix products, arithmetic and copies ran while one was open for 0% of the time, Pallas kernels for 5%

profile of v6, /device:TPU:0, one launch (start us, length us, event | category | flops | bytes accessed | tf_op | source)
XLA Modules:
  0.0 44.5 jit_solution(1926277302980354479)
XLA Ops:
  0.6 1.7 %pack.1 = (bf16[480,128]{1,0:T(8,128)(2,1)S(1)}, bf16[480,128]{1,0:T(8,128)(2,1)S(1)}, bf16[480,128]{1,0:T(8,128)(2,1)S(1)}, bf16[480,128]{1,0:T(8,128)(2,1)S(1)...) custom-call(bf16[128,1024]{1,0:T(8,128)(2,1)} %refs_0_.1, ...), custom_call_target="tpu_custom_call" | custom-call | tf_op jit(solution)/shard_map/pack/pallas_call | solution.py:229
  2.3 3.1 %collective-permute-start = (bf16[480,128]{1,0:T(8,128)(2,1)S(1)}, bf16[480,128]{1,0:T(8,128)(2,1)S(1)}, u32[]{:S(2)}, u32[]{:S(2)}) collective-permute-start(bf16[480,128]{1,0:T(8,128)(2,1)S(1)} %get-tuple-element.22), channel_id=1, source_target_pairs={{0,4},{2,6},{4,0},{6,2},{8,12},{10,14},{12,8},{14,10},{1,5},{3,7},... | collective-permute-start | bytes 368648 | tf_op jit(solution)/shard_map/ppermute | solution.py:83
  5.4 2.6 %collective-permute-start.1 = (bf16[480,128]{1,0:T(8,128)(2,1)S(1)}, bf16[480,128]{1,0:T(8,128)(2,1)S(1)}, u32[]{:S(2)}, u32[]{:S(2)}) collective-permute-start(bf16[480,128]{1,0:T(8,128)(2,1)S(1)} %get-tuple-element.23), channel_id=1, source_target_pairs={{0,8},{2,10},{4,12},{6,14},{8,0},{10,2},{12,4},{14,6},{1,9},{3,11}... | collective-permute-start | bytes 368648 | tf_op jit(solution)/shard_map/ppermute | solution.py:83
  8.0 1.5 %collective-permute-start.2 = (bf16[480,128]{1,0:T(8,128)(2,1)S(1)}, bf16[480,128]{1,0:T(8,128)(2,1)S(1)}, u32[]{:S(2)}, u32[]{:S(2)}) collective-permute-start(bf16[480,128]{1,0:T(8,128)(2,1)S(1)} %get-tuple-element.24), channel_id=1, source_target_pairs={{0,2},{2,0},{4,6},{6,4},{8,10},{10,8},{12,14},{14,12},{1,3},{3,1},... | collective-permute-start | bytes 368648 | tf_op jit(solution)/shard_map/ppermute | solution.py:83
  9.5 0.3 collective-permute-start.3
  9.8 2.5 %collective-permute-start.4 = (bf16[480,128]{1,0:T(8,128)(2,1)S(1)}, bf16[480,128]{1,0:T(8,128)(2,1)S(1)}, u32[]{:S(2)}, u32[]{:S(2)}) collective-permute-start(bf16[480,128]{1,0:T(8,128)(2,1)S(1)} %get-tuple-element.26), channel_id=1, source_target_pairs={{0,12},{2,14},{4,8},{6,10},{8,4},{10,6},{12,0},{14,2},{1,13},{3,15... | collective-permute-start | bytes 368648 | tf_op jit(solution)/shard_map/ppermute | solution.py:83
  12.3 1.6 %collective-permute-start.5 = (bf16[480,128]{1,0:T(8,128)(2,1)S(1)}, bf16[480,128]{1,0:T(8,128)(2,1)S(1)}, u32[]{:S(2)}, u32[]{:S(2)}) collective-permute-start(bf16[480,128]{1,0:T(8,128)(2,1)S(1)} %get-tuple-element.27), channel_id=1, source_target_pairs={{0,6},{2,4},{4,2},{6,0},{8,14},{10,12},{12,10},{14,8},{1,7},{3,5},... | collective-permute-start | bytes 368648 | tf_op jit(solution)/shard_map/ppermute | solution.py:83
  13.9 4.7 %collective-permute-done.1.refs_2_ = bf16[480,128]{1,0:T(8,128)(2,1)S(1)} collective-permute-done((bf16[480,128]{1,0:T(8,128)(2,1)S(1)}, bf16[480,128]{1,0:T(8,128)(2,1)S(1)}, u32[]{:S(2)}, u32[]{:S(2)}) %collective-permute-start.1) | collective-permute-done | bytes 122912 | tf_op jit(solution)/shard_map/ppermute | solution.py:83
  18.6 5.2 %collective-permute-start.6 = (bf16[480,128]{1,0:T(8,128)(2,1)S(1)}, bf16[480,128]{1,0:T(8,128)(2,1)S(1)}, u32[]{:S(2)}, u32[]{:S(2)}) collective-permute-start(bf16[480,128]{1,0:T(8,128)(2,1)S(1)} %get-tuple-element.28), channel_id=1, source_target_pairs={{0,14},{2,12},{4,10},{6,8},{8,6},{10,4},{12,2},{14,0},{1,15},{3,13... | collective-permute-start | bytes 368648 | tf_op jit(solution)/shard_map/ppermute | solution.py:83
  23.8 0.4 collective-permute-done.3.refs_4_
  24.2 0.2 collective-permute-done.5.refs_6_
  24.4 2.1 %early.1 = (f32[1,896,128]{2,1,0:T(8,128)S(1)}, f32[1,896,256]{2,1,0:T(8,128)S(1)}, f32[4,8,128]{2,1,0:T(8,128)S(1)}) custom-call(bf16[480,128]{1,0:T(8,128)(2,1)S(1)} %get-tuple-element.21.refs_0_, bf16[480,128]{1,0:T(8,128)(2,1)S(1)} %collective-permute-done.refs_1_, bf16[480,128]{1,0:T(8,128)(2,1)S(1)} %collective-permute-done.1.refs_2_, ...), custom_call_target="tpu_custom_call" | custom-call | flops 411041792 | bytes 917504 | tf_op jit(solution)/shard_map/early/pallas_call | solution.py:247
  26.5 0.3 collective-permute-done.6.refs_7_
  26.7 1.8 %attention.1 = (bf16[160,128]{1,0:T(8,128)(2,1)S(1)}, bf16[160,128]{1,0:T(8,128)(2,1)S(1)}, bf16[160,128]{1,0:T(8,128)(2,1)S(1)}, bf16[160,128]{1,0:T(8,128)(2,1...) custom-call(bf16[480,128]{1,0:T(8,128)(2,1)S(1)} %get-tuple-element., ...), custom_call_target="tpu_custom_call" | custom-call | flops 436207616 | bytes 1048576 | tf_op jit(solution)/shard_map/attention/pallas_call | solution.py:264
  28.6 4.8 %collective-permute-start.7 = (bf16[160,128]{1,0:T(8,128)(2,1)S(1)}, bf16[160,128]{1,0:T(8,128)(2,1)S(1)}, u32[]{:S(2)}, u32[]{:S(2)}) collective-permute-start(bf16[160,128]{1,0:T(8,128)(2,1)S(1)} %get-tuple-element.33), channel_id=1, source_target_pairs={{14,0},{12,2},{10,4},{8,6},{6,8},{4,10},{2,12},{0,14},{15,1},{13,3... | collective-permute-start | bytes 122888 | tf_op jit(solution)/shard_map/ppermute | solution.py:83
  33.4 3.6 %collective-permute-start.9 = (bf16[160,128]{1,0:T(8,128)(2,1)S(1)}, bf16[160,128]{1,0:T(8,128)(2,1)S(1)}, u32[]{:S(2)}, u32[]{:S(2)}) collective-permute-start(bf16[160,128]{1,0:T(8,128)(2,1)S(1)} %get-tuple-element.35), channel_id=1, source_target_pairs={{10,0},{8,2},{14,4},{12,6},{2,8},{0,10},{6,12},{4,14},{11,1},{9,3}... | collective-permute-start | bytes 122888 | tf_op jit(solution)/shard_map/ppermute | solution.py:83
  37.0 2.1 %collective-permute-start.11 = (bf16[160,128]{1,0:T(8,128)(2,1)S(1)}, bf16[160,128]{1,0:T(8,128)(2,1)S(1)}, u32[]{:S(2)}, u32[]{:S(2)}) collective-permute-start(bf16[160,128]{1,0:T(8,128)(2,1)S(1)} %get-tuple-element.37), channel_id=1, source_target_pairs={{6,0},{4,2},{2,4},{0,6},{14,8},{12,10},{10,12},{8,14},{7,1},{5,3},... | collective-permute-start | bytes 122888 | tf_op jit(solution)/shard_map/ppermute | solution.py:83
  39.1 0.6 %collective-permute-start.12 = (bf16[160,128]{1,0:T(8,128)(2,1)S(1)}, bf16[160,128]{1,0:T(8,128)(2,1)S(1)}, u32[]{:S(2)}, u32[]{:S(2)}) collective-permute-start(bf16[160,128]{1,0:T(8,128)(2,1)S(1)} %get-tuple-element.38), channel_id=1, source_target_pairs={{4,0},{6,2},{0,4},{2,6},{12,8},{14,10},{8,12},{10,14},{5,1},{7,3},... | collective-permute-start | bytes 122888 | tf_op jit(solution)/shard_map/ppermute | solution.py:83
  39.7 0.8 %collective-permute-start.13 = (bf16[160,128]{1,0:T(8,128)(2,1)S(1)}, bf16[160,128]{1,0:T(8,128)(2,1)S(1)}, u32[]{:S(2)}, u32[]{:S(2)}) collective-permute-start(bf16[160,128]{1,0:T(8,128)(2,1)S(1)} %get-tuple-element.39), channel_id=1, source_target_pairs={{2,0},{0,2},{6,4},{4,6},{10,8},{8,10},{14,12},{12,14},{3,1},{1,3},... | collective-permute-start | bytes 122888 | tf_op jit(solution)/shard_map/ppermute | solution.py:83
  40.5 0.8 %collective-permute-done.9.refs_3_ = bf16[160,128]{1,0:T(8,128)(2,1)S(1)} collective-permute-done((bf16[160,128]{1,0:T(8,128)(2,1)S(1)}, bf16[160,128]{1,0:T(8,128)(2,1)S(1)}, u32[]{:S(2)}, u32[]{:S(2)}) %collective-permute-start.9) | collective-permute-done | bytes 40992 | tf_op jit(solution)/shard_map/ppermute | solution.py:83
  41.3 1.0 %collective-permute-done.10.refs_4_ = bf16[160,128]{1,0:T(8,128)(2,1)S(1)} collective-permute-done((bf16[160,128]{1,0:T(8,128)(2,1)S(1)}, bf16[160,128]{1,0:T(8,128)(2,1)S(1)}, u32[]{:S(2)}, u32[]{:S(2)}) %collective-permute-start.10) | collective-permute-done | bytes 40992 | tf_op jit(solution)/shard_map/ppermute | solution.py:83
  42.3 0.8 %collective-permute-done.12.refs_6_ = bf16[160,128]{1,0:T(8,128)(2,1)S(1)} collective-permute-done((bf16[160,128]{1,0:T(8,128)(2,1)S(1)}, bf16[160,128]{1,0:T(8,128)(2,1)S(1)}, u32[]{:S(2)}, u32[]{:S(2)}) %collective-permute-start.12) | collective-permute-done | bytes 40992 | tf_op jit(solution)/shard_map/ppermute | solution.py:83
  43.1 0.6 %collective-permute-done.13.refs_7_ = bf16[160,128]{1,0:T(8,128)(2,1)S(1)} collective-permute-done((bf16[160,128]{1,0:T(8,128)(2,1)S(1)}, bf16[160,128]{1,0:T(8,128)(2,1)S(1)}, u32[]{:S(2)}, u32[]{:S(2)}) %collective-permute-start.13) | collective-permute-done | bytes 40992 | tf_op jit(solution)/shard_map/ppermute | solution.py:83
  43.7 0.8 %unpack.1 = (bf16[128,1024]{1,0:T(8,128)(2,1)}, bf16[32,1024]{1,0:T(8,128)(2,1)}) custom-call(bf16[160,128]{1,0:T(8,128)(2,1)S(1)} %get-tuple-element.32.refs_0_, bf16[160,128]{1,0:T(8,128)(2,1)S(1)} %collective-permute-done.7.refs_1_, bf16[160,128]{1,0:T(8,128)(2,1)S(1)} %collective-permute-done.8.refs_2_, ...), custom_call_target="tpu_custom_call" | custom-call | tf_op jit(solution)/shard_map/unpack/pallas_call | solution.py:285
  (8 shorter events, 0.0 us)
Async XLA Ops:
  2.3 10.0 %collective-permute-start = (bf16[480,128]{1,0:T(8,128)(2,1)S(1)}, bf16[480,128]{1,0:T(8,128)(2,1)S(1)}, u32[]{:S(2)}, u32[]{:S(2)}) collective-permute-start(bf16[480,128]{1,0:T(8,128)(2,1)S(1)} %get-tuple-element.22), channel_id=1, source_target_pairs={{0,4},{2,6},{4,0},{6,2},{8,12},{10,14},{12,8},{14,10},{1,5},{3,7},... | collective-permute-start | bytes 368648 | tf_op jit(solution)/shard_map/ppermute | solution.py:83
  5.4 13.2 %collective-permute-start.1 = (bf16[480,128]{1,0:T(8,128)(2,1)S(1)}, bf16[480,128]{1,0:T(8,128)(2,1)S(1)}, u32[]{:S(2)}, u32[]{:S(2)}) collective-permute-start(bf16[480,128]{1,0:T(8,128)(2,1)S(1)} %get-tuple-element.23), channel_id=1, source_target_pairs={{0,8},{2,10},{4,12},{6,14},{8,0},{10,2},{12,4},{14,6},{1,9},{3,11}... | collective-permute-start | bytes 368648 | tf_op jit(solution)/shard_map/ppermute | solution.py:83
  8.0 15.8 %collective-permute-start.2 = (bf16[480,128]{1,0:T(8,128)(2,1)S(1)}, bf16[480,128]{1,0:T(8,128)(2,1)S(1)}, u32[]{:S(2)}, u32[]{:S(2)}) collective-permute-start(bf16[480,128]{1,0:T(8,128)(2,1)S(1)} %get-tuple-element.24), channel_id=1, source_target_pairs={{0,2},{2,0},{4,6},{6,4},{8,10},{10,8},{12,14},{14,12},{1,3},{3,1},... | collective-permute-start | bytes 368648 | tf_op jit(solution)/shard_map/ppermute | solution.py:83
  9.5 14.7 %collective-permute-start.3 = (bf16[480,128]{1,0:T(8,128)(2,1)S(1)}, bf16[480,128]{1,0:T(8,128)(2,1)S(1)}, u32[]{:S(2)}, u32[]{:S(2)}) collective-permute-start(bf16[480,128]{1,0:T(8,128)(2,1)S(1)} %get-tuple-element.25), channel_id=1, source_target_pairs={{0,10},{2,8},{4,14},{6,12},{8,2},{10,0},{12,6},{14,4},{1,11},{3,9}... | collective-permute-start | bytes 368648 | tf_op jit(solution)/shard_map/ppermute | solution.py:83
  9.8 14.4 %collective-permute-start.4 = (bf16[480,128]{1,0:T(8,128)(2,1)S(1)}, bf16[480,128]{1,0:T(8,128)(2,1)S(1)}, u32[]{:S(2)}, u32[]{:S(2)}) collective-permute-start(bf16[480,128]{1,0:T(8,128)(2,1)S(1)} %get-tuple-element.26), channel_id=1, source_target_pairs={{0,12},{2,14},{4,8},{6,10},{8,4},{10,6},{12,0},{14,2},{1,13},{3,15... | collective-permute-start | bytes 368648 | tf_op jit(solution)/shard_map/ppermute | solution.py:83
  12.3 12.2 %collective-permute-start.5 = (bf16[480,128]{1,0:T(8,128)(2,1)S(1)}, bf16[480,128]{1,0:T(8,128)(2,1)S(1)}, u32[]{:S(2)}, u32[]{:S(2)}) collective-permute-start(bf16[480,128]{1,0:T(8,128)(2,1)S(1)} %get-tuple-element.27), channel_id=1, source_target_pairs={{0,6},{2,4},{4,2},{6,0},{8,14},{10,12},{12,10},{14,8},{1,7},{3,5},... | collective-permute-start | bytes 368648 | tf_op jit(solution)/shard_map/ppermute | solution.py:83
  18.6 8.1 %collective-permute-start.6 = (bf16[480,128]{1,0:T(8,128)(2,1)S(1)}, bf16[480,128]{1,0:T(8,128)(2,1)S(1)}, u32[]{:S(2)}, u32[]{:S(2)}) collective-permute-start(bf16[480,128]{1,0:T(8,128)(2,1)S(1)} %get-tuple-element.28), channel_id=1, source_target_pairs={{0,14},{2,12},{4,10},{6,8},{8,6},{10,4},{12,2},{14,0},{1,15},{3,13... | collective-permute-start | bytes 368648 | tf_op jit(solution)/shard_map/ppermute | solution.py:83
  28.6 10.5 %collective-permute-start.7 = (bf16[160,128]{1,0:T(8,128)(2,1)S(1)}, bf16[160,128]{1,0:T(8,128)(2,1)S(1)}, u32[]{:S(2)}, u32[]{:S(2)}) collective-permute-start(bf16[160,128]{1,0:T(8,128)(2,1)S(1)} %get-tuple-element.33), channel_id=1, source_target_pairs={{14,0},{12,2},{10,4},{8,6},{6,8},{4,10},{2,12},{0,14},{15,1},{13,3... | collective-permute-start | bytes 122888 | tf_op jit(solution)/shard_map/ppermute | solution.py:83
  33.4 6.3 %collective-permute-start.8 = (bf16[160,128]{1,0:T(8,128)(2,1)S(1)}, bf16[160,128]{1,0:T(8,128)(2,1)S(1)}, u32[]{:S(2)}, u32[]{:S(2)}) collective-permute-start(bf16[160,128]{1,0:T(8,128)(2,1)S(1)} %get-tuple-element.34), channel_id=1, source_target_pairs={{12,0},{14,2},{8,4},{10,6},{4,8},{6,10},{0,12},{2,14},{13,1},{15,3... | collective-permute-start | bytes 122888 | tf_op jit(solution)/shard_map/ppermute | solution.py:83
  33.4 7.9 %collective-permute-start.9 = (bf16[160,128]{1,0:T(8,128)(2,1)S(1)}, bf16[160,128]{1,0:T(8,128)(2,1)S(1)}, u32[]{:S(2)}, u32[]{:S(2)}) collective-permute-start(bf16[160,128]{1,0:T(8,128)(2,1)S(1)} %get-tuple-element.35), channel_id=1, source_target_pairs={{10,0},{8,2},{14,4},{12,6},{2,8},{0,10},{6,12},{4,14},{11,1},{9,3}... | collective-permute-start | bytes 122888 | tf_op jit(solution)/shard_map/ppermute | solution.py:83
  37.0 5.3 %collective-permute-start.10 = (bf16[160,128]{1,0:T(8,128)(2,1)S(1)}, bf16[160,128]{1,0:T(8,128)(2,1)S(1)}, u32[]{:S(2)}, u32[]{:S(2)}) collective-permute-start(bf16[160,128]{1,0:T(8,128)(2,1)S(1)} %get-tuple-element.36), channel_id=1, source_target_pairs={{8,0},{10,2},{12,4},{14,6},{0,8},{2,10},{4,12},{6,14},{9,1},{11,3}... | collective-permute-start | bytes 122888 | tf_op jit(solution)/shard_map/ppermute | solution.py:83
  37.0 5.3 %collective-permute-start.11 = (bf16[160,128]{1,0:T(8,128)(2,1)S(1)}, bf16[160,128]{1,0:T(8,128)(2,1)S(1)}, u32[]{:S(2)}, u32[]{:S(2)}) collective-permute-start(bf16[160,128]{1,0:T(8,128)(2,1)S(1)} %get-tuple-element.37), channel_id=1, source_target_pairs={{6,0},{4,2},{2,4},{0,6},{14,8},{12,10},{10,12},{8,14},{7,1},{5,3},... | collective-permute-start | bytes 122888 | tf_op jit(solution)/shard_map/ppermute | solution.py:83
  39.1 4.0 %collective-permute-start.12 = (bf16[160,128]{1,0:T(8,128)(2,1)S(1)}, bf16[160,128]{1,0:T(8,128)(2,1)S(1)}, u32[]{:S(2)}, u32[]{:S(2)}) collective-permute-start(bf16[160,128]{1,0:T(8,128)(2,1)S(1)} %get-tuple-element.38), channel_id=1, source_target_pairs={{4,0},{6,2},{0,4},{2,6},{12,8},{14,10},{8,12},{10,14},{5,1},{7,3},... | collective-permute-start | bytes 122888 | tf_op jit(solution)/shard_map/ppermute | solution.py:83
  39.7 4.0 %collective-permute-start.13 = (bf16[160,128]{1,0:T(8,128)(2,1)S(1)}, bf16[160,128]{1,0:T(8,128)(2,1)S(1)}, u32[]{:S(2)}, u32[]{:S(2)}) collective-permute-start(bf16[160,128]{1,0:T(8,128)(2,1)S(1)} %get-tuple-element.39), channel_id=1, source_target_pairs={{2,0},{0,2},{6,4},{4,6},{10,8},{8,10},{14,12},{12,14},{3,1},{1,3},... | collective-permute-start | bytes 122888 | tf_op jit(solution)/shard_map/ppermute | solution.py:83

commit v7 on v6

--- a/solution.py
+++ b/solution.py
@@ -12,6 +12,7 @@
 SCALE = HEAD_DIM ** (-0.5)
 SCALE_LOG2 = SCALE * math.log2(math.e)
 VMEM_LIMIT = 48 * 1024 * 1024
+SOON = 5
 PACK_VMEM = 16 * 1024 * 1024
 
 
@@ -129,8 +130,8 @@
 
 def start_attend(queries, key_rows, values_and_ones):
     scores = dot_t(queries, key_rows)
-    top = jnp.max(scores, axis=1, keepdims=True)
-    return top, times(jnp.exp2((scores - top) * SCALE_LOG2), values_and_ones)
+    top = across(jnp.max(scores, axis=1, keepdims=True), HEAD_DIM)
+    return top, times(jnp.exp2((scores - across(top, scores.shape[1])) * SCALE_LOG2), values_and_ones)
 
 
 def across(column, width):
@@ -179,7 +180,7 @@
     for head in range(tops.shape[0]):
         assemble(blocks, pl.ds(head * HEAD_DIM, HEAD_DIM), ((vq, rv), (vk, rv), (vv, rv)))
         top, products[head] = start_attend(vq[...], vk[...], vv[...])
-        tops[head] = jnp.broadcast_to(top, tops.shape[1:])
+        tops[head] = top
     for copy in copies:
         copy.wait()
 
@@ -226,17 +227,24 @@
 
     arrays = [pltpu.with_memory_space_constraint(x, pltpu.HBM) for x in (vq, vk, vv, aq, ak, av)]
     order = [0, *send_order(size)]
-    sends = pl.pallas_call(
-        functools.partial(pack_kernel, size, order),
-        out_shape=[jax.ShapeDtypeStruct((3 * (rv + ra), width), vq.dtype)] * size,
-        in_specs=[in_hbm] * 6,
-        out_specs=[in_vmem] * size,
-        scratch_shapes=[pltpu.SemaphoreType.DMA((6 * size,))],
-        compiler_params=pltpu.CompilerParams(vmem_limit_bytes=PACK_VMEM),
-        name="pack",
-    )(*arrays)
-    sends = dict(zip(order, sends))
-    blocks = {0: sends[0], **exchange(sends, moves, order[1:])}
+
+    def pack(steps, after=()):
+        return pl.pallas_call(
+            functools.partial(pack_kernel, size, steps),
+            out_shape=[jax.ShapeDtypeStruct((3 * (rv + ra), width), vq.dtype)] * len(steps),
+            in_specs=[in_hbm] * 6 + [pl.BlockSpec(memory_space=pl.ANY)] * len(after),
+            out_specs=[in_vmem] * len(steps),
+            scratch_shapes=[pltpu.SemaphoreType.DMA((6 * len(steps),))],
+            compiler_params=pltpu.CompilerParams(vmem_limit_bytes=PACK_VMEM),
+            name="pack",
+        )(*arrays, *after)
+
+    first, rest = order[1 : 1 + SOON], [0, *order[1 + SOON :]]
+    sends = dict(zip(first, pack(first)))
+    blocks = exchange(sends, moves, first)
+    sends.update(zip(rest, pack(rest, [blocks[first[0]]])))
+    blocks.update(exchange(sends, moves, rest[1:]))
+    blocks[0] = sends[0]
 
     gains = [
         pltpu.with_memory_space_constraint(gain.reshape(columns // HEAD_DIM, HEAD_DIM), pltpu.HBM)

time: 44.7 us -> 44.5 us (level)
  waiting for transfers between devices: 8.84 us -> 8 us
  Pallas kernels: 6.36 us -> 7.19 us
    ppermute x14, waiting for transfers between devices: 8.84 us -> 8 us  [exchange(): lax.ppermute(blocks[step], 'seq', moves[step])]
    pallas_call x1 -> x2, Pallas kernels: 1.66 us -> 2.48 us  [pack(): pl.pallas_call(functools.partial(pack_kernel, size, steps), out_shape=[ja...]
  transfers between devices with their start and end apart: 14 -> 14, of which waited for: 8 -> 7; matrix products, arithmetic and copies ran while one was open for 0% -> 0% of each run, Pallas kernels for 5% -> 7%
where the time goes in v7:
time: 44.5 us; the launch traced here: 44.2 us
  starting transfers between devices  28.3 us (64%)
  waiting for transfers between devices  8 us (18%)
  Pallas kernels  7.19 us (16%)
  between operations  0.68 us (2%)
    ppermute x14, starting transfers between devices, exchange(): lax.ppermute(blocks[step], 'seq', moves[step])  28.3 us
    ppermute x14, waiting for transfers between devices, exchange(): lax.ppermute(blocks[step], 'seq', moves[step])  8 us
    pallas_call x2, Pallas kernels, pack(): pl.pallas_call(functools.partial(pack_kernel, size, steps), out_shape=[ja...  2.48 us
    pallas_call x1, Pallas kernels, head_plan(): pl.pallas_call(functools.partial(early_kernel, rv), out_shape=[jax.ShapeD...  2.06 us
    pallas_call x1, Pallas kernels, head_plan(): pl.pallas_call(functools.partial(attention_kernel, size, rv, ra), out_sha...  1.85 us
  transfers between devices with their start and end apart: 14, of which 7 were waited for; matrix products, arithmetic and copies ran while one was open for 0% of the time, Pallas kernels for 7%

profile of v7, /device:TPU:0, one launch (start us, length us, event | category | flops | bytes accessed | tf_op | source)
XLA Modules:
  0.0 44.2 jit_solution(17314859348852760925)
XLA Ops:
  0.6 1.4 %pack.2 = (bf16[480,128]{1,0:T(8,128)(2,1)S(1)}, bf16[480,128]{1,0:T(8,128)(2,1)S(1)}, bf16[480,128]{1,0:T(8,128)(2,1)S(1)}, bf16[480,128]{1,0:T(8,128)(2,1)S(1)}, bf16[480,128]{1,0:T(8,128)(2,1)S(1)}) custom-call(bf16[128,1024]{1,0:T(8,128)(2,1)} %refs_0_.3, bf16[128,1024]{1,0:T(8,128)(2,1)} %refs_1_.3, bf16[128,1024]{1,0:T(8,128)(2,1)} %refs_2_.3, ...), custom_call_target="tpu_custom_call" | custom-call | tf_op jit(solution)/shard_map/pack/pallas_call | solution.py:232
  2.0 3.1 %collective-permute-start = (bf16[480,128]{1,0:T(8,128)(2,1)S(1)}, bf16[480,128]{1,0:T(8,128)(2,1)S(1)}, u32[]{:S(2)}, u32[]{:S(2)}) collective-permute-start(bf16[480,128]{1,0:T(8,128)(2,1)S(1)} %get-tuple-element.21), channel_id=1, source_target_pairs={{0,4},{2,6},{4,0},{6,2},{8,12},{10,14},{12,8},{14,10},{1,5},{3,7},... | collective-permute-start | bytes 368648 | tf_op jit(solution)/shard_map/ppermute | solution.py:84
  5.1 2.6 %collective-permute-start.1 = (bf16[480,128]{1,0:T(8,128)(2,1)S(1)}, bf16[480,128]{1,0:T(8,128)(2,1)S(1)}, u32[]{:S(2)}, u32[]{:S(2)}) collective-permute-start(bf16[480,128]{1,0:T(8,128)(2,1)S(1)} %get-tuple-element.23), channel_id=1, source_target_pairs={{0,8},{2,10},{4,12},{6,14},{8,0},{10,2},{12,4},{14,6},{1,9},{3,11}... | collective-permute-start | bytes 368648 | tf_op jit(solution)/shard_map/ppermute | solution.py:84
  7.7 1.5 %collective-permute-start.2 = (bf16[480,128]{1,0:T(8,128)(2,1)S(1)}, bf16[480,128]{1,0:T(8,128)(2,1)S(1)}, u32[]{:S(2)}, u32[]{:S(2)}) collective-permute-start(bf16[480,128]{1,0:T(8,128)(2,1)S(1)} %get-tuple-element.24), channel_id=1, source_target_pairs={{0,2},{2,0},{4,6},{6,4},{8,10},{10,8},{12,14},{14,12},{1,3},{3,1},... | collective-permute-start | bytes 368648 | tf_op jit(solution)/shard_map/ppermute | solution.py:84
  9.2 0.3 collective-permute-start.3
  9.5 2.5 %collective-permute-start.4 = (bf16[480,128]{1,0:T(8,128)(2,1)S(1)}, bf16[480,128]{1,0:T(8,128)(2,1)S(1)}, u32[]{:S(2)}, u32[]{:S(2)}) collective-permute-start(bf16[480,128]{1,0:T(8,128)(2,1)S(1)} %get-tuple-element.26), channel_id=1, source_target_pairs={{0,12},{2,14},{4,8},{6,10},{8,4},{10,6},{12,0},{14,2},{1,13},{3,15... | collective-permute-start | bytes 368648 | tf_op jit(solution)/shard_map/ppermute | solution.py:84
  12.0 1.1 %pack.3 = (bf16[480,128]{1,0:T(8,128)(2,1)S(1)}, bf16[480,128]{1,0:T(8,128)(2,1)S(1)}, bf16[480,128]{1,0:T(8,128)(2,1)S(1)}) custom-call(bf16[128,1024]{1,0:T(8,128)(2,1)} %refs_0_.3, bf16[128,1024]{1,0:T(8,128)(2,1)} %refs_1_.3, bf16[128,1024]{1,0:T(8,128)(2,1)} %refs_2_.3, bf16[32,1024]{1,0:T(8,128)(2,1)} %refs_3_.3, bf16[32,1024]{1,0:T(8,128)(2,1)} %refs_4_.3, ...), custom_call_target="tpu_custom_call" | custom-call | tf_op jit(solution)/shard_map/pack/pallas_call | solution.py:232
  13.1 1.7 %collective-permute-start.5 = (bf16[480,128]{1,0:T(8,128)(2,1)S(1)}, bf16[480,128]{1,0:T(8,128)(2,1)S(1)}, u32[]{:S(2)}, u32[]{:S(2)}) collective-permute-start(bf16[480,128]{1,0:T(8,128)(2,1)S(1)} %get-tuple-element.27), channel_id=1, source_target_pairs={{0,6},{2,4},{4,2},{6,0},{8,14},{10,12},{12,10},{14,8},{1,7},{3,5},... | collective-permute-start | bytes 368648 | tf_op jit(solution)/shard_map/ppermute | solution.py:84
  14.8 3.5 %collective-permute-done.1.refs_2_ = bf16[480,128]{1,0:T(8,128)(2,1)S(1)} collective-permute-done((bf16[480,128]{1,0:T(8,128)(2,1)S(1)}, bf16[480,128]{1,0:T(8,128)(2,1)S(1)}, u32[]{:S(2)}, u32[]{:S(2)}) %collective-permute-start.1) | collective-permute-done | bytes 122912 | tf_op jit(solution)/shard_map/ppermute | solution.py:84
  18.3 5.2 %collective-permute-start.6 = (bf16[480,128]{1,0:T(8,128)(2,1)S(1)}, bf16[480,128]{1,0:T(8,128)(2,1)S(1)}, u32[]{:S(2)}, u32[]{:S(2)}) collective-permute-start(bf16[480,128]{1,0:T(8,128)(2,1)S(1)} %get-tuple-element.28), channel_id=1, source_target_pairs={{0,14},{2,12},{4,10},{6,8},{8,6},{10,4},{12,2},{14,0},{1,15},{3,13... | collective-permute-start | bytes 368648 | tf_op jit(solution)/shard_map/ppermute | solution.py:84
  23.5 0.4 collective-permute-done.3.refs_4_
  23.9 0.8 %collective-permute-done.5.refs_6_ = bf16[480,128]{1,0:T(8,128)(2,1)S(1)} collective-permute-done((bf16[480,128]{1,0:T(8,128)(2,1)S(1)}, bf16[480,128]{1,0:T(8,128)(2,1)S(1)}, u32[]{:S(2)}, u32[]{:S(2)}) %collective-permute-start.5) | collective-permute-done | bytes 122912 | tf_op jit(solution)/shard_map/ppermute | solution.py:84
  24.7 2.1 %early.1 = (f32[1,896,128]{2,1,0:T(8,128)S(1)}, f32[1,896,256]{2,1,0:T(8,128)S(1)}, f32[4,8,128]{2,1,0:T(8,128)S(1)}) custom-call(bf16[480,128]{1,0:T(8,128)(2,1)S(1)} %get-tuple-element.22.refs_0_, bf16[480,128]{1,0:T(8,128)(2,1)S(1)} %collective-permute-done.refs_6_.refs_1_, bf16[480,128]{1,0:T(8,128)(2,1)S(1)} %collective-permute-done.1.refs_2_, ...), custom_call_target="tpu_custom_call" | custom-call | flops 411041792 | bytes 917504 | tf_op jit(solution)/shard_map/early/pallas_call | solution.py:255
  26.8 1.9 %attention.1 = (bf16[160,128]{1,0:T(8,128)(2,1)S(1)}, bf16[160,128]{1,0:T(8,128)(2,1)S(1)}, bf16[160,128]{1,0:T(8,128)(2,1)S(1)}, bf16[160,128]{1,0:T(8,128)(2,1...) custom-call(bf16[480,128]{1,0:T(8,128)(2,1)S(1)} %get-tuple-element., ...), custom_call_target="tpu_custom_call" | custom-call | flops 436207616 | bytes 1048576 | tf_op jit(solution)/shard_map/attention/pallas_call | solution.py:272
  28.6 4.4 %collective-permute-start.7 = (bf16[160,128]{1,0:T(8,128)(2,1)S(1)}, bf16[160,128]{1,0:T(8,128)(2,1)S(1)}, u32[]{:S(2)}, u32[]{:S(2)}) collective-permute-start(bf16[160,128]{1,0:T(8,128)(2,1)S(1)} %get-tuple-element.33), channel_id=1, source_target_pairs={{14,0},{12,2},{10,4},{8,6},{6,8},{4,10},{2,12},{0,14},{15,1},{13,3... | collective-permute-start | bytes 122888 | tf_op jit(solution)/shard_map/ppermute | solution.py:84
  33.1 3.6 %collective-permute-start.9 = (bf16[160,128]{1,0:T(8,128)(2,1)S(1)}, bf16[160,128]{1,0:T(8,128)(2,1)S(1)}, u32[]{:S(2)}, u32[]{:S(2)}) collective-permute-start(bf16[160,128]{1,0:T(8,128)(2,1)S(1)} %get-tuple-element.35), channel_id=1, source_target_pairs={{10,0},{8,2},{14,4},{12,6},{2,8},{0,10},{6,12},{4,14},{11,1},{9,3}... | collective-permute-start | bytes 122888 | tf_op jit(solution)/shard_map/ppermute | solution.py:84
  36.7 2.1 %collective-permute-start.11 = (bf16[160,128]{1,0:T(8,128)(2,1)S(1)}, bf16[160,128]{1,0:T(8,128)(2,1)S(1)}, u32[]{:S(2)}, u32[]{:S(2)}) collective-permute-start(bf16[160,128]{1,0:T(8,128)(2,1)S(1)} %get-tuple-element.37), channel_id=1, source_target_pairs={{6,0},{4,2},{2,4},{0,6},{14,8},{12,10},{10,12},{8,14},{7,1},{5,3},... | collective-permute-start | bytes 122888 | tf_op jit(solution)/shard_map/ppermute | solution.py:84
  38.8 0.6 %collective-permute-start.12 = (bf16[160,128]{1,0:T(8,128)(2,1)S(1)}, bf16[160,128]{1,0:T(8,128)(2,1)S(1)}, u32[]{:S(2)}, u32[]{:S(2)}) collective-permute-start(bf16[160,128]{1,0:T(8,128)(2,1)S(1)} %get-tuple-element.38), channel_id=1, source_target_pairs={{4,0},{6,2},{0,4},{2,6},{12,8},{14,10},{8,12},{10,14},{5,1},{7,3},... | collective-permute-start | bytes 122888 | tf_op jit(solution)/shard_map/ppermute | solution.py:84
  39.4 0.8 %collective-permute-start.13 = (bf16[160,128]{1,0:T(8,128)(2,1)S(1)}, bf16[160,128]{1,0:T(8,128)(2,1)S(1)}, u32[]{:S(2)}, u32[]{:S(2)}) collective-permute-start(bf16[160,128]{1,0:T(8,128)(2,1)S(1)} %get-tuple-element.39), channel_id=1, source_target_pairs={{2,0},{0,2},{6,4},{4,6},{10,8},{8,10},{14,12},{12,14},{3,1},{1,3},... | collective-permute-start | bytes 122888 | tf_op jit(solution)/shard_map/ppermute | solution.py:84
  40.2 0.8 %collective-permute-done.9.refs_3_ = bf16[160,128]{1,0:T(8,128)(2,1)S(1)} collective-permute-done((bf16[160,128]{1,0:T(8,128)(2,1)S(1)}, bf16[160,128]{1,0:T(8,128)(2,1)S(1)}, u32[]{:S(2)}, u32[]{:S(2)}) %collective-permute-start.9) | collective-permute-done | bytes 40992 | tf_op jit(solution)/shard_map/ppermute | solution.py:84
  41.0 1.0 %collective-permute-done.10.refs_4_ = bf16[160,128]{1,0:T(8,128)(2,1)S(1)} collective-permute-done((bf16[160,128]{1,0:T(8,128)(2,1)S(1)}, bf16[160,128]{1,0:T(8,128)(2,1)S(1)}, u32[]{:S(2)}, u32[]{:S(2)}) %collective-permute-start.10) | collective-permute-done | bytes 40992 | tf_op jit(solution)/shard_map/ppermute | solution.py:84
  42.0 0.8 %collective-permute-done.12.refs_6_ = bf16[160,128]{1,0:T(8,128)(2,1)S(1)} collective-permute-done((bf16[160,128]{1,0:T(8,128)(2,1)S(1)}, bf16[160,128]{1,0:T(8,128)(2,1)S(1)}, u32[]{:S(2)}, u32[]{:S(2)}) %collective-permute-start.12) | collective-permute-done | bytes 40992 | tf_op jit(solution)/shard_map/ppermute | solution.py:84
  42.8 0.6 %collective-permute-done.13.refs_7_ = bf16[160,128]{1,0:T(8,128)(2,1)S(1)} collective-permute-done((bf16[160,128]{1,0:T(8,128)(2,1)S(1)}, bf16[160,128]{1,0:T(8,128)(2,1)S(1)}, u32[]{:S(2)}, u32[]{:S(2)}) %collective-permute-start.13) | collective-permute-done | bytes 40992 | tf_op jit(solution)/shard_map/ppermute | solution.py:84
  43.4 0.8 %unpack.1 = (bf16[128,1024]{1,0:T(8,128)(2,1)}, bf16[32,1024]{1,0:T(8,128)(2,1)}) custom-call(bf16[160,128]{1,0:T(8,128)(2,1)S(1)} %get-tuple-element.32.refs_0_, bf16[160,128]{1,0:T(8,128)(2,1)S(1)} %collective-permute-done.7.refs_1_, bf16[160,128]{1,0:T(8,128)(2,1)S(1)} %collective-permute-done.8.refs_2_, ...), custom_call_target="tpu_custom_call" | custom-call | tf_op jit(solution)/shard_map/unpack/pallas_call | solution.py:293
  (9 shorter events, 0.0 us)
Async XLA Ops:
  2.0 10.0 %collective-permute-start = (bf16[480,128]{1,0:T(8,128)(2,1)S(1)}, bf16[480,128]{1,0:T(8,128)(2,1)S(1)}, u32[]{:S(2)}, u32[]{:S(2)}) collective-permute-start(bf16[480,128]{1,0:T(8,128)(2,1)S(1)} %get-tuple-element.21), channel_id=1, source_target_pairs={{0,4},{2,6},{4,0},{6,2},{8,12},{10,14},{12,8},{14,10},{1,5},{3,7},... | collective-permute-start | bytes 368648 | tf_op jit(solution)/shard_map/ppermute | solution.py:84
  5.1 13.2 %collective-permute-start.1 = (bf16[480,128]{1,0:T(8,128)(2,1)S(1)}, bf16[480,128]{1,0:T(8,128)(2,1)S(1)}, u32[]{:S(2)}, u32[]{:S(2)}) collective-permute-start(bf16[480,128]{1,0:T(8,128)(2,1)S(1)} %get-tuple-element.23), channel_id=1, source_target_pairs={{0,8},{2,10},{4,12},{6,14},{8,0},{10,2},{12,4},{14,6},{1,9},{3,11}... | collective-permute-start | bytes 368648 | tf_op jit(solution)/shard_map/ppermute | solution.py:84
  7.7 15.8 %collective-permute-start.2 = (bf16[480,128]{1,0:T(8,128)(2,1)S(1)}, bf16[480,128]{1,0:T(8,128)(2,1)S(1)}, u32[]{:S(2)}, u32[]{:S(2)}) collective-permute-start(bf16[480,128]{1,0:T(8,128)(2,1)S(1)} %get-tuple-element.24), channel_id=1, source_target_pairs={{0,2},{2,0},{4,6},{6,4},{8,10},{10,8},{12,14},{14,12},{1,3},{3,1},... | collective-permute-start | bytes 368648 | tf_op jit(solution)/shard_map/ppermute | solution.py:84
  9.2 14.7 %collective-permute-start.3 = (bf16[480,128]{1,0:T(8,128)(2,1)S(1)}, bf16[480,128]{1,0:T(8,128)(2,1)S(1)}, u32[]{:S(2)}, u32[]{:S(2)}) collective-permute-start(bf16[480,128]{1,0:T(8,128)(2,1)S(1)} %get-tuple-element.25), channel_id=1, source_target_pairs={{0,10},{2,8},{4,14},{6,12},{8,2},{10,0},{12,6},{14,4},{1,11},{3,9}... | collective-permute-start | bytes 368648 | tf_op jit(solution)/shard_map/ppermute | solution.py:84
  9.5 14.4 %collective-permute-start.4 = (bf16[480,128]{1,0:T(8,128)(2,1)S(1)}, bf16[480,128]{1,0:T(8,128)(2,1)S(1)}, u32[]{:S(2)}, u32[]{:S(2)}) collective-permute-start(bf16[480,128]{1,0:T(8,128)(2,1)S(1)} %get-tuple-element.26), channel_id=1, source_target_pairs={{0,12},{2,14},{4,8},{6,10},{8,4},{10,6},{12,0},{14,2},{1,13},{3,15... | collective-permute-start | bytes 368648 | tf_op jit(solution)/shard_map/ppermute | solution.py:84
  13.1 11.6 %collective-permute-start.5 = (bf16[480,128]{1,0:T(8,128)(2,1)S(1)}, bf16[480,128]{1,0:T(8,128)(2,1)S(1)}, u32[]{:S(2)}, u32[]{:S(2)}) collective-permute-start(bf16[480,128]{1,0:T(8,128)(2,1)S(1)} %get-tuple-element.27), channel_id=1, source_target_pairs={{0,6},{2,4},{4,2},{6,0},{8,14},{10,12},{12,10},{14,8},{1,7},{3,5},... | collective-permute-start | bytes 368648 | tf_op jit(solution)/shard_map/ppermute | solution.py:84
  18.3 8.5 %collective-permute-start.6 = (bf16[480,128]{1,0:T(8,128)(2,1)S(1)}, bf16[480,128]{1,0:T(8,128)(2,1)S(1)}, u32[]{:S(2)}, u32[]{:S(2)}) collective-permute-start(bf16[480,128]{1,0:T(8,128)(2,1)S(1)} %get-tuple-element.28), channel_id=1, source_target_pairs={{0,14},{2,12},{4,10},{6,8},{8,6},{10,4},{12,2},{14,0},{1,15},{3,13... | collective-permute-start | bytes 368648 | tf_op jit(solution)/shard_map/ppermute | solution.py:84
  28.6 10.2 %collective-permute-start.7 = (bf16[160,128]{1,0:T(8,128)(2,1)S(1)}, bf16[160,128]{1,0:T(8,128)(2,1)S(1)}, u32[]{:S(2)}, u32[]{:S(2)}) collective-permute-start(bf16[160,128]{1,0:T(8,128)(2,1)S(1)} %get-tuple-element.33), channel_id=1, source_target_pairs={{14,0},{12,2},{10,4},{8,6},{6,8},{4,10},{2,12},{0,14},{15,1},{13,3... | collective-permute-start | bytes 122888 | tf_op jit(solution)/shard_map/ppermute | solution.py:84
  33.1 6.3 %collective-permute-start.8 = (bf16[160,128]{1,0:T(8,128)(2,1)S(1)}, bf16[160,128]{1,0:T(8,128)(2,1)S(1)}, u32[]{:S(2)}, u32[]{:S(2)}) collective-permute-start(bf16[160,128]{1,0:T(8,128)(2,1)S(1)} %get-tuple-element.34), channel_id=1, source_target_pairs={{12,0},{14,2},{8,4},{10,6},{4,8},{6,10},{0,12},{2,14},{13,1},{15,3... | collective-permute-start | bytes 122888 | tf_op jit(solution)/shard_map/ppermute | solution.py:84
  33.1 7.9 %collective-permute-start.9 = (bf16[160,128]{1,0:T(8,128)(2,1)S(1)}, bf16[160,128]{1,0:T(8,128)(2,1)S(1)}, u32[]{:S(2)}, u32[]{:S(2)}) collective-permute-start(bf16[160,128]{1,0:T(8,128)(2,1)S(1)} %get-tuple-element.35), channel_id=1, source_target_pairs={{10,0},{8,2},{14,4},{12,6},{2,8},{0,10},{6,12},{4,14},{11,1},{9,3}... | collective-permute-start | bytes 122888 | tf_op jit(solution)/shard_map/ppermute | solution.py:84
  36.7 5.3 %collective-permute-start.10 = (bf16[160,128]{1,0:T(8,128)(2,1)S(1)}, bf16[160,128]{1,0:T(8,128)(2,1)S(1)}, u32[]{:S(2)}, u32[]{:S(2)}) collective-permute-start(bf16[160,128]{1,0:T(8,128)(2,1)S(1)} %get-tuple-element.36), channel_id=1, source_target_pairs={{8,0},{10,2},{12,4},{14,6},{0,8},{2,10},{4,12},{6,14},{9,1},{11,3}... | collective-permute-start | bytes 122888 | tf_op jit(solution)/shard_map/ppermute | solution.py:84
  36.7 5.3 %collective-permute-start.11 = (bf16[160,128]{1,0:T(8,128)(2,1)S(1)}, bf16[160,128]{1,0:T(8,128)(2,1)S(1)}, u32[]{:S(2)}, u32[]{:S(2)}) collective-permute-start(bf16[160,128]{1,0:T(8,128)(2,1)S(1)} %get-tuple-element.37), channel_id=1, source_target_pairs={{6,0},{4,2},{2,4},{0,6},{14,8},{12,10},{10,12},{8,14},{7,1},{5,3},... | collective-permute-start | bytes 122888 | tf_op jit(solution)/shard_map/ppermute | solution.py:84
  38.8 4.0 %collective-permute-start.12 = (bf16[160,128]{1,0:T(8,128)(2,1)S(1)}, bf16[160,128]{1,0:T(8,128)(2,1)S(1)}, u32[]{:S(2)}, u32[]{:S(2)}) collective-permute-start(bf16[160,128]{1,0:T(8,128)(2,1)S(1)} %get-tuple-element.38), channel_id=1, source_target_pairs={{4,0},{6,2},{0,4},{2,6},{12,8},{14,10},{8,12},{10,14},{5,1},{7,3},... | collective-permute-start | bytes 122888 | tf_op jit(solution)/shard_map/ppermute | solution.py:84
  39.4 4.0 %collective-permute-start.13 = (bf16[160,128]{1,0:T(8,128)(2,1)S(1)}, bf16[160,128]{1,0:T(8,128)(2,1)S(1)}, u32[]{:S(2)}, u32[]{:S(2)}) collective-permute-start(bf16[160,128]{1,0:T(8,128)(2,1)S(1)} %get-tuple-element.39), channel_id=1, source_target_pairs={{2,0},{0,2},{6,4},{4,6},{10,8},{8,10},{14,12},{12,14},{3,1},{1,3},... | collective-permute-start | bytes 122888 | tf_op jit(solution)/shard_map/ppermute | solution.py:84

commit v8 on v7

--- a/solution.py
+++ b/solution.py
@@ -11,9 +11,9 @@
 HEAD_DIM = 128
 SCALE = HEAD_DIM ** (-0.5)
 SCALE_LOG2 = SCALE * math.log2(math.e)
-VMEM_LIMIT = 48 * 1024 * 1024
+VMEM_LIMIT = 24 * 1024 * 1024
 SOON = 5
-PACK_VMEM = 16 * 1024 * 1024
+PACK_VMEM = 4 * 1024 * 1024
 
 
 def normed(tokens, gain_row):
@@ -199,10 +199,10 @@
         a_result = weighed(product).astype(jnp.bfloat16)
         a_self[:, :HEAD_DIM] = a_result
         product = more_attend(tops[head], products[head], vq[early, :], vk[late, :], vv[late, :])
-        v_self[early, :HEAD_DIM] = weighed(product).astype(jnp.bfloat16)
+        early_result = weighed(product).astype(jnp.bfloat16)
         _, product = start_attend(vq[late, :], vk[...], vv[...])
-        v_self[late, :HEAD_DIM] = weighed(product).astype(jnp.bfloat16)
-        v_result = v_self[:, :HEAD_DIM]
+        v_result = jnp.concatenate([early_result, weighed(product).astype(jnp.bfloat16)], axis=0)
+        v_self[:, :HEAD_DIM] = v_result
         vq_gain, vk_gain, aq_gain, ak_gain = [
             gains[at, pl.ds(me * tops.shape[0] + head, 1), :] for at in range(4)
         ]

time: 44.5 us -> 44.5 us (level)
  no operation moved by 1% of the time
where the time goes in v8:
time: 44.5 us; the launch traced here: 44.2 us
  starting transfers between devices  28.3 us (64%)
  waiting for transfers between devices  7.99 us (18%)
  Pallas kernels  7.18 us (16%)
  between operations  0.68 us (2%)
    ppermute x14, starting transfers between devices, exchange(): lax.ppermute(blocks[step], 'seq', moves[step])  28.3 us
    ppermute x14, waiting for transfers between devices, exchange(): lax.ppermute(blocks[step], 'seq', moves[step])  7.99 us
    pallas_call x2, Pallas kernels, pack(): pl.pallas_call(functools.partial(pack_kernel, size, steps), out_shape=[ja...  2.48 us
    pallas_call x1, Pallas kernels, head_plan(): pl.pallas_call(functools.partial(early_kernel, rv), out_shape=[jax.ShapeD...  2.06 us
    pallas_call x1, Pallas kernels, head_plan(): pl.pallas_call(functools.partial(attention_kernel, size, rv, ra), out_sha...  1.84 us
  transfers between devices with their start and end apart: 14, of which 7 were waited for; matrix products, arithmetic and copies ran while one was open for 0% of the time, Pallas kernels for 7%

profile of v8, /device:TPU:0, one launch (start us, length us, event | category | flops | bytes accessed | tf_op | source)
XLA Modules:
  0.0 44.2 jit_solution(1777388979442274622)
XLA Ops:
  0.6 1.4 %pack.2 = (bf16[480,128]{1,0:T(8,128)(2,1)S(1)}, bf16[480,128]{1,0:T(8,128)(2,1)S(1)}, bf16[480,128]{1,0:T(8,128)(2,1)S(1)}, bf16[480,128]{1,0:T(8,128)(2,1)S(1)}, bf16[480,128]{1,0:T(8,128)(2,1)S(1)}) custom-call(bf16[128,1024]{1,0:T(8,128)(2,1)} %refs_0_.3, bf16[128,1024]{1,0:T(8,128)(2,1)} %refs_1_.3, bf16[128,1024]{1,0:T(8,128)(2,1)} %refs_2_.3, ...), custom_call_target="tpu_custom_call" | custom-call | tf_op jit(solution)/shard_map/pack/pallas_call | solution.py:232
  2.0 3.1 %collective-permute-start = (bf16[480,128]{1,0:T(8,128)(2,1)S(1)}, bf16[480,128]{1,0:T(8,128)(2,1)S(1)}, u32[]{:S(2)}, u32[]{:S(2)}) collective-permute-start(bf16[480,128]{1,0:T(8,128)(2,1)S(1)} %get-tuple-element.21), channel_id=1, source_target_pairs={{0,4},{2,6},{4,0},{6,2},{8,12},{10,14},{12,8},{14,10},{1,5},{3,7},... | collective-permute-start | bytes 368648 | tf_op jit(solution)/shard_map/ppermute | solution.py:84
  5.1 2.6 %collective-permute-start.1 = (bf16[480,128]{1,0:T(8,128)(2,1)S(1)}, bf16[480,128]{1,0:T(8,128)(2,1)S(1)}, u32[]{:S(2)}, u32[]{:S(2)}) collective-permute-start(bf16[480,128]{1,0:T(8,128)(2,1)S(1)} %get-tuple-element.23), channel_id=1, source_target_pairs={{0,8},{2,10},{4,12},{6,14},{8,0},{10,2},{12,4},{14,6},{1,9},{3,11}... | collective-permute-start | bytes 368648 | tf_op jit(solution)/shard_map/ppermute | solution.py:84
  7.7 1.5 %collective-permute-start.2 = (bf16[480,128]{1,0:T(8,128)(2,1)S(1)}, bf16[480,128]{1,0:T(8,128)(2,1)S(1)}, u32[]{:S(2)}, u32[]{:S(2)}) collective-permute-start(bf16[480,128]{1,0:T(8,128)(2,1)S(1)} %get-tuple-element.24), channel_id=1, source_target_pairs={{0,2},{2,0},{4,6},{6,4},{8,10},{10,8},{12,14},{14,12},{1,3},{3,1},... | collective-permute-start | bytes 368648 | tf_op jit(solution)/shard_map/ppermute | solution.py:84
  9.2 0.3 collective-permute-start.3
  9.5 2.5 %collective-permute-start.4 = (bf16[480,128]{1,0:T(8,128)(2,1)S(1)}, bf16[480,128]{1,0:T(8,128)(2,1)S(1)}, u32[]{:S(2)}, u32[]{:S(2)}) collective-permute-start(bf16[480,128]{1,0:T(8,128)(2,1)S(1)} %get-tuple-element.26), channel_id=1, source_target_pairs={{0,12},{2,14},{4,8},{6,10},{8,4},{10,6},{12,0},{14,2},{1,13},{3,15... | collective-permute-start | bytes 368648 | tf_op jit(solution)/shard_map/ppermute | solution.py:84
  12.0 1.1 %pack.3 = (bf16[480,128]{1,0:T(8,128)(2,1)S(1)}, bf16[480,128]{1,0:T(8,128)(2,1)S(1)}, bf16[480,128]{1,0:T(8,128)(2,1)S(1)}) custom-call(bf16[128,1024]{1,0:T(8,128)(2,1)} %refs_0_.3, bf16[128,1024]{1,0:T(8,128)(2,1)} %refs_1_.3, bf16[128,1024]{1,0:T(8,128)(2,1)} %refs_2_.3, bf16[32,1024]{1,0:T(8,128)(2,1)} %refs_3_.3, bf16[32,1024]{1,0:T(8,128)(2,1)} %refs_4_.3, ...), custom_call_target="tpu_custom_call" | custom-call | tf_op jit(solution)/shard_map/pack/pallas_call | solution.py:232
  13.1 1.7 %collective-permute-start.5 = (bf16[480,128]{1,0:T(8,128)(2,1)S(1)}, bf16[480,128]{1,0:T(8,128)(2,1)S(1)}, u32[]{:S(2)}, u32[]{:S(2)}) collective-permute-start(bf16[480,128]{1,0:T(8,128)(2,1)S(1)} %get-tuple-element.27), channel_id=1, source_target_pairs={{0,6},{2,4},{4,2},{6,0},{8,14},{10,12},{12,10},{14,8},{1,7},{3,5},... | collective-permute-start | bytes 368648 | tf_op jit(solution)/shard_map/ppermute | solution.py:84
  14.8 3.5 %collective-permute-done.1.refs_2_ = bf16[480,128]{1,0:T(8,128)(2,1)S(1)} collective-permute-done((bf16[480,128]{1,0:T(8,128)(2,1)S(1)}, bf16[480,128]{1,0:T(8,128)(2,1)S(1)}, u32[]{:S(2)}, u32[]{:S(2)}) %collective-permute-start.1) | collective-permute-done | bytes 122912 | tf_op jit(solution)/shard_map/ppermute | solution.py:84
  18.3 5.2 %collective-permute-start.6 = (bf16[480,128]{1,0:T(8,128)(2,1)S(1)}, bf16[480,128]{1,0:T(8,128)(2,1)S(1)}, u32[]{:S(2)}, u32[]{:S(2)}) collective-permute-start(bf16[480,128]{1,0:T(8,128)(2,1)S(1)} %get-tuple-element.28), channel_id=1, source_target_pairs={{0,14},{2,12},{4,10},{6,8},{8,6},{10,4},{12,2},{14,0},{1,15},{3,13... | collective-permute-start | bytes 368648 | tf_op jit(solution)/shard_map/ppermute | solution.py:84
  23.5 0.4 collective-permute-done.3.refs_4_
  23.9 0.8 %collective-permute-done.5.refs_6_ = bf16[480,128]{1,0:T(8,128)(2,1)S(1)} collective-permute-done((bf16[480,128]{1,0:T(8,128)(2,1)S(1)}, bf16[480,128]{1,0:T(8,128)(2,1)S(1)}, u32[]{:S(2)}, u32[]{:S(2)}) %collective-permute-start.5) | collective-permute-done | bytes 122912 | tf_op jit(solution)/shard_map/ppermute | solution.py:84
  24.7 2.1 %early.1 = (f32[1,896,128]{2,1,0:T(8,128)S(1)}, f32[1,896,256]{2,1,0:T(8,128)S(1)}, f32[4,8,128]{2,1,0:T(8,128)S(1)}) custom-call(bf16[480,128]{1,0:T(8,128)(2,1)S(1)} %get-tuple-element.22.refs_0_, bf16[480,128]{1,0:T(8,128)(2,1)S(1)} %collective-permute-done.refs_6_.refs_1_, bf16[480,128]{1,0:T(8,128)(2,1)S(1)} %collective-permute-done.1.refs_2_, ...), custom_call_target="tpu_custom_call" | custom-call | flops 411041792 | bytes 917504 | tf_op jit(solution)/shard_map/early/pallas_call | solution.py:255
  26.8 1.8 %attention.1 = (bf16[160,128]{1,0:T(8,128)(2,1)S(1)}, bf16[160,128]{1,0:T(8,128)(2,1)S(1)}, bf16[160,128]{1,0:T(8,128)(2,1)S(1)}, bf16[160,128]{1,0:T(8,128)(2,1...) custom-call(bf16[480,128]{1,0:T(8,128)(2,1)S(1)} %get-tuple-element., ...), custom_call_target="tpu_custom_call" | custom-call | flops 436207616 | bytes 1048576 | tf_op jit(solution)/shard_map/attention/pallas_call | solution.py:272
  28.6 4.4 %collective-permute-start.7 = (bf16[160,128]{1,0:T(8,128)(2,1)S(1)}, bf16[160,128]{1,0:T(8,128)(2,1)S(1)}, u32[]{:S(2)}, u32[]{:S(2)}) collective-permute-start(bf16[160,128]{1,0:T(8,128)(2,1)S(1)} %get-tuple-element.33), channel_id=1, source_target_pairs={{14,0},{12,2},{10,4},{8,6},{6,8},{4,10},{2,12},{0,14},{15,1},{13,3... | collective-permute-start | bytes 122888 | tf_op jit(solution)/shard_map/ppermute | solution.py:84
  33.1 3.6 %collective-permute-start.9 = (bf16[160,128]{1,0:T(8,128)(2,1)S(1)}, bf16[160,128]{1,0:T(8,128)(2,1)S(1)}, u32[]{:S(2)}, u32[]{:S(2)}) collective-permute-start(bf16[160,128]{1,0:T(8,128)(2,1)S(1)} %get-tuple-element.35), channel_id=1, source_target_pairs={{10,0},{8,2},{14,4},{12,6},{2,8},{0,10},{6,12},{4,14},{11,1},{9,3}... | collective-permute-start | bytes 122888 | tf_op jit(solution)/shard_map/ppermute | solution.py:84
  36.7 2.1 %collective-permute-start.11 = (bf16[160,128]{1,0:T(8,128)(2,1)S(1)}, bf16[160,128]{1,0:T(8,128)(2,1)S(1)}, u32[]{:S(2)}, u32[]{:S(2)}) collective-permute-start(bf16[160,128]{1,0:T(8,128)(2,1)S(1)} %get-tuple-element.37), channel_id=1, source_target_pairs={{6,0},{4,2},{2,4},{0,6},{14,8},{12,10},{10,12},{8,14},{7,1},{5,3},... | collective-permute-start | bytes 122888 | tf_op jit(solution)/shard_map/ppermute | solution.py:84
  38.8 0.6 %collective-permute-start.12 = (bf16[160,128]{1,0:T(8,128)(2,1)S(1)}, bf16[160,128]{1,0:T(8,128)(2,1)S(1)}, u32[]{:S(2)}, u32[]{:S(2)}) collective-permute-start(bf16[160,128]{1,0:T(8,128)(2,1)S(1)} %get-tuple-element.38), channel_id=1, source_target_pairs={{4,0},{6,2},{0,4},{2,6},{12,8},{14,10},{8,12},{10,14},{5,1},{7,3},... | collective-permute-start | bytes 122888 | tf_op jit(solution)/shard_map/ppermute | solution.py:84
  39.4 0.8 %collective-permute-start.13 = (bf16[160,128]{1,0:T(8,128)(2,1)S(1)}, bf16[160,128]{1,0:T(8,128)(2,1)S(1)}, u32[]{:S(2)}, u32[]{:S(2)}) collective-permute-start(bf16[160,128]{1,0:T(8,128)(2,1)S(1)} %get-tuple-element.39), channel_id=1, source_target_pairs={{2,0},{0,2},{6,4},{4,6},{10,8},{8,10},{14,12},{12,14},{3,1},{1,3},... | collective-permute-start | bytes 122888 | tf_op jit(solution)/shard_map/ppermute | solution.py:84
  40.2 0.8 %collective-permute-done.9.refs_3_ = bf16[160,128]{1,0:T(8,128)(2,1)S(1)} collective-permute-done((bf16[160,128]{1,0:T(8,128)(2,1)S(1)}, bf16[160,128]{1,0:T(8,128)(2,1)S(1)}, u32[]{:S(2)}, u32[]{:S(2)}) %collective-permute-start.9) | collective-permute-done | bytes 40992 | tf_op jit(solution)/shard_map/ppermute | solution.py:84
  41.0 1.0 %collective-permute-done.10.refs_4_ = bf16[160,128]{1,0:T(8,128)(2,1)S(1)} collective-permute-done((bf16[160,128]{1,0:T(8,128)(2,1)S(1)}, bf16[160,128]{1,0:T(8,128)(2,1)S(1)}, u32[]{:S(2)}, u32[]{:S(2)}) %collective-permute-start.10) | collective-permute-done | bytes 40992 | tf_op jit(solution)/shard_map/ppermute | solution.py:84
  42.0 0.8 %collective-permute-done.12.refs_6_ = bf16[160,128]{1,0:T(8,128)(2,1)S(1)} collective-permute-done((bf16[160,128]{1,0:T(8,128)(2,1)S(1)}, bf16[160,128]{1,0:T(8,128)(2,1)S(1)}, u32[]{:S(2)}, u32[]{:S(2)}) %collective-permute-start.12) | collective-permute-done | bytes 40992 | tf_op jit(solution)/shard_map/ppermute | solution.py:84
  42.8 0.6 %collective-permute-done.13.refs_7_ = bf16[160,128]{1,0:T(8,128)(2,1)S(1)} collective-permute-done((bf16[160,128]{1,0:T(8,128)(2,1)S(1)}, bf16[160,128]{1,0:T(8,128)(2,1)S(1)}, u32[]{:S(2)}, u32[]{:S(2)}) %collective-permute-start.13) | collective-permute-done | bytes 40992 | tf_op jit(solution)/shard_map/ppermute | solution.py:84
  43.4 0.8 %unpack.1 = (bf16[128,1024]{1,0:T(8,128)(2,1)}, bf16[32,1024]{1,0:T(8,128)(2,1)}) custom-call(bf16[160,128]{1,0:T(8,128)(2,1)S(1)} %get-tuple-element.32.refs_0_, bf16[160,128]{1,0:T(8,128)(2,1)S(1)} %collective-permute-done.7.refs_1_, bf16[160,128]{1,0:T(8,128)(2,1)S(1)} %collective-permute-done.8.refs_2_, ...), custom_call_target="tpu_custom_call" | custom-call | tf_op jit(solution)/shard_map/unpack/pallas_call | solution.py:293
  (9 shorter events, 0.0 us)
Async XLA Ops:
  2.0 10.0 %collective-permute-start = (bf16[480,128]{1,0:T(8,128)(2,1)S(1)}, bf16[480,128]{1,0:T(8,128)(2,1)S(1)}, u32[]{:S(2)}, u32[]{:S(2)}) collective-permute-start(bf16[480,128]{1,0:T(8,128)(2,1)S(1)} %get-tuple-element.21), channel_id=1, source_target_pairs={{0,4},{2,6},{4,0},{6,2},{8,12},{10,14},{12,8},{14,10},{1,5},{3,7},... | collective-permute-start | bytes 368648 | tf_op jit(solution)/shard_map/ppermute | solution.py:84
  5.1 13.2 %collective-permute-start.1 = (bf16[480,128]{1,0:T(8,128)(2,1)S(1)}, bf16[480,128]{1,0:T(8,128)(2,1)S(1)}, u32[]{:S(2)}, u32[]{:S(2)}) collective-permute-start(bf16[480,128]{1,0:T(8,128)(2,1)S(1)} %get-tuple-element.23), channel_id=1, source_target_pairs={{0,8},{2,10},{4,12},{6,14},{8,0},{10,2},{12,4},{14,6},{1,9},{3,11}... | collective-permute-start | bytes 368648 | tf_op jit(solution)/shard_map/ppermute | solution.py:84
  7.7 15.8 %collective-permute-start.2 = (bf16[480,128]{1,0:T(8,128)(2,1)S(1)}, bf16[480,128]{1,0:T(8,128)(2,1)S(1)}, u32[]{:S(2)}, u32[]{:S(2)}) collective-permute-start(bf16[480,128]{1,0:T(8,128)(2,1)S(1)} %get-tuple-element.24), channel_id=1, source_target_pairs={{0,2},{2,0},{4,6},{6,4},{8,10},{10,8},{12,14},{14,12},{1,3},{3,1},... | collective-permute-start | bytes 368648 | tf_op jit(solution)/shard_map/ppermute | solution.py:84
  9.2 14.7 %collective-permute-start.3 = (bf16[480,128]{1,0:T(8,128)(2,1)S(1)}, bf16[480,128]{1,0:T(8,128)(2,1)S(1)}, u32[]{:S(2)}, u32[]{:S(2)}) collective-permute-start(bf16[480,128]{1,0:T(8,128)(2,1)S(1)} %get-tuple-element.25), channel_id=1, source_target_pairs={{0,10},{2,8},{4,14},{6,12},{8,2},{10,0},{12,6},{14,4},{1,11},{3,9}... | collective-permute-start | bytes 368648 | tf_op jit(solution)/shard_map/ppermute | solution.py:84
  9.5 14.4 %collective-permute-start.4 = (bf16[480,128]{1,0:T(8,128)(2,1)S(1)}, bf16[480,128]{1,0:T(8,128)(2,1)S(1)}, u32[]{:S(2)}, u32[]{:S(2)}) collective-permute-start(bf16[480,128]{1,0:T(8,128)(2,1)S(1)} %get-tuple-element.26), channel_id=1, source_target_pairs={{0,12},{2,14},{4,8},{6,10},{8,4},{10,6},{12,0},{14,2},{1,13},{3,15... | collective-permute-start | bytes 368648 | tf_op jit(solution)/shard_map/ppermute | solution.py:84
  13.1 11.6 %collective-permute-start.5 = (bf16[480,128]{1,0:T(8,128)(2,1)S(1)}, bf16[480,128]{1,0:T(8,128)(2,1)S(1)}, u32[]{:S(2)}, u32[]{:S(2)}) collective-permute-start(bf16[480,128]{1,0:T(8,128)(2,1)S(1)} %get-tuple-element.27), channel_id=1, source_target_pairs={{0,6},{2,4},{4,2},{6,0},{8,14},{10,12},{12,10},{14,8},{1,7},{3,5},... | collective-permute-start | bytes 368648 | tf_op jit(solution)/shard_map/ppermute | solution.py:84
  18.3 8.5 %collective-permute-start.6 = (bf16[480,128]{1,0:T(8,128)(2,1)S(1)}, bf16[480,128]{1,0:T(8,128)(2,1)S(1)}, u32[]{:S(2)}, u32[]{:S(2)}) collective-permute-start(bf16[480,128]{1,0:T(8,128)(2,1)S(1)} %get-tuple-element.28), channel_id=1, source_target_pairs={{0,14},{2,12},{4,10},{6,8},{8,6},{10,4},{12,2},{14,0},{1,15},{3,13... | collective-permute-start | bytes 368648 | tf_op jit(solution)/shard_map/ppermute | solution.py:84
  28.6 10.2 %collective-permute-start.7 = (bf16[160,128]{1,0:T(8,128)(2,1)S(1)}, bf16[160,128]{1,0:T(8,128)(2,1)S(1)}, u32[]{:S(2)}, u32[]{:S(2)}) collective-permute-start(bf16[160,128]{1,0:T(8,128)(2,1)S(1)} %get-tuple-element.33), channel_id=1, source_target_pairs={{14,0},{12,2},{10,4},{8,6},{6,8},{4,10},{2,12},{0,14},{15,1},{13,3... | collective-permute-start | bytes 122888 | tf_op jit(solution)/shard_map/ppermute | solution.py:84
  33.1 6.3 %collective-permute-start.8 = (bf16[160,128]{1,0:T(8,128)(2,1)S(1)}, bf16[160,128]{1,0:T(8,128)(2,1)S(1)}, u32[]{:S(2)}, u32[]{:S(2)}) collective-permute-start(bf16[160,128]{1,0:T(8,128)(2,1)S(1)} %get-tuple-element.34), channel_id=1, source_target_pairs={{12,0},{14,2},{8,4},{10,6},{4,8},{6,10},{0,12},{2,14},{13,1},{15,3... | collective-permute-start | bytes 122888 | tf_op jit(solution)/shard_map/ppermute | solution.py:84
  33.1 7.9 %collective-permute-start.9 = (bf16[160,128]{1,0:T(8,128)(2,1)S(1)}, bf16[160,128]{1,0:T(8,128)(2,1)S(1)}, u32[]{:S(2)}, u32[]{:S(2)}) collective-permute-start(bf16[160,128]{1,0:T(8,128)(2,1)S(1)} %get-tuple-element.35), channel_id=1, source_target_pairs={{10,0},{8,2},{14,4},{12,6},{2,8},{0,10},{6,12},{4,14},{11,1},{9,3}... | collective-permute-start | bytes 122888 | tf_op jit(solution)/shard_map/ppermute | solution.py:84
  36.7 5.3 %collective-permute-start.10 = (bf16[160,128]{1,0:T(8,128)(2,1)S(1)}, bf16[160,128]{1,0:T(8,128)(2,1)S(1)}, u32[]{:S(2)}, u32[]{:S(2)}) collective-permute-start(bf16[160,128]{1,0:T(8,128)(2,1)S(1)} %get-tuple-element.36), channel_id=1, source_target_pairs={{8,0},{10,2},{12,4},{14,6},{0,8},{2,10},{4,12},{6,14},{9,1},{11,3}... | collective-permute-start | bytes 122888 | tf_op jit(solution)/shard_map/ppermute | solution.py:84
  36.7 5.3 %collective-permute-start.11 = (bf16[160,128]{1,0:T(8,128)(2,1)S(1)}, bf16[160,128]{1,0:T(8,128)(2,1)S(1)}, u32[]{:S(2)}, u32[]{:S(2)}) collective-permute-start(bf16[160,128]{1,0:T(8,128)(2,1)S(1)} %get-tuple-element.37), channel_id=1, source_target_pairs={{6,0},{4,2},{2,4},{0,6},{14,8},{12,10},{10,12},{8,14},{7,1},{5,3},... | collective-permute-start | bytes 122888 | tf_op jit(solution)/shard_map/ppermute | solution.py:84
  38.8 4.0 %collective-permute-start.12 = (bf16[160,128]{1,0:T(8,128)(2,1)S(1)}, bf16[160,128]{1,0:T(8,128)(2,1)S(1)}, u32[]{:S(2)}, u32[]{:S(2)}) collective-permute-start(bf16[160,128]{1,0:T(8,128)(2,1)S(1)} %get-tuple-element.38), channel_id=1, source_target_pairs={{4,0},{6,2},{0,4},{2,6},{12,8},{14,10},{8,12},{10,14},{5,1},{7,3},... | collective-permute-start | bytes 122888 | tf_op jit(solution)/shard_map/ppermute | solution.py:84
  39.4 4.0 %collective-permute-start.13 = (bf16[160,128]{1,0:T(8,128)(2,1)S(1)}, bf16[160,128]{1,0:T(8,128)(2,1)S(1)}, u32[]{:S(2)}, u32[]{:S(2)}) collective-permute-start(bf16[160,128]{1,0:T(8,128)(2,1)S(1)} %get-tuple-element.39), channel_id=1, source_target_pairs={{2,0},{0,2},{6,4},{4,6},{10,8},{8,10},{14,12},{12,14},{3,1},{1,3},... | collective-permute-start | bytes 122888 | tf_op jit(solution)/shard_map/ppermute | solution.py:84
